TPU v7x, 512 devices: a whole 4x4x16 slice. The times are simulated.
512 devices in a mesh: gx: 32 (over z_lo, y, core), gy: 16 (over x, z_hi).
Axes of the slice: x: 4, y: 4, z: 16 (z_hi: 4, z_lo: 4; z = z_hi * 4 + z_lo), core: 2. Of those that a mesh axis runs over, the one named last changes fastest.
Arguments:
- fine_now: float32 [3, 8, 512, 4096], P(None, None, 'gx', 'gy'), may hold values from -6 to 6
- fine_before: float32 [3, 8, 512, 4096], P(None, None, 'gx', 'gy'), may hold values from -6 to 6
- fine_density: float32 [8, 512, 4096], P(None, 'gx', 'gy'), may hold values from 1.5 to 3
- fine_shear: float32 [8, 512, 4096], P(None, 'gx', 'gy'), may hold values from 0.3 to 1.5
- fine_lame: float32 [8, 512, 4096], P(None, 'gx', 'gy'), may hold values from 0.3 to 3
- coarse_now: float32 [3, 8, 256, 2048], P(None, None, 'gx', 'gy'), may hold values from -6 to 6
- coarse_before: float32 [3, 8, 256, 2048], P(None, None, 'gx', 'gy'), may hold values from -6 to 6
- coarse_density: float32 [8, 256, 2048], P(None, 'gx', 'gy'), may hold values from 1.5 to 3
- coarse_shear: float32 [8, 256, 2048], P(None, 'gx', 'gy'), may hold values from 0.3 to 1.5
- coarse_lame: float32 [8, 256, 2048], P(None, 'gx', 'gy'), may hold values from 0.3 to 3
Outputs:
- fine_next: float32 [3, 8, 512, 4096], P(None, None, 'gx', 'gy')
- coarse_next: float32 [3, 8, 256, 2048], P(None, None, 'gx', 'gy')
- reduction: float32 [], replicated
All inputs are finite; a program needn't handle non-finite values. Where the computation divides by a largest or mean magnitude, that divisor is 1e-20 or more.
Results may differ from a plain program's by a relative error of at most 0.000023.
Values sent between devices are 32-bit elements; how exact they have to be, the bound alone decides.
No kernel may reach another device: no remote copies, remote signals or barrier semaphores. Data moves between devices by JAX's collectives and lax.ppermute only.
A program may use at most 64 MiB of HBM per device.

v0:
```python
import jax
import jax.numpy as jnp
from jax import lax
from jax.sharding import PartitionSpec as P

ITERS = 3


def padded_2(cells, sides, width):
    for axis, dim in sides:
        count = lax.axis_size(axis)
        ends = count - 1
        head = lax.slice_in_dim(cells, 0, width, axis=dim)
        tail = lax.slice_in_dim(cells, cells.shape[dim] - width, cells.shape[dim], axis=dim)
        cells = jnp.concatenate(
            [
                lax.ppermute(tail, axis, [(i, (i + 1) % count) for i in range(ends)]),
                cells,
                lax.ppermute(head, axis, [((i + 1) % count, i) for i in range(ends)]),
            ],
            axis=dim,
        )
    return cells


def shifted(value, axis, steps):
    count = lax.axis_size(axis)
    leading, last = (max(0, -steps), min(count, count - steps))
    return lax.ppermute(value, axis, [(source, source + steps) for source in range(leading, last)])


def first_diff(field, along, spacing):
    length = field.shape[along] - 4

    def piece(start):
        return lax.slice_in_dim(field, start, start + length, axis=along)

    return (piece(0) - 8.0 * piece(1) + 8.0 * piece(3) - piece(4)) / (12.0 * spacing)


def second_diff(field, along, spacing):
    length = field.shape[along] - 4

    def piece(start):
        return lax.slice_in_dim(field, start, start + length, axis=along)

    return (-piece(0) + 16.0 * piece(1) - 30.0 * piece(2) + 16.0 * piece(3) - piece(4)) / (
        12.0 * spacing * spacing
    )


def vertical_first(field, spacing):
    return (field[2:] - field[:-2]) / (2.0 * spacing)


def vertical_second(field, spacing):
    return (field[2:] - 2.0 * field[1:-1] + field[:-2]) / (spacing * spacing)


def laplace(field, spacing):
    return (
        second_diff(field[1:-1, :, 2:-2], 1, spacing)
        + second_diff(field[1:-1, 2:-2, :], 2, spacing)
        + vertical_second(field[:, 2:-2, 2:-2], spacing)
    )


def elastic(extended, shear, lame_param, spacing, slope_x, slope_y):
    comp_x, comp_y, comp_z = (extended[0], extended[1], extended[2])
    vert_z = vertical_first(comp_z, spacing)
    div_x = (
        second_diff(comp_x[1:-1, :, 2:-2], 1, spacing)
        + first_diff(slope_y, 1, spacing)
        + first_diff(vert_z[:, :, 2:-2], 1, spacing)
    )
    div_y = (
        first_diff(slope_x, 1, spacing)
        + second_diff(comp_y[1:-1, 2:-2, :], 2, spacing)
        + first_diff(vert_z[:, 2:-2, :], 2, spacing)
    )
    across_x = first_diff(comp_x[:, :, 2:-2], 1, spacing)
    across_y = first_diff(comp_y[:, 2:-2, :], 2, spacing)
    div_z = (
        vertical_first(across_x, spacing)
        + vertical_first(across_y, spacing)
        + vertical_second(comp_z[:, 2:-2, 2:-2], spacing)
    )
    bulk = lame_param + shear
    return jnp.stack(
        [
            shear * laplace(comp_x, spacing) + bulk * div_x,
            shear * laplace(comp_y, spacing) + bulk * div_y,
            shear * laplace(comp_z, spacing) + bulk * div_z,
        ]
    )


def wave(lame_param, shear, density):
    return jnp.sqrt((lame_param + 2.0 * shear) / density)


def modulus(shear, lame_param):
    return jnp.stack([shear, shear, lame_param + 2.0 * shear])


def refine(field, along):
    length = field.shape[along]
    even_rows = lax.slice_in_dim(field, 0, length - 1, axis=along)
    next_rows = lax.slice_in_dim(field, 1, length, axis=along)
    odd_rows = 0.5 * (even_rows + next_rows)
    woven = jnp.stack([even_rows, odd_rows], axis=along + 1)
    shape = list(field.shape)
    shape[along] = 2 * (length - 1)
    woven = woven.reshape(shape)
    tail = lax.slice_in_dim(field, length - 1, length, axis=along)
    joined = jnp.concatenate([woven, tail], axis=along)
    return lax.slice_in_dim(joined, 1, 2 * length - 1, axis=along)


def prolong(padded):
    return refine(refine(padded, 1), 2)


def restrict_once(field, along):
    length = field.shape[along]
    left = lax.slice_in_dim(field, 0, length - 2, 2, axis=along)
    centre = lax.slice_in_dim(field, 1, length - 1, 2, axis=along)
    right = lax.slice_in_dim(field, 2, length, 2, axis=along)
    return 0.25 * left + 0.5 * centre + 0.25 * right


def restrict(field):
    return restrict_once(restrict_once(field, 1), 2)


def shards(
    fine_now,
    fine_before,
    fine_density,
    fine_shear,
    fine_lame,
    coarse_now,
    coarse_before,
    coarse_density,
    coarse_shear,
    coarse_lame,
):
    local_peak = jnp.maximum(
        jnp.max(wave(fine_lame, fine_shear, fine_density)),
        0.5 * jnp.max(wave(coarse_lame, coarse_shear, coarse_density)),
    )
    wave_peak = lax.pmax(local_peak, ("gx", "gy"))
    time_step = 0.3 / wave_peak
    fine_pad = padded_2(fine_now, (("gx", 2), ("gy", 3)), 2)
    fine_ext = jnp.concatenate([fine_pad[:, 1:2], fine_pad], axis=1)
    fine_slope_x = first_diff(fine_ext[0, 1:-1], 2, 1.0)
    fine_slope_y = first_diff(fine_ext[1, 1:-1], 2, 1.0)
    coarse_pad = padded_2(coarse_now, (("gx", 2), ("gy", 3)), 2)
    coarse_ext = jnp.concatenate([coarse_pad, jnp.zeros_like(coarse_pad[:, :1])], axis=1)
    coarse_slope_x = first_diff(coarse_ext[0, 1:-1], 2, 2.0)
    coarse_slope_y = first_diff(coarse_ext[1, 1:-1], 2, 2.0)
    fine_accel = elastic(fine_ext, fine_shear[:-1], fine_lame[:-1], 1.0, fine_slope_x, fine_slope_y)
    fine_new = (
        2.0 * fine_now[:, :-1]
        - fine_before[:, :-1]
        + time_step * time_step * fine_accel / fine_density[:-1]
    )
    coarse_accel = elastic(
        coarse_ext, coarse_shear[1:], coarse_lame[1:], 2.0, coarse_slope_x, coarse_slope_y
    )
    coarse_new = (
        2.0 * coarse_now[:, 1:]
        - coarse_before[:, 1:]
        + time_step * time_step * coarse_accel / coarse_density[1:]
    )
    above = fine_new[:, -1]
    below = coarse_new[:, 0]
    fine_modulus = modulus(fine_shear[-1], fine_lame[-1])
    coarse_modulus = modulus(coarse_shear[0], coarse_lame[0])
    modulus_row = shifted(fine_modulus[:, -1:, :], "gx", 1)
    modulus_ext = jnp.concatenate([modulus_row, fine_modulus], axis=1)
    modulus_col = shifted(modulus_ext[:, :, -1:], "gy", 1)
    modulus_ext = jnp.concatenate([modulus_col, modulus_ext], axis=2)
    modulus_pad = jnp.pad(modulus_ext, ((0, 0), (0, 1), (0, 1)))
    jacobi_diag = 0.5 * coarse_modulus + 0.5625 * restrict(modulus_pad)

    def mismatch_of(interface):
        upper_row = shifted(interface[:, :1, :], "gx", -1)
        coarse_ext_plane = jnp.concatenate([interface, upper_row], axis=1)
        upper_col = shifted(coarse_ext_plane[:, :, :1], "gy", -1)
        coarse_ext_plane = jnp.concatenate([coarse_ext_plane, upper_col], axis=2)
        coarse_rim = jnp.pad(coarse_ext_plane, ((0, 0), (1, 0), (1, 0)))
        refined = prolong(coarse_rim)
        stress_terms = fine_modulus * (refined[:, 1:-1, 1:-1] - above)
        stress_row = shifted(stress_terms[:, -1:, :], "gx", 1)
        stress_ext = jnp.concatenate([stress_row, stress_terms], axis=1)
        stress_col = shifted(stress_ext[:, :, -1:], "gy", 1)
        stress_ext = jnp.concatenate([stress_col, stress_ext], axis=2)
        stress_pad = jnp.pad(stress_ext, ((0, 0), (0, 1), (0, 1)))
        return (0.5 * coarse_modulus * (interface - below) + restrict(stress_pad), refined)

    interface = 2.0 * coarse_now[:, 0] - coarse_before[:, 0]
    mismatch, refined = mismatch_of(interface)
    first_local = jnp.max(jnp.abs(mismatch))
    first_max = lax.pmax(first_local, ("gx", "gy"))
    for sweep in range(ITERS):
        interface = interface - mismatch / jacobi_diag
        mismatch, refined = mismatch_of(interface)
    last_local = jnp.max(jnp.abs(mismatch))
    last_max = lax.pmax(last_local, ("gx", "gy"))
    fine_next = jnp.concatenate([fine_new, refined[:, 1:-1, 1:-1][:, None]], axis=1)
    coarse_next = jnp.concatenate([interface[:, None], coarse_new], axis=1)
    return (fine_next, coarse_next, last_max / (first_max + 1e-06))


def solution(mesh):
    placed = (
        P(None, None, "gx", "gy"),
        P(None, None, "gx", "gy"),
        P(None, "gx", "gy"),
        P(None, "gx", "gy"),
        P(None, "gx", "gy"),
        P(None, None, "gx", "gy"),
        P(None, None, "gx", "gy"),
        P(None, "gx", "gy"),
        P(None, "gx", "gy"),
        P(None, "gx", "gy"),
    )
    return jax.shard_map(
        shards,
        mesh=mesh,
        in_specs=placed,
        out_specs=(P(None, None, "gx", "gy"), P(None, None, "gx", "gy"), P()),
        check_vma=False,
    )
```

profile of v0, /device:TPU:1, one launch (start us, length us, event | category | flops | bytes accessed | tf_op | source)
XLA Modules:
  0.0 433.2 jit_solution(1409021550999944403)
XLA Ops:
  0.7 1.1 fusion.223
  1.8 4.7 %collective-permute-start = (f32[3,8,2,256]{3,2,1,0:T(2,128)S(1)}, f32[3,8,2,256]{3,2,1,0:T(2,128)S(1)}, u32[]{:S(2)}, u32[]{:S(2)}) collective-permute-start(f32[3,8,2,256]{3,2,1,0:T(2,128)S(1)} %get-tuple-element.29), channel_id=1, source_target_pairs={{0,16},{16,32},{32,48},{48,64},{64,80},{80,96},{96,112},{112,128},... | collective-permute-start | bytes 147464 | tf_op jit(solution)/shard_map/ppermute | solution.py:17
  6.5 5.5 %collective-permute-start.1 = (f32[3,8,2,256]{3,2,1,0:T(2,128)S(1)}, f32[3,8,2,256]{3,2,1,0:T(2,128)S(1)}, u32[]{:S(2)}, u32[]{:S(2)}) collective-permute-start(f32[3,8,2,256]{3,2,1,0:T(2,128)S(1)} %get-tuple-element.30), channel_id=1, source_target_pairs={{16,0},{32,16},{48,32},{64,48},{80,64},{96,80},{112,96},{128,112},... | collective-permute-start | bytes 147464 | tf_op jit(solution)/shard_map/ppermute | solution.py:19
  12.0 0.7 fusion.221
  12.7 1.9 collective-permute-start.8
  14.6 1.0 fusion.226
  15.6 3.6 collective-permute-start.4
  19.3 1.9 collective-permute-start.5
  24.0 108.6 %pmax.21 = f32[]{:T(128)} all-reduce(f32[]{:T(128)S(6)} %max.9), channel_id=1, replica_groups=mesh['gx'=32,'gy'=16] {'gx','gy'}, use_global_device_ids=true, to_apply=%region_2.0 | all-reduce | flops 1 | bytes 8 | tf_op jit(solution)/shard_map/pmax | solution.py:152
  132.6 1.3 collective-permute-start.9
  134.6 7.0 %collective-permute-done.9 = f32[3,9,1]{2,1,0:T(8,128)S(1)} collective-permute-done((f32[3,9,1]{2,1,0:T(8,128)S(1)}, f32[3,9,1]{2,1,0:T(8,128)S(1)}, u32[]{:S(2)}, u32[]{:S(2)}) %collective-permute-start.9) | collective-permute-done | bytes 140 | tf_op jit(solution)/shard_map/ppermute | solution.py:29
  142.0 0.8 copy-done.3
  142.9 3.9 collective-permute-start.6
  146.8 1.3 collective-permute-start.7
  149.0 11.8 %collective-permute-done.6 = f32[3,8,12,2]{3,2,1,0:T(8,128)S(1)} collective-permute-done((f32[3,8,12,2]{3,2,1,0:T(8,128)S(1)}, f32[3,8,12,2]{3,2,1,0:T(8,128)S(1)}, u32[]{:S(2)}, u32[]{:S(2)}) %collective-permute-start.6) | collective-permute-done | bytes 2336 | tf_op jit(solution)/shard_map/ppermute | solution.py:17
  160.9 10.5 %collective-permute-done.7 = f32[3,8,12,2]{3,2,1,0:T(8,128)S(1)} collective-permute-done((f32[3,8,12,2]{3,2,1,0:T(8,128)S(1)}, f32[3,8,12,2]{3,2,1,0:T(8,128)S(1)}, u32[]{:S(2)}, u32[]{:S(2)}) %collective-permute-start.7) | collective-permute-done | bytes 2336 | tf_op jit(solution)/shard_map/ppermute | solution.py:19
  173.4 5.2 %collective-permute-start.2 = (f32[3,8,20,2]{3,2,1,0:T(8,128)S(1)}, f32[3,8,20,2]{3,2,1,0:T(8,128)S(1)}, u32[]{:S(2)}, u32[]{:S(2)}) collective-permute-start(f32[3,8,20,2]{3,2,1,0:T(8,128)S(1)} %get-tuple-element.21), channel_id=1, source_target_pairs={{0,1},{1,2},{2,3},{3,4},{4,5},{5,6},{6,7},{7,8},{8,9},{9,10},{10,1... | collective-permute-start | bytes 11528 | tf_op jit(solution)/shard_map/ppermute | solution.py:17
  178.6 1.3 collective-permute-start.3
  180.0 7.7 %collective-permute-done.2 = f32[3,8,20,2]{3,2,1,0:T(8,128)S(1)} collective-permute-done((f32[3,8,20,2]{3,2,1,0:T(8,128)S(1)}, f32[3,8,20,2]{3,2,1,0:T(8,128)S(1)}, u32[]{:S(2)}, u32[]{:S(2)}) %collective-permute-start.2) | collective-permute-done | bytes 3872 | tf_op jit(solution)/shard_map/ppermute | solution.py:17
  187.7 15.2 %collective-permute-done.3 = f32[3,8,20,2]{3,2,1,0:T(8,128)S(1)} collective-permute-done((f32[3,8,20,2]{3,2,1,0:T(8,128)S(1)}, f32[3,8,20,2]{3,2,1,0:T(8,128)S(1)}, u32[]{:S(2)}, u32[]{:S(2)}) %collective-permute-start.3) | collective-permute-done | bytes 3872 | tf_op jit(solution)/shard_map/ppermute | solution.py:19
  207.0 1.9 collective-permute-start.12
  209.0 1.9 collective-permute-start.10
  211.0 7.1 %collective-permute-start.13 = (f32[3,17,1]{2,1,0:T(8,128)S(1)}, f32[3,17,1]{2,1,0:T(8,128)S(1)}, u32[]{:S(2)}, u32[]{:S(2)}) collective-permute-start(f32[3,17,1]{2,1,0:T(8,128)S(1)} %pad_maximum_fusion.25), channel_id=1, source_target_pairs={{0,1},{1,2},{2,3},{3,4},{4,5},{5,6},{6,7},{7,8},{8,9},{9,10},{10,1... | collective-permute-start | bytes 620 | tf_op jit(solution)/shard_map/ppermute | solution.py:29
  218.3 2.1 collective-permute-start.11
  224.3 3.2 collective-permute-start.14
  227.5 2.5 collective-permute-done.14
  230.0 1.3 collective-permute-start.15
  231.3 8.1 %collective-permute-done.15 = f32[3,9,1]{2,1,0:T(8,128)S(1)} collective-permute-done((f32[3,9,1]{2,1,0:T(8,128)S(1)}, f32[3,9,1]{2,1,0:T(8,128)S(1)}, u32[]{:S(2)}, u32[]{:S(2)}) %collective-permute-start.15) | collective-permute-done | bytes 140 | tf_op jit(solution)/shard_map/ppermute | solution.py:29
  240.7 2.7 collective-permute-start.16
  243.5 0.7 collective-permute-done.16
  244.3 7.7 %collective-permute-start.17 = (f32[3,17,1]{2,1,0:T(8,128)S(1)}, f32[3,17,1]{2,1,0:T(8,128)S(1)}, u32[]{:S(2)}, u32[]{:S(2)}) collective-permute-start(f32[3,17,1]{2,1,0:T(8,128)S(1)} %pad_maximum_fusion.24), channel_id=1, source_target_pairs={{0,1},{1,2},{2,3},{3,4},{4,5},{5,6},{6,7},{7,8},{8,9},{9,10},{10,1... | collective-permute-start | bytes 620 | tf_op jit(solution)/shard_map/ppermute | solution.py:29
  252.0 0.9 collective-permute-done.17
  254.5 3.0 collective-permute-start.18
  257.5 3.3 collective-permute-done.18
  260.8 1.3 collective-permute-start.19
  262.1 7.8 %collective-permute-done.19 = f32[3,9,1]{2,1,0:T(8,128)S(1)} collective-permute-done((f32[3,9,1]{2,1,0:T(8,128)S(1)}, f32[3,9,1]{2,1,0:T(8,128)S(1)}, u32[]{:S(2)}, u32[]{:S(2)}) %collective-permute-start.19) | collective-permute-done | bytes 140 | tf_op jit(solution)/shard_map/ppermute | solution.py:29
  271.3 3.1 collective-permute-start.20
  274.3 0.7 collective-permute-done.20
  275.1 7.4 %collective-permute-start.21 = (f32[3,17,1]{2,1,0:T(8,128)S(1)}, f32[3,17,1]{2,1,0:T(8,128)S(1)}, u32[]{:S(2)}, u32[]{:S(2)}) collective-permute-start(f32[3,17,1]{2,1,0:T(8,128)S(1)} %pad_maximum_fusion.23), channel_id=1, source_target_pairs={{0,1},{1,2},{2,3},{3,4},{4,5},{5,6},{6,7},{7,8},{8,9},{9,10},{10,1... | collective-permute-start | bytes 620 | tf_op jit(solution)/shard_map/ppermute | solution.py:29
  282.5 1.0 collective-permute-done.21
  285.2 2.1 collective-permute-start.22
  287.3 4.7 %collective-permute-done.22 = f32[3,1,128]{2,1,0:T(1,128)S(1)} collective-permute-done((f32[3,1,128]{2,1,0:T(1,128)S(1)}, f32[3,1,128]{2,1,0:T(1,128)S(1)}, u32[]{:S(2)}, u32[]{:S(2)}) %collective-permute-start.22) | collective-permute-done | bytes 1568 | tf_op jit(solution)/shard_map/ppermute | solution.py:29
  292.1 1.3 collective-permute-start.23
  293.3 7.9 %collective-permute-done.23 = f32[3,9,1]{2,1,0:T(8,128)S(1)} collective-permute-done((f32[3,9,1]{2,1,0:T(8,128)S(1)}, f32[3,9,1]{2,1,0:T(8,128)S(1)}, u32[]{:S(2)}, u32[]{:S(2)}) %collective-permute-start.23) | collective-permute-done | bytes 140 | tf_op jit(solution)/shard_map/ppermute | solution.py:29
  302.6 3.1 collective-permute-start.24
  306.5 7.6 %collective-permute-start.25 = (f32[3,17,1]{2,1,0:T(8,128)S(1)}, f32[3,17,1]{2,1,0:T(8,128)S(1)}, u32[]{:S(2)}, u32[]{:S(2)}) collective-permute-start(f32[3,17,1]{2,1,0:T(8,128)S(1)} %pad_maximum_fusion.22), channel_id=1, source_target_pairs={{0,1},{1,2},{2,3},{3,4},{4,5},{5,6},{6,7},{7,8},{8,9},{9,10},{10,1... | collective-permute-start | bytes 620 | tf_op jit(solution)/shard_map/ppermute | solution.py:29
  314.2 0.8 copy.47
  317.4 113.4 %all-reduce.10 = (f32[]{:T(128)}, f32[]{:T(128)}) all-reduce(f32[]{:T(128)} %abs_reduce_fusion.1, f32[]{:T(128)} %get-tuple-element.11), channel_id=1, replica_groups=mesh['gx'=32,'gy'=16] {'gx','gy'}, use_global_device_ids=true, to_apply=%region_4.5 | all-reduce | flops 2 | bytes 16 | tf_op jit(solution)/shard_map/pmax | solution.py:210
  (178 shorter events, 23.3 us)
Async XLA Ops:
  0.6 20.6 %copy-start.1 = (f32[8,16,256]{2,1,0:T(8,128)S(1)}, f32[8,16,256]{2,1,0:T(8,128)}, u32[]{:S(2)}) copy-start(f32[8,16,256]{2,1,0:T(8,128)} %param.13) | copy-start | bytes 393220
  0.6 20.6 %copy-start.2 = (f32[8,16,256]{2,1,0:T(8,128)S(1)}, f32[8,16,256]{2,1,0:T(8,128)}, u32[]{:S(2)}) copy-start(f32[8,16,256]{2,1,0:T(8,128)} %param.14) | copy-start | bytes 393220
  1.8 19.5 %copy-start.4 = (f32[8,16,256]{2,1,0:T(8,128)S(1)}, f32[8,16,256]{2,1,0:T(8,128)}, u32[]{:S(2)}) copy-start(f32[8,16,256]{2,1,0:T(8,128)} %param.12) | copy-start | bytes 393220
  1.8 170.7 %collective-permute-start = (f32[3,8,2,256]{3,2,1,0:T(2,128)S(1)}, f32[3,8,2,256]{3,2,1,0:T(2,128)S(1)}, u32[]{:S(2)}, u32[]{:S(2)}) collective-permute-start(f32[3,8,2,256]{3,2,1,0:T(2,128)S(1)} %get-tuple-element.29), channel_id=1, source_target_pairs={{0,16},{16,32},{32,48},{48,64},{64,80},{80,96},{96,112},{112,128},... | collective-permute-start | bytes 147464 | tf_op jit(solution)/shard_map/ppermute | solution.py:17
  6.5 166.0 %collective-permute-start.1 = (f32[3,8,2,256]{3,2,1,0:T(2,128)S(1)}, f32[3,8,2,256]{3,2,1,0:T(2,128)S(1)}, u32[]{:S(2)}, u32[]{:S(2)}) collective-permute-start(f32[3,8,2,256]{3,2,1,0:T(2,128)S(1)} %get-tuple-element.30), channel_id=1, source_target_pairs={{16,0},{32,16},{48,32},{64,48},{80,64},{96,80},{112,96},{128,112},... | collective-permute-start | bytes 147464 | tf_op jit(solution)/shard_map/ppermute | solution.py:19
  12.7 119.8 %collective-permute-start.8 = (f32[3,1,128]{2,1,0:T(1,128)S(1)}, f32[3,1,128]{2,1,0:T(1,128)S(1)}, u32[]{:S(2)}, u32[]{:S(2)}) collective-permute-start(f32[3,1,128]{2,1,0:T(1,128)S(1)} %slice.1377), channel_id=1, source_target_pairs={{16,0},{32,16},{48,32},{64,48},{80,64},{96,80},{112,96},{128,112},... | collective-permute-start | bytes 4616 | tf_op jit(solution)/shard_map/ppermute | solution.py:29
  15.6 126.3 %collective-permute-start.4 = (f32[3,8,2,128]{3,2,1,0:T(2,128)S(1)}, f32[3,8,2,128]{3,2,1,0:T(2,128)S(1)}, u32[]{:S(2)}, u32[]{:S(2)}) collective-permute-start(f32[3,8,2,128]{3,2,1,0:T(2,128)S(1)} %get-tuple-element.35), channel_id=1, source_target_pairs={{0,16},{16,32},{32,48},{48,64},{64,80},{80,96},{96,112},{112,128},... | collective-permute-start | bytes 73736 | tf_op jit(solution)/shard_map/ppermute | solution.py:17
  19.3 122.7 %collective-permute-start.5 = (f32[3,8,2,128]{3,2,1,0:T(2,128)S(1)}, f32[3,8,2,128]{3,2,1,0:T(2,128)S(1)}, u32[]{:S(2)}, u32[]{:S(2)}) collective-permute-start(f32[3,8,2,128]{3,2,1,0:T(2,128)S(1)} %get-tuple-element.36), channel_id=1, source_target_pairs={{16,0},{32,16},{48,32},{64,48},{80,64},{96,80},{112,96},{128,112},... | collective-permute-start | bytes 73736 | tf_op jit(solution)/shard_map/ppermute | solution.py:19
  21.3 0.8 copy-start.5
  21.3 0.8 copy-start.6
  21.3 0.8 copy-start.8
  132.6 9.0 %collective-permute-start.9 = (f32[3,9,1]{2,1,0:T(8,128)S(1)}, f32[3,9,1]{2,1,0:T(8,128)S(1)}, u32[]{:S(2)}, u32[]{:S(2)}) collective-permute-start(f32[3,9,1]{2,1,0:T(8,128)S(1)} %pad_maximum_fusion.32), channel_id=1, source_target_pairs={{1,0},{2,1},{3,2},{4,3},{5,4},{6,5},{7,6},{8,7},{9,8},{10,9},{11,1... | collective-permute-start | bytes 332 | tf_op jit(solution)/shard_map/ppermute | solution.py:29
  141.8 0.9 copy-start.3
  142.9 18.0 %collective-permute-start.6 = (f32[3,8,12,2]{3,2,1,0:T(8,128)S(1)}, f32[3,8,12,2]{3,2,1,0:T(8,128)S(1)}, u32[]{:S(2)}, u32[]{:S(2)}) collective-permute-start(f32[3,8,12,2]{3,2,1,0:T(8,128)S(1)} %get-tuple-element.31), channel_id=1, source_target_pairs={{0,1},{1,2},{2,3},{3,4},{4,5},{5,6},{6,7},{7,8},{8,9},{9,10},{10,1... | collective-permute-start | bytes 6920 | tf_op jit(solution)/shard_map/ppermute | solution.py:17
  146.8 24.6 %collective-permute-start.7 = (f32[3,8,12,2]{3,2,1,0:T(8,128)S(1)}, f32[3,8,12,2]{3,2,1,0:T(8,128)S(1)}, u32[]{:S(2)}, u32[]{:S(2)}) collective-permute-start(f32[3,8,12,2]{3,2,1,0:T(8,128)S(1)} %get-tuple-element.32), channel_id=1, source_target_pairs={{1,0},{2,1},{3,2},{4,3},{5,4},{6,5},{7,6},{8,7},{9,8},{10,9},{11,1... | collective-permute-start | bytes 6920 | tf_op jit(solution)/shard_map/ppermute | solution.py:19
  172.1 1.0 copy-start
  173.4 14.3 %collective-permute-start.2 = (f32[3,8,20,2]{3,2,1,0:T(8,128)S(1)}, f32[3,8,20,2]{3,2,1,0:T(8,128)S(1)}, u32[]{:S(2)}, u32[]{:S(2)}) collective-permute-start(f32[3,8,20,2]{3,2,1,0:T(8,128)S(1)} %get-tuple-element.21), channel_id=1, source_target_pairs={{0,1},{1,2},{2,3},{3,4},{4,5},{5,6},{6,7},{7,8},{8,9},{9,10},{10,1... | collective-permute-start | bytes 11528 | tf_op jit(solution)/shard_map/ppermute | solution.py:17
  178.6 24.3 %collective-permute-start.3 = (f32[3,8,20,2]{3,2,1,0:T(8,128)S(1)}, f32[3,8,20,2]{3,2,1,0:T(8,128)S(1)}, u32[]{:S(2)}, u32[]{:S(2)}) collective-permute-start(f32[3,8,20,2]{3,2,1,0:T(8,128)S(1)} %get-tuple-element.22), channel_id=1, source_target_pairs={{1,0},{2,1},{3,2},{4,3},{5,4},{6,5},{7,6},{8,7},{9,8},{10,9},{11,1... | collective-permute-start | bytes 11528 | tf_op jit(solution)/shard_map/ppermute | solution.py:19
  205.8 0.9 slice-start
  205.8 1.1 copy-start.7
  207.0 2.0 slice-start.1
  207.0 2.0 copy-start.9
  207.0 3.9 collective-permute-start.12
  209.0 9.2 %collective-permute-start.10 = (f32[3,1,256]{2,1,0:T(1,128)S(1)}, f32[3,1,256]{2,1,0:T(1,128)S(1)}, u32[]{:S(2)}, u32[]{:S(2)}) collective-permute-start(f32[3,1,256]{2,1,0:T(1,128)S(1)} %slice.1385), channel_id=1, source_target_pairs={{0,16},{16,32},{32,48},{48,64},{64,80},{80,96},{96,112},{112,128},... | collective-permute-start | bytes 9224 | tf_op jit(solution)/shard_map/ppermute | solution.py:29
  211.0 9.3 %collective-permute-start.13 = (f32[3,17,1]{2,1,0:T(8,128)S(1)}, f32[3,17,1]{2,1,0:T(8,128)S(1)}, u32[]{:S(2)}, u32[]{:S(2)}) collective-permute-start(f32[3,17,1]{2,1,0:T(8,128)S(1)} %pad_maximum_fusion.25), channel_id=1, source_target_pairs={{0,1},{1,2},{2,3},{3,4},{4,5},{5,6},{6,7},{7,8},{8,9},{9,10},{10,1... | collective-permute-start | bytes 620 | tf_op jit(solution)/shard_map/ppermute | solution.py:29
  218.3 3.7 collective-permute-start.11
  224.3 5.7 %collective-permute-start.14 = (f32[3,1,128]{2,1,0:T(1,128)S(1)}, f32[3,1,128]{2,1,0:T(1,128)S(1)}, u32[]{:S(2)}, u32[]{:S(2)}) collective-permute-start(f32[3,1,128]{2,1,0:T(1,128)S(1)} %slice.1387), channel_id=1, source_target_pairs={{16,0},{32,16},{48,32},{64,48},{80,64},{96,80},{112,96},{128,112},... | collective-permute-start | bytes 4616 | tf_op jit(solution)/shard_map/ppermute | solution.py:29
  230.0 9.4 %collective-permute-start.15 = (f32[3,9,1]{2,1,0:T(8,128)S(1)}, f32[3,9,1]{2,1,0:T(8,128)S(1)}, u32[]{:S(2)}, u32[]{:S(2)}) collective-permute-start(f32[3,9,1]{2,1,0:T(8,128)S(1)} %pad_maximum_fusion.31), channel_id=1, source_target_pairs={{1,0},{2,1},{3,2},{4,3},{5,4},{6,5},{7,6},{8,7},{9,8},{10,9},{11,1... | collective-permute-start | bytes 332 | tf_op jit(solution)/shard_map/ppermute | solution.py:29
  240.7 3.5 collective-permute-start.16
  244.3 8.6 %collective-permute-start.17 = (f32[3,17,1]{2,1,0:T(8,128)S(1)}, f32[3,17,1]{2,1,0:T(8,128)S(1)}, u32[]{:S(2)}, u32[]{:S(2)}) collective-permute-start(f32[3,17,1]{2,1,0:T(8,128)S(1)} %pad_maximum_fusion.24), channel_id=1, source_target_pairs={{0,1},{1,2},{2,3},{3,4},{4,5},{5,6},{6,7},{7,8},{8,9},{9,10},{10,1... | collective-permute-start | bytes 620 | tf_op jit(solution)/shard_map/ppermute | solution.py:29
  254.5 6.3 %collective-permute-start.18 = (f32[3,1,128]{2,1,0:T(1,128)S(1)}, f32[3,1,128]{2,1,0:T(1,128)S(1)}, u32[]{:S(2)}, u32[]{:S(2)}) collective-permute-start(f32[3,1,128]{2,1,0:T(1,128)S(1)} %slice.1395), channel_id=1, source_target_pairs={{16,0},{32,16},{48,32},{64,48},{80,64},{96,80},{112,96},{128,112},... | collective-permute-start | bytes 4616 | tf_op jit(solution)/shard_map/ppermute | solution.py:29
  260.8 9.1 %collective-permute-start.19 = (f32[3,9,1]{2,1,0:T(8,128)S(1)}, f32[3,9,1]{2,1,0:T(8,128)S(1)}, u32[]{:S(2)}, u32[]{:S(2)}) collective-permute-start(f32[3,9,1]{2,1,0:T(8,128)S(1)} %pad_maximum_fusion.30), channel_id=1, source_target_pairs={{1,0},{2,1},{3,2},{4,3},{5,4},{6,5},{7,6},{8,7},{9,8},{10,9},{11,1... | collective-permute-start | bytes 332 | tf_op jit(solution)/shard_map/ppermute | solution.py:29
  271.3 3.8 collective-permute-start.20
  275.1 8.4 %collective-permute-start.21 = (f32[3,17,1]{2,1,0:T(8,128)S(1)}, f32[3,17,1]{2,1,0:T(8,128)S(1)}, u32[]{:S(2)}, u32[]{:S(2)}) collective-permute-start(f32[3,17,1]{2,1,0:T(8,128)S(1)} %pad_maximum_fusion.23), channel_id=1, source_target_pairs={{0,1},{1,2},{2,3},{3,4},{4,5},{5,6},{6,7},{7,8},{8,9},{9,10},{10,1... | collective-permute-start | bytes 620 | tf_op jit(solution)/shard_map/ppermute | solution.py:29
  285.2 6.8 %collective-permute-start.22 = (f32[3,1,128]{2,1,0:T(1,128)S(1)}, f32[3,1,128]{2,1,0:T(1,128)S(1)}, u32[]{:S(2)}, u32[]{:S(2)}) collective-permute-start(f32[3,1,128]{2,1,0:T(1,128)S(1)} %slice.1403), channel_id=1, source_target_pairs={{16,0},{32,16},{48,32},{64,48},{80,64},{96,80},{112,96},{128,112},... | collective-permute-start | bytes 4616 | tf_op jit(solution)/shard_map/ppermute | solution.py:29
  292.1 9.2 %collective-permute-start.23 = (f32[3,9,1]{2,1,0:T(8,128)S(1)}, f32[3,9,1]{2,1,0:T(8,128)S(1)}, u32[]{:S(2)}, u32[]{:S(2)}) collective-permute-start(f32[3,9,1]{2,1,0:T(8,128)S(1)} %pad_maximum_fusion.29), channel_id=1, source_target_pairs={{1,0},{2,1},{3,2},{4,3},{5,4},{6,5},{7,6},{8,7},{9,8},{10,9},{11,1... | collective-permute-start | bytes 332 | tf_op jit(solution)/shard_map/ppermute | solution.py:29
  302.6 3.8 collective-permute-start.24
  306.5 8.7 %collective-permute-start.25 = (f32[3,17,1]{2,1,0:T(8,128)S(1)}, f32[3,17,1]{2,1,0:T(8,128)S(1)}, u32[]{:S(2)}, u32[]{:S(2)}) collective-permute-start(f32[3,17,1]{2,1,0:T(8,128)S(1)} %pad_maximum_fusion.22), channel_id=1, source_target_pairs={{0,1},{1,2},{2,3},{3,4},{4,5},{5,6},{6,7},{7,8},{8,9},{9,10},{10,1... | collective-permute-start | bytes 620 | tf_op jit(solution)/shard_map/ppermute | solution.py:29
where the time goes:
time: 434 us; the launch traced here: 433 us
  blocking collectives  222 us (51%)
  waiting for transfers between devices  90.3 us (21%)
  starting transfers between devices  87.4 us (20%)
  local copies, waits for them, and re-layouts  17.5 us (4%)
  other arithmetic  9.82 us (2%)
  between operations  6.14 us (1%)
    pmax x1, blocking collectives, shards(): last_max = lax.pmax(last_local, ('gx', 'gy'))  113 us
    pmax x1, blocking collectives, shards(): wave_peak = lax.pmax(local_peak, ('gx', 'gy'))  109 us
    ppermute x18, starting transfers between devices, shifted(): lax.ppermute(value, axis, [(source, source + steps) for source in range(l...  60 us
    ppermute x18, waiting for transfers between devices, shifted(): lax.ppermute(value, axis, [(source, source + steps) for source in range(l...  45.1 us
    ppermute x4, waiting for transfers between devices, padded_2(): lax.ppermute(head, axis, [((i + 1) % count, i) for i in range(ends)])  25.7 us
    ppermute x4, waiting for transfers between devices, padded_2(): lax.ppermute(tail, axis, [(i, (i + 1) % count) for i in range(ends)])  19.6 us
    ppermute x4, starting transfers between devices, padded_2(): lax.ppermute(tail, axis, [(i, (i + 1) % count) for i in range(ends)])  17.4 us
    ppermute x4, starting transfers between devices, padded_2(): lax.ppermute(head, axis, [((i + 1) % count, i) for i in range(ends)])  9.99 us
  transfers between devices with their start and end apart: 26, of which 17 were waited for; matrix products, arithmetic and copies ran while one was open for 2% of the time, Pallas kernels for 0%

commit v1 on v0

v1 whole, which is shorter than its diff:
```python
import jax
import jax.numpy as jnp
import ml_dtypes
import numpy as np
from jax import lax
from jax.experimental import pallas as pl
from jax.experimental.pallas import tpu as pltpu
from jax.sharding import PartitionSpec as P

ITERS = 3
LANES = 128
NAMES = ("fn", "fb", "fd", "fs", "fl", "cn", "cb", "cd", "cs", "cl")

DEEP_NOW = [("fn", (c, k)) for c in range(3) for k in (5, 6, 7)]
THIN_NOW = [("fn", (c, k)) for c in range(3) for k in range(5)]
DEEP_REST = [("fb", (c, 6)) for c in range(3)] + [("fd", (6,)), ("fs", (6,)), ("fl", (6,)), ("fs", (7,)), ("fl", (7,))]
COARSE_NOW = [("cn", (c, k)) for c in range(3) for k in range(3)]
COARSE_REST = [("cb", (c, k)) for c in range(3) for k in range(2)] + [
    ("cd", (1,)),
    ("cs", (0,)),
    ("cl", (0,)),
    ("cs", (1,)),
    ("cl", (1,)),
]
COARSE_THIN = [("cn", (c, k)) for c in range(3) for k in range(3, 8)]

TILE_ROWS = {"A": (0, 16), "B": (16, 16), "C": (32, 8)}
TILE_RIM = {"A": 9, "B": 7, "C": 5}
PACKED_ROWS = 40


def plan():
    entries, lane, row = [], {"A": 0, "B": 0, "C": 0}, 0
    for tile, keys, low, high in (
        ("A", DEEP_NOW, 9, 8),
        ("A", THIN_NOW, 2, 2),
        ("B", DEEP_REST, 7, 6),
        ("C", COARSE_NOW, 5, 5),
        ("C", COARSE_REST, 4, 4),
        ("C", COARSE_THIN, 2, 2),
    ):
        for key in keys:
            own = 1 if tile == "C" else 2
            entries.append((key, low, high, tile, lane[tile], row, own))
            lane[tile] += low
            row += own * low
    corners = []
    for tile in "ABC":
        for side in range(2):
            corners.append((tile, side, row))
            row += TILE_RIM[tile]
    return entries, corners, -(-row // 8) * 8


ENTRIES, CORNERS, RIM_ROWS = plan()

SLOTS = 31
PEAK_LANE = 31
FLAG_LANE = 63
STEP_LOW = 0.02
FAR = -1.0e30


def iota(shape, dim):
    return lax.broadcasted_iota(jnp.int32, shape, dim)


def turned(value, steps, axis):
    size = value.shape[axis]
    steps = steps % size
    return value if steps == 0 else pltpu.roll(value, steps, axis)


def own_tile(refs, key, tile):
    name, index = key
    return refs[name][index + (slice(None), slice(tile * LANES, (tile + 1) * LANES))]


def pack_columns(*refs):
    named = dict(zip(NAMES, refs[:10]))
    low_out, high_out = refs[10:]
    for tile, (base, rows) in TILE_ROWS.items():
        lane = iota((rows, LANES), 1)
        low_sum = jnp.zeros((rows, LANES), jnp.float32)
        high_sum = low_sum
        for key, low, _, where, at, _, own in ENTRIES:
            if where != tile:
                continue
            inside = (lane >= at) & (lane < at + low)
            low_sum = jnp.where(inside, turned(own_tile(named, key, own - 1), at + low, 1), low_sum)
            high_sum = jnp.where(inside, turned(own_tile(named, key, 0), at, 1), high_sum)
        low_out[base : base + rows, :] = low_sum
        high_out[base : base + rows, :] = high_sum


def pack_rows(*refs):
    named = dict(zip(NAMES, refs[:10]))
    sides = refs[10:12]
    low_out, high_out = refs[12:]
    low_out[RIM_ROWS - 8 :, :] = jnp.zeros((8, LANES), jnp.float32)
    high_out[RIM_ROWS - 8 :, :] = jnp.zeros((8, LANES), jnp.float32)
    for (name, index), low, high, _, _, row, own in ENTRIES:
        ref = named[name]
        rows = ref.shape[-2]
        for tile in range(own):
            lanes = slice(tile * LANES, (tile + 1) * LANES)
            start = row + tile * low
            low_out[start : start + low, :] = ref[index + (slice(rows - low, rows), lanes)]
            high_out[start : start + high, :] = ref[index + (slice(0, high), lanes)]
            if high < low:
                high_out[start + high : start + low, :] = jnp.zeros((low - high, LANES), jnp.float32)
    for tile, side, row in CORNERS:
        base, rows = TILE_ROWS[tile]
        rim = TILE_RIM[tile]
        low_out[row : row + rim, :] = sides[side][base + rows - rim : base + rows, :]
        high_out[row : row + rim, :] = sides[side][base : base + rim, :]


def across(tiles, steps, wanted):
    count = len(tiles)
    lane = iota(tiles[0].shape, 1)
    rolled = [turned(tile, -steps, 1) for tile in tiles]
    if steps > 0:
        return [jnp.where(lane < LANES - steps, rolled[t], rolled[(t + 1) % count]) for t in range(wanted)]
    return [jnp.where(lane >= -steps, rolled[t], rolled[(t - 1) % count]) for t in range(wanted)]


def first_of(down2, down1, up1, up2, spacing):
    return (8.0 * (up1 - down1) - (up2 - down2)) * (1.0 / (12.0 * spacing))


def second_of(down2, down1, here, up1, up2, spacing):
    return (16.0 * (up1 + down1) - (up2 + down2) - 30.0 * here) * (1.0 / (12.0 * spacing * spacing))


def across_all(tiles, wanted):
    return [across(tiles, steps, wanted) for steps in (-2, -1, 1, 2)]


def slopes(field, along_x, along_y, plane, start, rows, wanted, spacing):
    count = field.shape[2]
    for t in range(count):
        down2, down1, up1, up2 = (field[0, plane, t, pl.ds(start + d, rows), :] for d in (-2, -1, 1, 2))
        along_x[plane, t, start : start + rows, :] = first_of(down2, down1, up1, up2, spacing)
    span = slice(start - 4, start + rows + 4)
    shifted = across_all([field[1, plane, t, span, :] for t in range(count)], wanted)
    for t in range(wanted):
        along_y[plane, t, span, :] = first_of(*(s[t] for s in shifted), spacing)


def acceleration(field, along_x, along_y, mixed, planes, start, rows, wanted, spacing, shear, lame):
    above, plane, under = planes
    count = field.shape[2]
    half = 1.0 / (2.0 * spacing)
    square = 1.0 / (spacing * spacing)
    span = slice(start, start + rows)
    wide = slice(start - 4, start + rows + 4)
    for t in range(wanted):
        mixed[t, wide, :] = along_y[plane, t, wide, :] + half * (
            field[2, under, t, wide, :] - field[2, above, t, wide, :]
        )
    twist = [
        along_x[plane, t, span, :] + half * (field[2, under, t, span, :] - field[2, above, t, span, :])
        for t in range(count)
    ]
    twist = across_all(twist, wanted)
    laps, seconds = [], []
    for c in range(3):
        shifted = across_all([field[c, plane, t, span, :] for t in range(count)], wanted)
        lap, second = [], []
        for t in range(wanted):
            here = field[c, plane, t, span, :]
            down2, down1, up1, up2 = (field[c, plane, t, pl.ds(start + d, rows), :] for d in (-2, -1, 1, 2))
            in_x = second_of(down2, down1, here, up1, up2, spacing)
            in_y = second_of(shifted[0][t], shifted[1][t], here, shifted[2][t], shifted[3][t], spacing)
            in_z = square * (field[c, under, t, span, :] - 2.0 * here + field[c, above, t, span, :])
            lap.append(in_x + in_y + in_z)
            second.append((in_x, in_y, in_z)[c])
        laps.append(lap)
        seconds.append(second)
    out = [[], [], []]
    for t in range(wanted):
        ends = (mixed[t, pl.ds(start + d, rows), :] for d in (-2, -1, 1, 2))
        div_x = seconds[0][t] + first_of(*ends, spacing)
        div_y = seconds[1][t] + first_of(*(s[t] for s in twist), spacing)
        lower = along_x[under, t, span, :] + along_y[under, t, span, :]
        upper = along_x[above, t, span, :] + along_y[above, t, span, :]
        div_z = seconds[2][t] + half * (lower - upper)
        bulk = lame[t] + shear[t]
        for c, div in enumerate((div_x, div_y, div_z)):
            out[c].append(shear[t] * laps[c][t] + bulk * div)
    return out


def exact_dot(value, pick):
    high = value.astype(jnp.bfloat16)
    rest = value - high.astype(jnp.float32)
    middle = rest.astype(jnp.bfloat16)
    low = (rest - middle.astype(jnp.float32)).astype(jnp.bfloat16)
    dot = lambda part: jnp.dot(part, pick, preferred_element_type=jnp.float32)
    return dot(high) + (dot(middle) + dot(low))


def prolonged(tiles):
    odd_x = [0.5 * (tile + turned(tile, -1, 0)) for tile in tiles]
    next_y = across(tiles, 1, 2)
    next_odd = across(odd_x, 1, 2)
    return (
        tiles,
        [0.5 * (a + b) for a, b in zip(tiles, next_y)],
        odd_x,
        [0.5 * (a + b) for a, b in zip(odd_x, next_odd)],
    )


def restricted(parts):
    even_even, even_odd, odd_even, odd_odd = parts
    even = [0.5 * a + 0.25 * (b + turned(b, 1, 0)) for a, b in zip(even_even, odd_even)]
    odd = [0.5 * a + 0.25 * (b + turned(b, 1, 0)) for a, b in zip(even_odd, odd_odd)]
    return [0.5 * a + 0.25 * (b + c) for a, b, c in zip(even, odd, across(odd, -1, 2))]


def largest(values):
    total = values[0]
    for value in values[1:]:
        total = jnp.maximum(total, value)
    return jnp.max(total)


def start_line(lines):
    ends = [a + STEP_LOW * b for a, b in lines]
    top = largest(ends)
    slope = largest([jnp.where(e == top, b, FAR) for e, (_, b) in zip(ends, lines)])
    begin = largest([jnp.where((e == top) & (b == slope), a, FAR) for e, (a, b) in zip(ends, lines)])
    return begin, slope


def next_line(lines, begin, slope, limit):
    crossings = []
    for a, b in lines:
        steeper = b - slope
        crossings.append(jnp.where(steeper > 0.0, (begin - a) / steeper, -FAR))
    nearest = -largest([-s for s in crossings])
    found = nearest <= limit
    new_slope = largest([jnp.where(s == nearest, b, FAR) for s, (_, b) in zip(crossings, lines)])
    new_begin = largest(
        [jnp.where((s == nearest) & (b == new_slope), a, FAR) for s, (a, b) in zip(crossings, lines)]
    )
    return jnp.where(found, new_begin, begin), jnp.where(found, new_slope, slope), found


def envelopes(first, last, peak):
    lane = iota((1, LANES), 1)
    bound = 0.3 / jnp.full((8, LANES), peak, jnp.float32)
    limit = jnp.max(bound * bound) * 1.00001
    first_begin, first_slope = start_line(first)
    last_begin, last_slope = start_line(last)
    message = jnp.where(
        lane < 32,
        first_begin,
        jnp.where(lane < 64, first_slope, jnp.where(lane < 96, last_begin, last_slope)),
    )

    def more(state):
        return (state[0] < SLOTS) & (state[1] > 0)

    def step(state):
        n, _, fa, fb, la, lb, message = state
        message = jnp.where(lane == n, fa, message)
        message = jnp.where(lane == n + 32, fb, message)
        message = jnp.where(lane == n + 64, la, message)
        message = jnp.where(lane == n + 96, lb, message)
        fa, fb, found_first = next_line(first, fa, fb, limit)
        la, lb, found_last = next_line(last, la, lb, limit)
        found = (found_first | found_last).astype(jnp.int32)
        return n + 1, found, fa, fb, la, lb, message

    start = (jnp.int32(0), jnp.int32(1), first_begin, first_slope, last_begin, last_slope, message)
    _, left, _, _, _, _, message = lax.while_loop(more, step, start)
    return message, left.astype(jnp.float32)


def sealed(message, peak, flag):
    lane = iota((1, LANES), 1)
    return jnp.where(lane == PEAK_LANE, peak, jnp.where(lane == FLAG_LANE, flag, message))


def opened(received):
    first, last = [], []
    rows = received.shape[0]
    lane = iota((8, LANES), 1)
    peak, flag = [], []
    for r in range(0, rows, 8):
        begin = received[r : r + 8, :]
        slope = turned(begin, -32, 1)
        in_first = lane < SLOTS
        in_last = (lane >= 64) & (lane < 64 + SLOTS)
        first.append((jnp.where(in_first, begin, FAR), jnp.where(in_first, slope, 0.0)))
        last.append((jnp.where(in_last, begin, FAR), jnp.where(in_last, slope, 0.0)))
        peak.append(jnp.where(lane == PEAK_LANE, begin, 0.0))
        flag.append(jnp.where(lane == FLAG_LANE, begin, 0.0))
    return first, last, largest(peak), largest(flag)


def main_kernel(*refs):
    named = dict(zip(NAMES, refs[:10]))
    place, side_low, side_high, row_low, row_high, split_pick, weave_pick = refs[10:17]
    fine_rate, coarse_rate, plane_out, iterate_out, lines_out, message_out = refs[17:23]
    fine, fine_x, fine_y, rest, coarse, coarse_x, coarse_y, coarse_rest = refs[23:31]
    mixed, planes, parted, woven, ends = refs[31:36]
    packed = dict(zip("ABC", zip(refs[36:39], refs[39:42])))

    for tile in "ABC":
        base, rows = TILE_ROWS[tile]
        rim = TILE_RIM[tile]
        for side, source in enumerate((side_low, side_high)):
            target = packed[tile][side]
            target[...] = jnp.zeros(target.shape, jnp.float32)
            target[rows : 2 * rows, :] = source[base : base + rows, :]
            row = [r for t, s, r in CORNERS if t == tile and s == side][0]
            target[rows - rim : rows, :] = row_low[row : row + rim, :]
            high = min(rim, 8)
            target[2 * rows : 2 * rows + high, :] = row_high[row : row + high, :]

    slot = {key: i for i, key in enumerate(DEEP_REST)}
    coarse_slot = {key: i for i, key in enumerate(COARSE_REST)}

    def home(key):
        if key in slot:
            return rest.at[slot[key]]
        if key in coarse_slot:
            return coarse_rest.at[coarse_slot[key]]
        return (fine if key[0] == "fn" else coarse).at[key[1]]

    for key, low, high, tile, at, row, own in ENTRIES:
        target = home(key)
        rows = TILE_ROWS[tile][1]
        total = target.shape[1]
        if low > 2:
            for t in range(own):
                target[t, 0:rows, :] = jnp.zeros((rows, LANES), jnp.float32)
                target[t, 2 * rows : total, :] = jnp.zeros((total - 2 * rows, LANES), jnp.float32)
        for t in range(own):
            target[t, rows : 2 * rows, :] = own_tile(named, key, t)
            begin = row + t * low
            target[t, rows - low : rows, :] = row_low[begin : begin + low, :]
            target[t, 2 * rows : 2 * rows + high, :] = row_high[begin : begin + high, :]
        low_side, high_side = packed[tile][0][...], packed[tile][1][...]
        lane = iota(low_side.shape, 1)
        target[own, :, :] = jnp.where(
            lane < high,
            turned(high_side, -at, 1),
            jnp.where(lane >= LANES - low, turned(low_side, -(at + low), 1), 0.0),
        )
    coarse[:, 8] = jnp.zeros(coarse.shape[:1] + coarse.shape[2:], jnp.float32)

    def fine_slopes(k, carry):
        slopes(fine, fine_x, fine_y, k, 16, 16, 2, 1.0)
        return carry

    lax.fori_loop(0, 5, fine_slopes, 0)
    for k in (5, 6, 7):
        slopes(fine, fine_x, fine_y, k, 8, 32, 3, 1.0)

    def fine_plane(k, carry):
        above = jnp.where(k == 0, 1, k - 1)
        own = [slice(t * LANES, (t + 1) * LANES) for t in range(2)]
        shear = [named["fs"][k, :, lanes] for lanes in own]
        lame = [named["fl"][k, :, lanes] for lanes in own]
        accel = acceleration(fine, fine_x, fine_y, mixed, (above, k, k + 1), 16, 16, 2, 1.0, shear, lame)
        for c in range(3):
            for t in range(2):
                fine_rate[c, k, :, own[t]] = accel[c][t] / named["fd"][k, :, own[t]]
        return carry

    lax.fori_loop(0, 6, fine_plane, 0)

    window = slice(8, 40)
    shear = [rest[slot[("fs", (6,))], t, window, :] for t in range(3)]
    lame = [rest[slot[("fl", (6,))], t, window, :] for t in range(3)]
    accel = acceleration(fine, fine_x, fine_y, mixed, (5, 6, 7), 8, 32, 3, 1.0, shear, lame)
    for t in range(3):
        density = rest[slot[("fd", (6,))], t, window, :]
        filled = density > 0.0
        density = jnp.where(filled, density, 1.0)
        for c in range(3):
            rate = jnp.where(filled, accel[c][t] / density, 0.0)
            planes[3 + c, t, :, :] = rate
            planes[c, t, :, :] = 2.0 * fine[c, 6, t, window, :] - rest[c, t, window, :]
            if t < 2:
                fine_rate[c, 6, :, t * LANES : (t + 1) * LANES] = rate[8:24, :]
        fine_shear = rest[slot[("fs", (7,))], t, window, :]
        planes[6, t, :, :] = fine_shear
        planes[7, t, :, :] = rest[slot[("fl", (7,))], t, window, :] + 2.0 * fine_shear

    stacked = jnp.concatenate(
        [
            jnp.concatenate([planes[p, t, pl.ds(odd, 16, stride=2), :] for t in range(3)], axis=1)
            for p in range(8)
            for odd in range(2)
        ],
        axis=0,
    )
    parted[...] = exact_dot(stacked, split_pick[...])

    def four(p):
        return tuple(
            [
                parted[p * 32 + odd_x * 16 : p * 32 + odd_x * 16 + 16, (odd_y * 2 + t) * LANES : (odd_y * 2 + t + 1) * LANES]
                for t in range(2)
            ]
            for odd_x in range(2)
            for odd_y in range(2)
        )

    for k in range(8):
        slopes(coarse, coarse_x, coarse_y, k, 4, 16, 2, 2.0)
    coarse_x[8] = jnp.zeros(coarse_x.shape[1:], jnp.float32)
    coarse_y[8] = jnp.zeros(coarse_y.shape[1:], jnp.float32)

    def coarse_plane(k, carry):
        shear = [named["cs"][k]]
        lame = [named["cl"][k]]
        accel = acceleration(coarse, coarse_x, coarse_y, mixed, (k - 1, k, k + 1), 8, 8, 1, 2.0, shear, lame)
        for c in range(3):
            coarse_rate[c, k - 1] = accel[c][0] / named["cd"][k]
        return carry

    lax.fori_loop(2, 8, coarse_plane, 0)
    band = slice(4, 20)

    def coarse_pair(name, k):
        return [coarse_rest[coarse_slot[(name, (k,))], t, band, :] for t in range(2)]

    shear, lame, density = coarse_pair("cs", 1), coarse_pair("cl", 1), coarse_pair("cd", 1)
    accel = acceleration(coarse, coarse_x, coarse_y, mixed, (0, 1, 2), 4, 16, 2, 2.0, shear, lame)
    below_rate = [[], [], []]
    for c in range(3):
        for t in range(2):
            filled = density[t] > 0.0
            rate = jnp.where(filled, accel[c][t] / jnp.where(filled, density[t], 1.0), 0.0)
            below_rate[c].append(rate)
        coarse_rate[c, 0] = below_rate[c][0][4:12, :]

    shear, lame = coarse_pair("cs", 0), coarse_pair("cl", 0)
    row = iota((16, LANES), 0) + (place[0] * 8 - 4)
    lane = iota((16, LANES), 1)
    column = [lane, jnp.where(lane < 64, lane + LANES, lane - LANES)]
    fine_moduli = (four(6), four(6), four(7))
    coarse_moduli = (shear, shear, [l + 2.0 * s for l, s in zip(lame, shear)])
    for c in range(3):
        moduli = fine_moduli[c]
        half = [0.5 * m for m in coarse_moduli[c]]
        spread = restricted(moduli)
        inverse = []
        for t in range(2):
            diagonal = half[t] + 0.5625 * spread[t]
            x, y = row, column[t] + place[1] * LANES
            inside = (x >= 0) & (x < place[2]) & (y >= 0) & (y < place[3]) & (diagonal > 0.0)
            inverse.append(jnp.where(inside, 1.0 / jnp.where(inside, diagonal, 1.0), 0.0))
        for part in range(2):
            if part == 0:
                now = [coarse[c, 0, t, band, :] for t in range(2)]
                before = [coarse_rest[coarse_slot[("cb", (c, 0))], t, band, :] for t in range(2)]
                iterate = [2.0 * a - b for a, b in zip(now, before)]
                now = [coarse[c, 1, t, band, :] for t in range(2)]
                before = [coarse_rest[coarse_slot[("cb", (c, 1))], t, band, :] for t in range(2)]
                below = [2.0 * a - b for a, b in zip(now, before)]
            else:
                iterate = [jnp.zeros((16, LANES), jnp.float32)] * 2
                below = below_rate[c]
            above = four(3 * part + c)
            fixed = restricted([[m * a for m, a in zip(ms, as_)] for ms, as_ in zip(moduli, above)])
            fixed = [h * b + f for h, b, f in zip(half, below, fixed)]

            def mismatch_of(iterate):
                stress = [[m * a for m, a in zip(ms, ps)] for ms, ps in zip(moduli, prolonged(iterate))]
                return [h * i + (s - f) for h, i, s, f in zip(half, iterate, restricted(stress), fixed)]

            mismatch = mismatch_of(iterate)
            ends[part, c] = mismatch[0]
            for _ in range(ITERS):
                iterate = [i - m * v for i, m, v in zip(iterate, mismatch, inverse)]
                mismatch = mismatch_of(iterate)
            ends[2 + part, c] = mismatch[0]
            ends[4 + part, c] = iterate[0]
            even_even, even_odd, odd_even, odd_odd = prolonged(iterate)
            at = (part * 3 + c) * 32
            woven[at : at + 16, 0:LANES] = even_even[0]
            woven[at : at + 16, LANES : 2 * LANES] = even_odd[0]
            woven[at + 16 : at + 32, 0:LANES] = odd_even[0]
            woven[at + 16 : at + 32, LANES : 2 * LANES] = odd_odd[0]

    woven[...] = exact_dot(woven[...], weave_pick[...])
    for part in range(2):
        for c in range(3):
            iterate_out[part, c] = ends[4 + part, c, 4:12, :]
            for odd in range(2):
                at = (part * 3 + c) * 32 + odd * 16 + 4
                for t in range(2):
                    plane_out[part, c, t, pl.ds(odd, 8, stride=2), :] = woven[
                        at : at + 8, t * LANES : (t + 1) * LANES
                    ]

    lines = []
    for which in range(2):
        found = []
        for c in range(3):
            begin, slope = ends[2 * which, c, 4:12, :], ends[2 * which + 1, c, 4:12, :]
            lines_out[2 * which, c] = begin
            lines_out[2 * which + 1, c] = slope
            found += [(begin, slope), (-begin, -slope)]
        lines.append(found)
    ratio = (named["fl"][...] + 2.0 * named["fs"][...]) / named["fd"][...]
    coarse_ratio = (named["cl"][...] + 2.0 * named["cs"][...]) / named["cd"][...]
    fine_peak = jnp.sqrt(jnp.full((8, LANES), jnp.max(ratio), jnp.float32))
    coarse_peak = jnp.sqrt(jnp.full((8, LANES), jnp.max(coarse_ratio), jnp.float32))
    peak = jnp.max(jnp.maximum(fine_peak, 0.5 * coarse_peak))
    message, flag = envelopes(lines[0], lines[1], peak)
    message_out[...] = jnp.broadcast_to(sealed(message, peak, flag), message_out.shape)


def merge_kernel(received, message_out):
    first, last, peak, flag = opened(received)
    message, full = envelopes(first, last, peak)
    message_out[...] = jnp.broadcast_to(sealed(message, peak, jnp.maximum(flag, full)), message_out.shape)


def final_kernel(received, fn, fb, cn, cb, fine_rate, coarse_rate, plane, iterate, fine_out, coarse_out, scalars):
    first, last, peak, flag = opened(received)
    step = 0.3 / jnp.full((8, LANES), peak, jnp.float32)
    square = step * step
    first_max = largest([a + square * b for a, b in first])
    last_max = largest([a + square * b for a, b in last])
    reduction = last_max / (jnp.full((8, LANES), first_max, jnp.float32) + 1e-06)
    flag = jnp.where(square < STEP_LOW, 1.0, flag)
    row = iota((8, LANES), 0)
    scalars[...] = jnp.where(row == 0, reduction, jnp.where(row == 1, square, flag))
    square = square[0:1, 0:1]
    for c in range(3):
        fine_out[c, 0:7] = 2.0 * fn[c, 0:7] - fb[c, 0:7] + square * fine_rate[c]
        coarse_out[c, 1:8] = 2.0 * cn[c, 1:8] - cb[c, 1:8] + square * coarse_rate[c]
        coarse_out[c, 0] = iterate[0, c] + square * iterate[1, c]
        for t in range(2):
            fine_out[c, 7, :, t * LANES : (t + 1) * LANES] = plane[0, c, t] + square * plane[1, c, t]


def shifts(count, up):
    return [(i, i + 1) if up else (i + 1, i) for i in range(count - 1)]


def gather_groups(columns, rows):
    near, ring = {}, {}
    for i in range(columns):
        for j in range(rows):
            near.setdefault((i // 8, j % 4), []).append(i * rows + j)
            ring.setdefault((i % 8, j // 4), []).append(i * rows + j)
    return list(near.values()), list(ring.values())


def split_matrix():
    lane = np.arange(3 * LANES)
    fine_column = np.where(lane < 320, lane, lane - 384)[:, None]
    circle = np.arange(2 * LANES)
    coarse_column = np.where(circle < 192, circle, circle - 256)[None, :]
    return np.concatenate(
        [fine_column == 2 * coarse_column, fine_column == 2 * coarse_column + 1], axis=1
    ).astype(ml_dtypes.bfloat16)


def weave_matrix():
    lane = np.arange(2 * LANES)
    target = np.where(lane < LANES, 2 * lane, 2 * (lane - LANES) + 1)[:, None]
    return (target == lane[None, :]).astype(ml_dtypes.bfloat16)


def f32(*shape):
    return jax.ShapeDtypeStruct(shape, jnp.float32)


def vm(*shape):
    return pltpu.VMEM(shape, jnp.float32)


PARAMS = pltpu.CompilerParams(vmem_limit_bytes=48 * 1024 * 1024)


def make_shards(columns, rows):
    near, ring = gather_groups(columns, rows)
    axes = ("gx", "gy")

    def shards(*args):
        fn, fb, fd, fs, fl, cn, cb, cd, cs, cl = args
        in_vmem = pl.BlockSpec(memory_space=pltpu.VMEM)
        call = lambda kernel, n_in, outs, scratch=(), specs=None: pl.pallas_call(
            kernel,
            out_shape=outs,
            in_specs=specs or [in_vmem] * n_in,
            out_specs=[in_vmem] * len(outs) if isinstance(outs, tuple) else in_vmem,
            scratch_shapes=list(scratch),
            compiler_params=PARAMS,
        )
        low, high = call(pack_columns, 10, (f32(PACKED_ROWS, LANES),) * 2)(*args)
        side_low = lax.ppermute(low, "gy", shifts(rows, True))
        side_high = lax.ppermute(high, "gy", shifts(rows, False))
        low, high = call(pack_rows, 12, (f32(RIM_ROWS, LANES),) * 2)(*args, side_low, side_high)
        row_low = lax.ppermute(low, "gx", shifts(columns, True))
        row_high = lax.ppermute(high, "gx", shifts(columns, False))
        place = jnp.stack(
            [
                lax.axis_index("gx"),
                lax.axis_index("gy"),
                jnp.int32(columns * 8),
                jnp.int32(rows * LANES),
            ]
        ).astype(jnp.int32)
        near_size, ring_size = len(near[0]), len(ring[0])
        outs = (
            f32(3, 7, 16, 256),
            f32(3, 7, 8, 128),
            f32(2, 3, 2, 16, 128),
            f32(2, 3, 8, 128),
            f32(4, 3, 8, 128),
            f32(near_size, LANES),
        )
        scratch = (
            vm(3, 8, 3, 48, LANES),
            vm(8, 3, 48, LANES),
            vm(8, 3, 48, LANES),
            vm(8, 3, 48, LANES),
            vm(3, 9, 2, 24, LANES),
            vm(9, 2, 24, LANES),
            vm(9, 2, 24, LANES),
            vm(11, 2, 24, LANES),
            vm(3, 48, LANES),
            vm(8, 3, 32, LANES),
            vm(256, 512),
            vm(192, 256),
            vm(6, 3, 16, LANES),
        ) + (vm(48, LANES), vm(48, LANES), vm(24, LANES)) * 2
        specs = [in_vmem] * 10 + [pl.BlockSpec(memory_space=pltpu.SMEM)] + [in_vmem] * 6
        fine_rate, coarse_rate, plane, iterate, lines, message = call(main_kernel, 17, outs, scratch, specs)(
            *args,
            place,
            side_low,
            side_high,
            row_low,
            row_high,
            jnp.asarray(split_matrix()),
            jnp.asarray(weave_matrix()),
        )
        received = lax.all_to_all(message, axes, 0, 0, tiled=True, axis_index_groups=near)
        message = call(merge_kernel, 1, f32(ring_size, LANES))(received)
        received = lax.all_to_all(message, axes, 0, 0, tiled=True, axis_index_groups=ring)
        fine_next, coarse_next, scalars = call(final_kernel, 9, (f32(*fn.shape), f32(*cn.shape), f32(8, LANES)))(
            received, fn, fb, cn, cb, fine_rate, coarse_rate, plane, iterate
        )

        def plain():
            square = scalars[1, 0]
            values = jnp.abs(lines[0::2] + square * lines[1::2])
            tops = lax.pmax(jnp.max(values, axis=(1, 2, 3)), axes)
            return tops[1] / (tops[0] + 1e-06)

        reduction = lax.cond(scalars[2, 0] > 0.0, plain, lambda: scalars[0, 0])
        return fine_next, coarse_next, reduction

    return shards


def solution(mesh):
    placed = (
        P(None, None, "gx", "gy"),
        P(None, None, "gx", "gy"),
        P(None, "gx", "gy"),
        P(None, "gx", "gy"),
        P(None, "gx", "gy"),
        P(None, None, "gx", "gy"),
        P(None, None, "gx", "gy"),
        P(None, "gx", "gy"),
        P(None, "gx", "gy"),
        P(None, "gx", "gy"),
    )
    return jax.shard_map(
        make_shards(mesh.shape["gx"], mesh.shape["gy"]),
        mesh=mesh,
        in_specs=placed,
        out_specs=(P(None, None, "gx", "gy"), P(None, None, "gx", "gy"), P()),
        check_vma=False,
    )
```

time: 434 us -> 88.5 us (0.20)
  blocking collectives: 222 us -> 34.6 us
  waiting for transfers between devices: 90.3 us -> 14.3 us
  starting transfers between devices: 87.4 us -> 18.1 us
  other arithmetic: 9.82 us -> 0.08 us
  Pallas kernels: 0 us -> 9.33 us
  local copies, waits for them, and re-layouts: 17.5 us -> 9.84 us
  between operations: 6.14 us -> 1.51 us
    pmax x2 -> x0, blocking collectives: 222 us -> none  [the longest x1 113 us: shards(): last_max = lax.pmax(last_local, ('gx', 'gy'))]
    ppermute x26 -> x4, waiting for transfers between devices: 90.3 us -> 14.3 us  [the longest x1 8.67 us: shards(): side_high = lax.ppermute(high, 'gy', shifts(rows, False))]
    ppermute x26 -> x4, starting transfers between devices: 87.4 us -> 18.1 us  [the longest x1 9.64 us: shards(): side_low = lax.ppermute(low, 'gy', shifts(rows, True))]
    all_to_all x0 -> x2, blocking collectives: none -> 34.6 us  [the longest x1 19.9 us: shards(): lax.all_to_all(message, axes, 0, 0, tiled=True, axis_index_groups=ring)]
    slice x55 -> x2, local copies, waits for them, and re-layouts: 11 us -> 1.03 us  [shards(): reduction = lax.cond(scalars[2, 0] > 0.0, plain, lambda: scalars[0, 0])]
    pallas_call x0 -> x5, Pallas kernels: none -> 9.33 us  [the longest x1 6.73 us: shards(): call(main_kernel, 17, outs, scratch, specs)]
    unnamed x26 -> x44, local copies, waits for them, and re-layouts: 3.64 us -> 8.82 us
  transfers between devices with their start and end apart: 26 -> 4, of which waited for: 17 -> 3; matrix products, arithmetic and copies ran while one was open for 2% -> 0% of each run, Pallas kernels for 0% -> 0%
where the time goes in v1:
time: 88.5 us; the launch traced here: 87.8 us
  blocking collectives  34.6 us (39%)
  starting transfers between devices  18.1 us (20%)
  waiting for transfers between devices  14.3 us (16%)
  local copies, waits for them, and re-layouts  9.84 us (11%)
  Pallas kernels  9.33 us (11%)
  between operations  1.51 us (2%)
    all_to_all x1, blocking collectives, shards(): lax.all_to_all(message, axes, 0, 0, tiled=True, axis_index_groups=ring)  19.9 us
    all_to_all x1, blocking collectives, shards(): lax.all_to_all(message, axes, 0, 0, tiled=True, axis_index_groups=near)  14.7 us
    ppermute x1, starting transfers between devices, shards(): side_low = lax.ppermute(low, 'gy', shifts(rows, True))  9.64 us
    unnamed x44, local copies, waits for them, and re-layouts  8.82 us
    ppermute x1, waiting for transfers between devices, shards(): side_high = lax.ppermute(high, 'gy', shifts(rows, False))  8.67 us
    pallas_call x1, Pallas kernels, shards(): call(main_kernel, 17, outs, scratch, specs)  6.73 us
    ppermute x1, starting transfers between devices, shards(): row_low = lax.ppermute(low, 'gx', shifts(columns, True))  5.13 us
    ppermute x1, waiting for transfers between devices, shards(): row_high = lax.ppermute(high, 'gx', shifts(columns, False))  4.4 us
  transfers between devices with their start and end apart: 4, of which 3 were waited for; matrix products, arithmetic and copies ran while one was open for 0% of the time, Pallas kernels for 0%

profile of v1, /device:TPU:1, one launch (start us, length us, event | category | flops | bytes accessed | tf_op | source)
XLA Modules:
  0.0 87.8 jit_solution(9485699771411002447)
XLA Ops:
  0.6 0.0 copy-start
  0.6 1.0 %copy-done = f32[3,8,16,256]{3,2,1,0:T(8,128)S(1)} copy-done((f32[3,8,16,256]{3,2,1,0:T(8,128)S(1)}, f32[3,8,16,256]{3,2,1,0:T(8,128)}, u32[]{:S(2)}) %copy-start) | copy-done | bytes 393240
  1.6 1.0 %copy-done.2 = f32[3,8,16,256]{3,2,1,0:T(8,128)S(1)} copy-done((f32[3,8,16,256]{3,2,1,0:T(8,128)S(1)}, f32[3,8,16,256]{3,2,1,0:T(8,128)}, u32[]{:S(2)}) %copy-start.2) | copy-done | bytes 393240
  2.6 0.9 %copy-done.4 = f32[3,8,8,128]{3,2,1,0:T(8,128)S(1)} copy-done((f32[3,8,8,128]{3,2,1,0:T(8,128)S(1)}, f32[3,8,8,128]{3,2,1,0:T(8,128)}, u32[]{:S(2)}) %copy-start.4) | copy-done | bytes 98328
  3.5 0.9 %copy-done.6 = f32[3,8,8,128]{3,2,1,0:T(8,128)S(1)} copy-done((f32[3,8,8,128]{3,2,1,0:T(8,128)S(1)}, f32[3,8,8,128]{3,2,1,0:T(8,128)}, u32[]{:S(2)}) %copy-start.6) | copy-done | bytes 98328
  4.4 0.9 %copy-done.8 = f32[8,16,256]{2,1,0:T(8,128)S(1)} copy-done((f32[8,16,256]{2,1,0:T(8,128)S(1)}, f32[8,16,256]{2,1,0:T(8,128)}, u32[]{:S(2)}) %copy-start.8) | copy-done | bytes 131096
  5.3 0.9 %copy-done.10 = f32[8,16,256]{2,1,0:T(8,128)S(1)} copy-done((f32[8,16,256]{2,1,0:T(8,128)S(1)}, f32[8,16,256]{2,1,0:T(8,128)}, u32[]{:S(2)}) %copy-start.10) | copy-done | bytes 131096
  6.2 0.9 %copy-done.12 = f32[8,16,256]{2,1,0:T(8,128)S(1)} copy-done((f32[8,16,256]{2,1,0:T(8,128)S(1)}, f32[8,16,256]{2,1,0:T(8,128)}, u32[]{:S(2)}) %copy-start.12) | copy-done | bytes 131096
  7.1 0.8 copy-done.15
  7.9 0.8 copy-done.17
  8.6 0.8 copy-done.19
  9.4 0.3 shard_map.139
  9.7 9.6 %collective-permute-start = (f32[40,128]{1,0:T(8,128)S(1)}, f32[40,128]{1,0:T(8,128)S(1)}, u32[]{:S(2)}, u32[]{:S(2)}) collective-permute-start(f32[40,128]{1,0:T(8,128)S(1)} %get-tuple-element.26), channel_id=1, source_target_pairs={{0,1},{1,2},{2,3},{3,4},{4,5},{5,6},{6,7},{7,8},{8,9},{9,10},{10,1... | collective-permute-start | bytes 61448 | tf_op jit(solution)/shard_map/ppermute | solution.py:604
  19.3 0.0 copy-start.1
  19.3 0.0 copy-start.3
  19.4 0.0 copy-start.5
  19.4 0.0 copy-start.7
  19.4 0.0 copy-start.9
  19.4 0.0 copy-start.11
  19.4 0.0 copy-start.13
  19.4 1.4 %collective-permute-start.1 = (f32[40,128]{1,0:T(8,128)S(1)}, f32[40,128]{1,0:T(8,128)S(1)}, u32[]{:S(2)}, u32[]{:S(2)}) collective-permute-start(f32[40,128]{1,0:T(8,128)S(1)} %get-tuple-element.27), channel_id=1, source_target_pairs={{1,0},{2,1},{3,2},{4,3},{5,4},{6,5},{7,6},{8,7},{9,8},{10,9},{11,1... | collective-permute-start | bytes 61448 | tf_op jit(solution)/shard_map/ppermute | solution.py:605
  20.8 0.0 collective-permute-done.refs_10_.refs_11_
  20.9 8.7 %collective-permute-done.1.refs_11_.refs_12_ = f32[40,128]{1,0:T(8,128)S(1)} collective-permute-done((f32[40,128]{1,0:T(8,128)S(1)}, f32[40,128]{1,0:T(8,128)S(1)}, u32[]{:S(2)}, u32[]{:S(2)}) %collective-permute-start.1) | collective-permute-done | bytes 20512 | tf_op jit(solution)/shard_map/ppermute | solution.py:605
  29.5 0.1 shard_map.140
  29.6 5.1 %collective-permute-start.2 = (f32[496,128]{1,0:T(8,128)S(1)}, f32[496,128]{1,0:T(8,128)S(1)}, u32[]{:S(2)}, u32[]{:S(2)}) collective-permute-start(f32[496,128]{1,0:T(8,128)S(1)} %get-tuple-element.28), channel_id=1, source_target_pairs={{0,16},{16,32},{32,48},{48,64},{64,80},{80,96},{96,112},{112,128},... | collective-permute-start | bytes 761864 | tf_op jit(solution)/shard_map/ppermute | solution.py:607
  34.8 1.9 %collective-permute-start.3 = (f32[496,128]{1,0:T(8,128)S(1)}, f32[496,128]{1,0:T(8,128)S(1)}, u32[]{:S(2)}, u32[]{:S(2)}) collective-permute-start(f32[496,128]{1,0:T(8,128)S(1)} %get-tuple-element.29), channel_id=1, source_target_pairs={{16,0},{32,16},{48,32},{64,48},{80,64},{96,80},{112,96},{128,112},... | collective-permute-start | bytes 761864 | tf_op jit(solution)/shard_map/ppermute | solution.py:608
  36.7 0.1 pad_add_fusion.refs_10_
  36.8 1.2 %collective-permute-done.2.refs_13_ = f32[496,128]{1,0:T(8,128)S(1)} collective-permute-done((f32[496,128]{1,0:T(8,128)S(1)}, f32[496,128]{1,0:T(8,128)S(1)}, u32[]{:S(2)}, u32[]{:S(2)}) %collective-permute-start.2) | collective-permute-done | bytes 253984 | tf_op jit(solution)/shard_map/ppermute | solution.py:607
  38.0 4.4 %collective-permute-done.3.refs_14_ = f32[496,128]{1,0:T(8,128)S(1)} collective-permute-done((f32[496,128]{1,0:T(8,128)S(1)}, f32[496,128]{1,0:T(8,128)S(1)}, u32[]{:S(2)}, u32[]{:S(2)}) %collective-permute-start.3) | collective-permute-done | bytes 253984 | tf_op jit(solution)/shard_map/ppermute | solution.py:608
  42.4 0.0 copy-done.14
  42.4 0.0 copy-done.21
  42.4 0.0 copy-done.1
  42.4 0.0 copy-done.3
  42.4 0.0 copy-done.5
  42.4 0.0 copy-done.7
  42.4 0.0 copy-done.9
  42.4 0.0 copy-done.11
  42.4 0.0 copy-done.13
  42.4 0.0 copy-done.16
  42.5 0.0 copy-done.18
  42.5 6.7 %shard_map.141 = (f32[3,7,16,256]{3,2,1,0:T(8,128)S(1)}, f32[3,7,8,128]{3,2,1,0:T(8,128)S(1)}, f32[2,3,2,16,128]{4,3,2,1,0:T(8,128)S(1)}, f32[2,3,8,128]{3,2,1,0...) custom-call(f32[3,8,16,256]{3,2,1,0:T(8,128)S(1)} %copy-done.1, f32[3,8,16,256]{3,2,1,0:T(8,128)S(1)} %copy-done.3, ...), custom_call_target="tpu_custom_call" | custom-call | tf_op jit(solution)/shard_map/pallas_call | solution.py:642
  49.2 14.7 %all_to_all.22 = f32[32,1,128]{2,1,0:T(1,128)S(1)} all-to-all(f32[32,1,128]{2,1,0:T(1,128)S(1)} %bitcast.17), channel_id=1, replica_groups={{0,4,8,12,16,20,24,28,32,36,40,44,48,52,56,60,64,68,72,76,80,84,88,92,9..., dimensions={0} | all-to-all | bytes 32768 | tf_op jit(solution)/shard_map/all_to_all | solution.py:652
  64.0 1.3 %shard_map.142 = f32[16,128]{1,0:T(8,128)S(1)} custom-call(f32[32,128]{1,0:T(8,128)S(1)} %bitcast.14), custom_call_target="tpu_custom_call" | custom-call | tf_op jit(solution)/shard_map/pallas_call | solution.py:653
  65.2 19.9 %all_to_all.23 = f32[16,1,128]{2,1,0:T(1,128)S(1)} all-to-all(f32[16,1,128]{2,1,0:T(1,128)S(1)} %bitcast.16), channel_id=1, replica_groups={{0,1,2,3,128,129,130,131,256,257,258,259,384,385,386,387},{4,5,6,7,132,..., dimensions={0} | all-to-all | bytes 16384 | tf_op jit(solution)/shard_map/all_to_all | solution.py:654
  85.1 1.0 %shard_map.143 = (f32[3,8,16,256]{3,2,1,0:T(8,128)}, f32[3,8,8,128]{3,2,1,0:T(8,128)}, f32[8,128]{1,0:T(8,128)S(1)}) custom-call(f32[16,128]{1,0:T(8,128)S(1)} %bitcast.15, f32[3,8,16,256]{3,2,1,0:T(8,128)S(1)} %copy-done.1, f32[3,8,16,256]{3,2,1,0:T(8,128)S(1)} %copy-done.3, f32[3,8,8,128]{3,2,1,0:T(8,128)S(1)} %copy-done.5, ...), custom_call_target="tpu_custom_call" | custom-call | tf_op jit(solution)/shard_map/pallas_call | solution.py:655
  86.1 0.5 slice.21
  87.2 0.5 conditional.1
  87.3 0.5 slice.14
  (15 shorter events, 0.0 us)
Async XLA Ops:
  0.6 1.0 %copy-start = (f32[3,8,16,256]{3,2,1,0:T(8,128)S(1)}, f32[3,8,16,256]{3,2,1,0:T(8,128)}, u32[]{:S(2)}) copy-start(f32[3,8,16,256]{3,2,1,0:T(8,128)} %fn.1) | copy-start | bytes 1179652
  1.6 1.0 %copy-start.2 = (f32[3,8,16,256]{3,2,1,0:T(8,128)S(1)}, f32[3,8,16,256]{3,2,1,0:T(8,128)}, u32[]{:S(2)}) copy-start(f32[3,8,16,256]{3,2,1,0:T(8,128)} %fb.1) | copy-start | bytes 1179652
  2.6 0.9 %copy-start.4 = (f32[3,8,8,128]{3,2,1,0:T(8,128)S(1)}, f32[3,8,8,128]{3,2,1,0:T(8,128)}, u32[]{:S(2)}) copy-start(f32[3,8,8,128]{3,2,1,0:T(8,128)} %cn.1) | copy-start | bytes 294916
  3.5 0.9 %copy-start.6 = (f32[3,8,8,128]{3,2,1,0:T(8,128)S(1)}, f32[3,8,8,128]{3,2,1,0:T(8,128)}, u32[]{:S(2)}) copy-start(f32[3,8,8,128]{3,2,1,0:T(8,128)} %cb.1) | copy-start | bytes 294916
  4.4 0.9 %copy-start.8 = (f32[8,16,256]{2,1,0:T(8,128)S(1)}, f32[8,16,256]{2,1,0:T(8,128)}, u32[]{:S(2)}) copy-start(f32[8,16,256]{2,1,0:T(8,128)} %refs_2_.5) | copy-start | bytes 393220
  5.3 0.9 %copy-start.10 = (f32[8,16,256]{2,1,0:T(8,128)S(1)}, f32[8,16,256]{2,1,0:T(8,128)}, u32[]{:S(2)}) copy-start(f32[8,16,256]{2,1,0:T(8,128)} %refs_3_.5) | copy-start | bytes 393220
  6.2 0.9 %copy-start.12 = (f32[8,16,256]{2,1,0:T(8,128)S(1)}, f32[8,16,256]{2,1,0:T(8,128)}, u32[]{:S(2)}) copy-start(f32[8,16,256]{2,1,0:T(8,128)} %refs_4_.5) | copy-start | bytes 393220
  7.1 0.8 copy-start.15
  7.9 0.8 copy-start.17
  8.6 0.8 copy-start.19
  9.4 33.0 %copy-start.14 = (bf16[384,512]{1,0:T(8,128)(2,1)S(1)}, bf16[384,512]{1,0:T(8,128)(2,1)}, u32[]{:S(2)}) copy-start(bf16[384,512]{1,0:T(8,128)(2,1)} %constant.25.clone.refs_15_) | copy-start | bytes 1179652
  9.4 33.0 %copy-start.21 = (bf16[256,256]{1,0:T(8,128)(2,1)S(1)}, bf16[256,256]{1,0:T(8,128)(2,1)}, u32[]{:S(2)}) copy-start(bf16[256,256]{1,0:T(8,128)(2,1)} %constant.26.clone.refs_16_) | copy-start | bytes 393220
  9.7 11.2 %collective-permute-start = (f32[40,128]{1,0:T(8,128)S(1)}, f32[40,128]{1,0:T(8,128)S(1)}, u32[]{:S(2)}, u32[]{:S(2)}) collective-permute-start(f32[40,128]{1,0:T(8,128)S(1)} %get-tuple-element.26), channel_id=1, source_target_pairs={{0,1},{1,2},{2,3},{3,4},{4,5},{5,6},{6,7},{7,8},{8,9},{9,10},{10,1... | collective-permute-start | bytes 61448 | tf_op jit(solution)/shard_map/ppermute | solution.py:604
  19.3 23.1 %copy-start.1 = (f32[3,8,16,256]{3,2,1,0:T(8,128)S(1)}, f32[3,8,16,256]{3,2,1,0:T(8,128)}, u32[]{:S(2)}) copy-start(f32[3,8,16,256]{3,2,1,0:T(8,128)} %fn.1) | copy-start | bytes 1179652
  19.3 23.0 %copy-start.3 = (f32[3,8,16,256]{3,2,1,0:T(8,128)S(1)}, f32[3,8,16,256]{3,2,1,0:T(8,128)}, u32[]{:S(2)}) copy-start(f32[3,8,16,256]{3,2,1,0:T(8,128)} %fb.1) | copy-start | bytes 1179652
  19.4 23.0 %copy-start.5 = (f32[3,8,8,128]{3,2,1,0:T(8,128)S(1)}, f32[3,8,8,128]{3,2,1,0:T(8,128)}, u32[]{:S(2)}) copy-start(f32[3,8,8,128]{3,2,1,0:T(8,128)} %cn.1) | copy-start | bytes 294916
  19.4 23.0 %copy-start.7 = (f32[3,8,8,128]{3,2,1,0:T(8,128)S(1)}, f32[3,8,8,128]{3,2,1,0:T(8,128)}, u32[]{:S(2)}) copy-start(f32[3,8,8,128]{3,2,1,0:T(8,128)} %cb.1) | copy-start | bytes 294916
  19.4 23.0 %copy-start.9 = (f32[8,16,256]{2,1,0:T(8,128)S(1)}, f32[8,16,256]{2,1,0:T(8,128)}, u32[]{:S(2)}) copy-start(f32[8,16,256]{2,1,0:T(8,128)} %refs_2_.5) | copy-start | bytes 393220
  19.4 23.0 %copy-start.11 = (f32[8,16,256]{2,1,0:T(8,128)S(1)}, f32[8,16,256]{2,1,0:T(8,128)}, u32[]{:S(2)}) copy-start(f32[8,16,256]{2,1,0:T(8,128)} %refs_3_.5) | copy-start | bytes 393220
  19.4 23.0 %copy-start.13 = (f32[8,16,256]{2,1,0:T(8,128)S(1)}, f32[8,16,256]{2,1,0:T(8,128)}, u32[]{:S(2)}) copy-start(f32[8,16,256]{2,1,0:T(8,128)} %refs_4_.5) | copy-start | bytes 393220
  19.4 10.1 %collective-permute-start.1 = (f32[40,128]{1,0:T(8,128)S(1)}, f32[40,128]{1,0:T(8,128)S(1)}, u32[]{:S(2)}, u32[]{:S(2)}) collective-permute-start(f32[40,128]{1,0:T(8,128)S(1)} %get-tuple-element.27), channel_id=1, source_target_pairs={{1,0},{2,1},{3,2},{4,3},{5,4},{6,5},{7,6},{8,7},{9,8},{10,9},{11,1... | collective-permute-start | bytes 61448 | tf_op jit(solution)/shard_map/ppermute | solution.py:605
  29.5 12.9 %copy-start.16 = (f32[8,8,128]{2,1,0:T(8,128)S(1)}, f32[8,8,128]{2,1,0:T(8,128)}, u32[]{:S(2)}) copy-start(f32[8,8,128]{2,1,0:T(8,128)} %refs_7_.5) | copy-start | bytes 98308
  29.5 12.9 %copy-start.18 = (f32[8,8,128]{2,1,0:T(8,128)S(1)}, f32[8,8,128]{2,1,0:T(8,128)}, u32[]{:S(2)}) copy-start(f32[8,8,128]{2,1,0:T(8,128)} %refs_8_.5) | copy-start | bytes 98308
  29.5 12.9 %copy-start.20 = (f32[8,8,128]{2,1,0:T(8,128)S(1)}, f32[8,8,128]{2,1,0:T(8,128)}, u32[]{:S(2)}) copy-start(f32[8,8,128]{2,1,0:T(8,128)} %refs_9_.5) | copy-start | bytes 98308
  29.6 8.3 %collective-permute-start.2 = (f32[496,128]{1,0:T(8,128)S(1)}, f32[496,128]{1,0:T(8,128)S(1)}, u32[]{:S(2)}, u32[]{:S(2)}) collective-permute-start(f32[496,128]{1,0:T(8,128)S(1)} %get-tuple-element.28), channel_id=1, source_target_pairs={{0,16},{16,32},{32,48},{48,64},{64,80},{80,96},{96,112},{112,128},... | collective-permute-start | bytes 761864 | tf_op jit(solution)/shard_map/ppermute | solution.py:607
  34.8 7.6 %collective-permute-start.3 = (f32[496,128]{1,0:T(8,128)S(1)}, f32[496,128]{1,0:T(8,128)S(1)}, u32[]{:S(2)}, u32[]{:S(2)}) collective-permute-start(f32[496,128]{1,0:T(8,128)S(1)} %get-tuple-element.29), channel_id=1, source_target_pairs={{16,0},{32,16},{48,32},{64,48},{80,64},{96,80},{112,96},{128,112},... | collective-permute-start | bytes 761864 | tf_op jit(solution)/shard_map/ppermute | solution.py:608

commit v2 on v1

--- a/solution.py
+++ b/solution.py
@@ -44,15 +44,28 @@
             entries.append((key, low, high, tile, lane[tile], row, own))
             lane[tile] += low
             row += own * low
-    corners = []
+    corners, corner_row = {}, 0
     for tile in "ABC":
         for side in range(2):
-            corners.append((tile, side, row))
-            row += TILE_RIM[tile]
-    return entries, corners, -(-row // 8) * 8
-
-
-ENTRIES, CORNERS, RIM_ROWS = plan()
+            corners[tile, side] = corner_row
+            corner_row += TILE_RIM[tile]
+    return entries, corners, -(-row // 8) * 8, -(-corner_row // 8) * 8
+
+
+ENTRIES, CORNERS, RIM_ROWS, CORNER_ROWS = plan()
+
+PACK_SOURCES = (
+    ("fn", ()),
+    ("fb", (slice(None), slice(6, 7))),
+    ("fd", (slice(6, 7),)),
+    ("fs", (slice(6, 8),)),
+    ("fl", (slice(6, 8),)),
+    ("cn", ()),
+    ("cb", (slice(None), slice(0, 2))),
+    ("cd", (slice(1, 2),)),
+    ("cs", (slice(0, 2),)),
+    ("cl", (slice(0, 2),)),
+)
 
 SLOTS = 31
 PEAK_LANE = 31
@@ -76,9 +89,30 @@
     return refs[name][index + (slice(None), slice(tile * LANES, (tile + 1) * LANES))]
 
 
-def pack_columns(*refs):
-    named = dict(zip(NAMES, refs[:10]))
-    low_out, high_out = refs[10:]
+def is_even(axis):
+    return lax.axis_index(axis) % 2 == 0
+
+
+def pair(axis, low, high):
+    even = is_even(axis)
+    return jnp.where(even, low, high), jnp.where(even, high, low)
+
+
+def pack(*refs):
+    sources = dict(zip(NAMES, refs[:10]))
+    column_outs, row_outs = refs[10:12], refs[12:14]
+    named = dict(zip(NAMES, refs[14:24]))
+    sems = refs[24]
+    copies = []
+    for i, (name, part) in enumerate(PACK_SOURCES):
+        source, target = sources[name], named[name]
+        if part:
+            source, target = source.at[part], target.at[part]
+        copies.append(pltpu.make_async_copy(source, target, sems.at[i]))
+    for copy in copies:
+        copy.start()
+    for copy in copies:
+        copy.wait()
     for tile, (base, rows) in TILE_ROWS.items():
         lane = iota((rows, LANES), 1)
         low_sum = jnp.zeros((rows, LANES), jnp.float32)
@@ -89,31 +123,32 @@
             inside = (lane >= at) & (lane < at + low)
             low_sum = jnp.where(inside, turned(own_tile(named, key, own - 1), at + low, 1), low_sum)
             high_sum = jnp.where(inside, turned(own_tile(named, key, 0), at, 1), high_sum)
-        low_out[base : base + rows, :] = low_sum
-        high_out[base : base + rows, :] = high_sum
-
-
-def pack_rows(*refs):
-    named = dict(zip(NAMES, refs[:10]))
-    sides = refs[10:12]
-    low_out, high_out = refs[12:]
-    low_out[RIM_ROWS - 8 :, :] = jnp.zeros((8, LANES), jnp.float32)
-    high_out[RIM_ROWS - 8 :, :] = jnp.zeros((8, LANES), jnp.float32)
-    for (name, index), low, high, _, _, row, own in ENTRIES:
+        span = slice(base, base + rows)
+        column_outs[0][span, :], column_outs[1][span, :] = pair("gy", low_sum, high_sum)
+    row_outs[0][RIM_ROWS - 8 :, :] = jnp.zeros((8, LANES), jnp.float32)
+    row_outs[1][RIM_ROWS - 8 :, :] = jnp.zeros((8, LANES), jnp.float32)
+    for (name, index), low, _, _, _, row, own in ENTRIES:
         ref = named[name]
         rows = ref.shape[-2]
         for tile in range(own):
             lanes = slice(tile * LANES, (tile + 1) * LANES)
-            start = row + tile * low
-            low_out[start : start + low, :] = ref[index + (slice(rows - low, rows), lanes)]
-            high_out[start : start + high, :] = ref[index + (slice(0, high), lanes)]
-            if high < low:
-                high_out[start + high : start + low, :] = jnp.zeros((low - high, LANES), jnp.float32)
-    for tile, side, row in CORNERS:
-        base, rows = TILE_ROWS[tile]
+            span = slice(row + tile * low, row + tile * low + low)
+            row_outs[0][span, :], row_outs[1][span, :] = pair(
+                "gx", ref[index + (slice(rows - low, rows), lanes)], ref[index + (slice(0, low), lanes)]
+            )
+
+
+def pack_corners(first, second, first_out, second_out):
+    first_out[CORNER_ROWS - 8 :, :] = jnp.zeros((8, LANES), jnp.float32)
+    second_out[CORNER_ROWS - 8 :, :] = jnp.zeros((8, LANES), jnp.float32)
+    for tile, (base, rows) in TILE_ROWS.items():
         rim = TILE_RIM[tile]
-        low_out[row : row + rim, :] = sides[side][base + rows - rim : base + rows, :]
-        high_out[row : row + rim, :] = sides[side][base : base + rim, :]
+        end, begin = slice(base + rows - rim, base + rows), slice(base, base + rim)
+        ends = pair("gy", second[end, :], first[end, :])
+        begins = pair("gy", second[begin, :], first[begin, :])
+        for side in range(2):
+            row = CORNERS[tile, side]
+            first_out[row : row + rim, :], second_out[row : row + rim, :] = pair("gx", ends[side], begins[side])
 
 
 def across(tiles, steps, wanted):
@@ -304,23 +339,27 @@
 
 def main_kernel(*refs):
     named = dict(zip(NAMES, refs[:10]))
-    place, side_low, side_high, row_low, row_high, split_pick, weave_pick = refs[10:17]
-    fine_rate, coarse_rate, plane_out, iterate_out, lines_out, message_out = refs[17:23]
-    fine, fine_x, fine_y, rest, coarse, coarse_x, coarse_y, coarse_rest = refs[23:31]
-    mixed, planes, parted, woven, ends = refs[31:36]
-    packed = dict(zip("ABC", zip(refs[36:39], refs[39:42])))
-
-    for tile in "ABC":
-        base, rows = TILE_ROWS[tile]
+    sides, rims, corners = refs[10:12], refs[12:14], refs[14:16]
+    split_pick, weave_pick = refs[16:18]
+    fine_rate, coarse_rate, plane_out, iterate_out, lines_out, message_out = refs[18:24]
+    fine, fine_x, fine_y, rest, coarse, coarse_x, coarse_y, coarse_rest = refs[24:32]
+    mixed, planes, parted, woven, ends = refs[32:37]
+    packed = dict(zip("ABC", zip(refs[37:40], refs[40:43])))
+
+    def received(axis, pieces, span):
+        return pair(axis, pieces[1][span, :], pieces[0][span, :])
+
+    for tile, (base, rows) in TILE_ROWS.items():
         rim = TILE_RIM[tile]
-        for side, source in enumerate((side_low, side_high)):
+        own = received("gy", sides, slice(base, base + rows))
+        for side in range(2):
             target = packed[tile][side]
             target[...] = jnp.zeros(target.shape, jnp.float32)
-            target[rows : 2 * rows, :] = source[base : base + rows, :]
-            row = [r for t, s, r in CORNERS if t == tile and s == side][0]
-            target[rows - rim : rows, :] = row_low[row : row + rim, :]
-            high = min(rim, 8)
-            target[2 * rows : 2 * rows + high, :] = row_high[row : row + high, :]
+            target[rows : 2 * rows, :] = own[side]
+            row = CORNERS[tile, side]
+            low, high = received("gx", corners, slice(row, row + rim))
+            target[rows - rim : rows, :] = low
+            target[2 * rows : 2 * rows + rim, :] = high
 
     slot = {key: i for i, key in enumerate(DEEP_REST)}
     coarse_slot = {key: i for i, key in enumerate(COARSE_REST)}
@@ -342,9 +381,9 @@
                 target[t, 2 * rows : total, :] = jnp.zeros((total - 2 * rows, LANES), jnp.float32)
         for t in range(own):
             target[t, rows : 2 * rows, :] = own_tile(named, key, t)
-            begin = row + t * low
-            target[t, rows - low : rows, :] = row_low[begin : begin + low, :]
-            target[t, 2 * rows : 2 * rows + high, :] = row_high[begin : begin + high, :]
+            below, beyond = received("gx", rims, slice(row + t * low, row + t * low + low))
+            target[t, rows - low : rows, :] = below
+            target[t, 2 * rows : 2 * rows + low, :] = beyond
         low_side, high_side = packed[tile][0][...], packed[tile][1][...]
         lane = iota(low_side.shape, 1)
         target[own, :, :] = jnp.where(
@@ -443,9 +482,10 @@
         coarse_rate[c, 0] = below_rate[c][0][4:12, :]
 
     shear, lame = coarse_pair("cs", 0), coarse_pair("cl", 0)
-    row = iota((16, LANES), 0) + (place[0] * 8 - 4)
-    lane = iota((16, LANES), 1)
-    column = [lane, jnp.where(lane < 64, lane + LANES, lane - LANES)]
+    row = iota((16, LANES), 0) + (lax.axis_index("gx") * 8 - 4)
+    lane = iota((16, LANES), 1) + lax.axis_index("gy") * LANES
+    column = [lane, jnp.where(iota((16, LANES), 1) < 64, lane + LANES, lane - LANES)]
+    extent = (lax.axis_size("gx") * 8, lax.axis_size("gy") * LANES)
     fine_moduli = (four(6), four(6), four(7))
     coarse_moduli = (shear, shear, [l + 2.0 * s for l, s in zip(lame, shear)])
     for c in range(3):
@@ -455,8 +495,8 @@
         inverse = []
         for t in range(2):
             diagonal = half[t] + 0.5625 * spread[t]
-            x, y = row, column[t] + place[1] * LANES
-            inside = (x >= 0) & (x < place[2]) & (y >= 0) & (y < place[3]) & (diagonal > 0.0)
+            x, y = row, column[t]
+            inside = (x >= 0) & (x < extent[0]) & (y >= 0) & (y < extent[1]) & (diagonal > 0.0)
             inverse.append(jnp.where(inside, 1.0 / jnp.where(inside, diagonal, 1.0), 0.0))
         for part in range(2):
             if part == 0:
@@ -526,16 +566,18 @@
     message_out[...] = jnp.broadcast_to(sealed(message, peak, jnp.maximum(flag, full)), message_out.shape)
 
 
-def final_kernel(received, fn, fb, cn, cb, fine_rate, coarse_rate, plane, iterate, fine_out, coarse_out, scalars):
+def final_kernel(
+    received, fn, fb, cn, cb, fine_rate, coarse_rate, plane, iterate, fine_out, coarse_out, ratio_out, square_out, flag_out
+):
     first, last, peak, flag = opened(received)
     step = 0.3 / jnp.full((8, LANES), peak, jnp.float32)
     square = step * step
     first_max = largest([a + square * b for a, b in first])
     last_max = largest([a + square * b for a, b in last])
-    reduction = last_max / (jnp.full((8, LANES), first_max, jnp.float32) + 1e-06)
-    flag = jnp.where(square < STEP_LOW, 1.0, flag)
-    row = iota((8, LANES), 0)
-    scalars[...] = jnp.where(row == 0, reduction, jnp.where(row == 1, square, flag))
+    ratio = last_max / (jnp.full((8, LANES), first_max, jnp.float32) + 1e-06)
+    ratio_out[0] = jnp.max(ratio)
+    square_out[0] = jnp.max(square)
+    flag_out[0] = jnp.where((flag > 0.0) | (jnp.max(square) < STEP_LOW), 1, 0)
     square = square[0:1, 0:1]
     for c in range(3):
         fine_out[c, 0:7] = 2.0 * fn[c, 0:7] - fb[c, 0:7] + square * fine_rate[c]
@@ -545,8 +587,10 @@
             fine_out[c, 7, :, t * LANES : (t + 1) * LANES] = plane[0, c, t] + square * plane[1, c, t]
 
 
-def shifts(count, up):
-    return [(i, i + 1) if up else (i + 1, i) for i in range(count - 1)]
+def exchange(first, second, axis, count):
+    near = [(i, i ^ 1) for i in range(count) if i ^ 1 < count]
+    far = [(i, i + 1) for i in range(1, count - 1, 2)] + [(i + 1, i) for i in range(1, count - 1, 2)]
+    return lax.ppermute(first, axis, near), lax.ppermute(second, axis, far)
 
 
 def gather_groups(columns, rows):
@@ -582,38 +626,43 @@
     return pltpu.VMEM(shape, jnp.float32)
 
 
-PARAMS = pltpu.CompilerParams(vmem_limit_bytes=48 * 1024 * 1024)
-
-
 def make_shards(columns, rows):
     near, ring = gather_groups(columns, rows)
     axes = ("gx", "gy")
 
     def shards(*args):
-        fn, fb, fd, fs, fl, cn, cb, cd, cs, cl = args
         in_vmem = pl.BlockSpec(memory_space=pltpu.VMEM)
-        call = lambda kernel, n_in, outs, scratch=(), specs=None: pl.pallas_call(
-            kernel,
-            out_shape=outs,
-            in_specs=specs or [in_vmem] * n_in,
-            out_specs=[in_vmem] * len(outs) if isinstance(outs, tuple) else in_vmem,
-            scratch_shapes=list(scratch),
-            compiler_params=PARAMS,
-        )
-        low, high = call(pack_columns, 10, (f32(PACKED_ROWS, LANES),) * 2)(*args)
-        side_low = lax.ppermute(low, "gy", shifts(rows, True))
-        side_high = lax.ppermute(high, "gy", shifts(rows, False))
-        low, high = call(pack_rows, 12, (f32(RIM_ROWS, LANES),) * 2)(*args, side_low, side_high)
-        row_low = lax.ppermute(low, "gx", shifts(columns, True))
-        row_high = lax.ppermute(high, "gx", shifts(columns, False))
-        place = jnp.stack(
-            [
-                lax.axis_index("gx"),
-                lax.axis_index("gy"),
-                jnp.int32(columns * 8),
-                jnp.int32(rows * LANES),
-            ]
-        ).astype(jnp.int32)
+        in_smem = pl.BlockSpec(memory_space=pltpu.SMEM)
+        in_hbm = pl.BlockSpec(memory_space=pltpu.HBM)
+
+        def call(kernel, ins, outs, scratch=(), out_specs=None, cost=None, limit=48):
+            return pl.pallas_call(
+                kernel,
+                out_shape=outs,
+                in_specs=ins,
+                out_specs=out_specs or ([in_vmem] * len(outs) if isinstance(outs, tuple) else in_vmem),
+                scratch_shapes=list(scratch),
+                compiler_params=pltpu.CompilerParams(vmem_limit_bytes=limit * 1024 * 1024),
+                cost_estimate=cost,
+            )
+
+        fn, fb, _, _, _, cn, cb, _, _, _ = args
+        first_side, second_side, first_rim, second_rim = call(
+            pack,
+            [in_hbm] * 10,
+            (f32(PACKED_ROWS, LANES),) * 2 + (f32(RIM_ROWS, LANES),) * 2,
+            [vm(*a.shape) for a in args] + [pltpu.SemaphoreType.DMA((len(PACK_SOURCES),))],
+            limit=63,
+        )(*args)
+        sides = exchange(first_side, second_side, "gy", rows)
+        rims = exchange(first_rim, second_rim, "gx", columns)
+        first, second = call(
+            pack_corners,
+            [in_vmem] * 2,
+            (f32(CORNER_ROWS, LANES),) * 2,
+            cost=pl.CostEstimate(flops=10**12, bytes_accessed=10**9, transcendentals=0),
+        )(*sides)
+        corners = exchange(first, second, "gx", columns)
         near_size, ring_size = len(near[0]), len(ring[0])
         outs = (
             f32(3, 7, 16, 256),
@@ -638,31 +687,30 @@
             vm(192, 256),
             vm(6, 3, 16, LANES),
         ) + (vm(48, LANES), vm(48, LANES), vm(24, LANES)) * 2
-        specs = [in_vmem] * 10 + [pl.BlockSpec(memory_space=pltpu.SMEM)] + [in_vmem] * 6
-        fine_rate, coarse_rate, plane, iterate, lines, message = call(main_kernel, 17, outs, scratch, specs)(
+        fine_rate, coarse_rate, plane, iterate, lines, message = call(main_kernel, [in_vmem] * 18, outs, scratch)(
             *args,
-            place,
-            side_low,
-            side_high,
-            row_low,
-            row_high,
+            *sides,
+            *rims,
+            *corners,
             jnp.asarray(split_matrix()),
             jnp.asarray(weave_matrix()),
         )
         received = lax.all_to_all(message, axes, 0, 0, tiled=True, axis_index_groups=near)
-        message = call(merge_kernel, 1, f32(ring_size, LANES))(received)
+        message = call(merge_kernel, [in_vmem], f32(ring_size, LANES))(received)
         received = lax.all_to_all(message, axes, 0, 0, tiled=True, axis_index_groups=ring)
-        fine_next, coarse_next, scalars = call(final_kernel, 9, (f32(*fn.shape), f32(*cn.shape), f32(8, LANES)))(
-            received, fn, fb, cn, cb, fine_rate, coarse_rate, plane, iterate
-        )
+        fine_next, coarse_next, ratio, square, flag = call(
+            final_kernel,
+            [in_vmem] * 9,
+            (f32(*fn.shape), f32(*cn.shape), f32(1), f32(1), jax.ShapeDtypeStruct((1,), jnp.int32)),
+            out_specs=[in_vmem] * 2 + [in_smem] * 3,
+        )(received, fn, fb, cn, cb, fine_rate, coarse_rate, plane, iterate)
 
         def plain():
-            square = scalars[1, 0]
-            values = jnp.abs(lines[0::2] + square * lines[1::2])
+            values = jnp.abs(lines[0::2] + square[0] * lines[1::2])
             tops = lax.pmax(jnp.max(values, axis=(1, 2, 3)), axes)
             return tops[1] / (tops[0] + 1e-06)
 
-        reduction = lax.cond(scalars[2, 0] > 0.0, plain, lambda: scalars[0, 0])
+        reduction = lax.cond(flag[0] > 0, plain, lambda: ratio[0])
         return fine_next, coarse_next, reduction
 
     return shards

time: 88.5 us -> 78.3 us (0.88)
  waiting for transfers between devices: 14.3 us -> 2.04 us
  local copies, waits for them, and re-layouts: 9.84 us -> 0.08 us
  blocking collectives: 34.6 us -> 40.5 us
  starting transfers between devices: 18.1 us -> 21.9 us
  Pallas kernels: 9.33 us -> 11.9 us
    ppermute x4 -> x6, waiting for transfers between devices: 14.3 us -> 2.04 us  [exchange(): return (lax.ppermute(first, axis, near), lax.ppermute(second, axis, far))]
    unnamed x44 -> x24, local copies, waits for them, and re-layouts: 8.82 us -> 0.08 us
    all_to_all x1, blocking collectives: 14.7 us -> 23.5 us  [shards(): lax.all_to_all(message, axes, 0, 0, tiled=True, axis_index_groups=near)]
    ppermute x4 -> x6, starting transfers between devices: 18.1 us -> 21.9 us  [exchange(): return (lax.ppermute(first, axis, near), lax.ppermute(second, axis, far))]
    all_to_all x1, blocking collectives: 19.9 us -> 17.1 us  [shards(): lax.all_to_all(message, axes, 0, 0, tiled=True, axis_index_groups=ring)]
    pallas_call x5, Pallas kernels: 9.33 us -> 11.9 us  [the longest x1 7.34 us: shards(): call(main_kernel, [in_vmem] * 18, outs, scratch)]
    slice x2 -> x0, local copies, waits for them, and re-layouts: 1.03 us -> none  [shards(): reduction = lax.cond(scalars[2, 0] > 0.0, plain, lambda: scalars[0, 0])]
  transfers between devices with their start and end apart: 4 -> 6, of which waited for: 3 -> 1; matrix products, arithmetic and copies ran while one was open for 0% -> 0% of each run, Pallas kernels for 0% -> 0%
where the time goes in v2:
time: 78.3 us; the launch traced here: 78 us
  blocking collectives  40.5 us (52%)
  starting transfers between devices  21.9 us (28%)
  Pallas kernels  11.9 us (15%)
  waiting for transfers between devices  2.04 us (3%)
  between operations  1.49 us (2%)
    all_to_all x1, blocking collectives, shards(): lax.all_to_all(message, axes, 0, 0, tiled=True, axis_index_groups=near)  23.5 us
    ppermute x6, starting transfers between devices, exchange(): return (lax.ppermute(first, axis, near), lax.ppermute(second, axis, far))  21.9 us
    all_to_all x1, blocking collectives, shards(): lax.all_to_all(message, axes, 0, 0, tiled=True, axis_index_groups=ring)  17.1 us
    pallas_call x1, Pallas kernels, shards(): call(main_kernel, [in_vmem] * 18, outs, scratch)  7.34 us
    pallas_call x1, Pallas kernels, shards(): call(pack, [in_hbm] * 10, (f32(PACKED_ROWS, LANES),) * 2 + (f32(RIM_ROWS,...  2.26 us
    ppermute x6, waiting for transfers between devices, exchange(): return (lax.ppermute(first, axis, near), lax.ppermute(second, axis, far))  2.04 us
  transfers between devices with their start and end apart: 6, of which 1 were waited for; matrix products, arithmetic and copies ran while one was open for 0% of the time, Pallas kernels for 0%

profile of v2, /device:TPU:1, one launch (start us, length us, event | category | flops | bytes accessed | tf_op | source)
XLA Modules:
  0.0 78.0 jit_solution(12985799992587070065)
XLA Ops:
  0.6 2.3 %shard_map.139 = (f32[40,128]{1,0:T(8,128)}, f32[40,128]{1,0:T(8,128)}, f32[456,128]{1,0:T(8,128)}, f32[456,128]{1,0:T(8,128)}) custom-call(f32[3,8,16,256]{3,2,1,0:T(8,128)} %fn.1, f32[3,8,16,256]{3,2,1,0:T(8,128)} %fb.1, f32[8,16,256]{2,1,0:T(8,128)} %refs_2_.3, f32[8,16,256]{2,1,0:T(8,128)} %refs_3_.3, f32[8,16,256]{2,1,0:T(8,128)} %refs_4_.3, ...), custom_call_target="tpu_custom_call" | custom-call | tf_op jit(solution)/shard_map/pallas_call | solution.py:650
  2.9 9.6 %collective-permute-start = (f32[40,128]{1,0:T(8,128)}, f32[40,128]{1,0:T(8,128)S(1)}, u32[]{:S(2)}, u32[]{:S(2)}) collective-permute-start(f32[40,128]{1,0:T(8,128)} %get-tuple-element.30), channel_id=1, source_target_pairs={{0,1},{1,0},{2,3},{3,2},{4,5},{5,4},{6,7},{7,6},{8,9},{9,8},{10,11... | collective-permute-start | bytes 61448 | tf_op jit(solution)/shard_map/ppermute | solution.py:593
  12.6 0.7 collective-permute-start.1
  13.2 2.9 %collective-permute-start.2 = (f32[456,128]{1,0:T(8,128)}, f32[456,128]{1,0:T(8,128)}, u32[]{:S(2)}, u32[]{:S(2)}) collective-permute-start(f32[456,128]{1,0:T(8,128)} %get-tuple-element.32), channel_id=1, source_target_pairs={{0,16},{16,0},{32,48},{48,32},{64,80},{80,64},{96,112},{112,96},{1... | collective-permute-start | bytes 700424 | tf_op jit(solution)/shard_map/ppermute | solution.py:593
  16.1 3.1 %collective-permute-start.3 = (f32[456,128]{1,0:T(8,128)}, f32[456,128]{1,0:T(8,128)}, u32[]{:S(2)}, u32[]{:S(2)}) collective-permute-start(f32[456,128]{1,0:T(8,128)} %get-tuple-element.33), channel_id=1, source_target_pairs={{16,32},{48,64},{80,96},{112,128},{144,160},{176,192},{208,224},{2... | collective-permute-start | bytes 700424 | tf_op jit(solution)/shard_map/ppermute | solution.py:593
  19.2 0.0 collective-permute-done.first.refs_10_
  19.2 0.0 collective-permute-done.1.second.refs_11_
  19.2 0.0 copy-start
  19.2 0.0 copy-start.1
  19.3 0.0 copy-start.2
  19.3 0.0 copy-start.3
  19.3 0.0 copy-start.4
  19.3 0.0 copy-start.5
  19.3 0.0 copy-start.6
  19.3 0.0 copy-start.7
  19.3 0.0 copy-start.8
  19.3 0.0 copy-start.9
  19.4 0.0 copy-start.10
  19.4 0.0 copy-start.11
  19.4 2.5 %collective-permute-start.4 = (f32[48,128]{1,0:T(8,128)S(1)}, f32[48,128]{1,0:T(8,128)S(1)}, u32[]{:S(2)}, u32[]{:S(2)}) collective-permute-start(f32[48,128]{1,0:T(8,128)S(1)} %get-tuple-element.34), channel_id=1, source_target_pairs={{0,16},{16,0},{32,48},{48,32},{64,80},{80,64},{96,112},{112,96},{1... | collective-permute-start | bytes 73736 | tf_op jit(solution)/shard_map/ppermute | solution.py:593
  22.0 3.1 %collective-permute-start.5 = (f32[48,128]{1,0:T(8,128)S(1)}, f32[48,128]{1,0:T(8,128)S(1)}, u32[]{:S(2)}, u32[]{:S(2)}) collective-permute-start(f32[48,128]{1,0:T(8,128)S(1)} %get-tuple-element.35), channel_id=1, source_target_pairs={{16,32},{48,64},{80,96},{112,128},{144,160},{176,192},{208,224},{2... | collective-permute-start | bytes 73736 | tf_op jit(solution)/shard_map/ppermute | solution.py:593
  25.1 0.0 collective-permute-done.4.refs_14_
  25.1 2.0 %collective-permute-done.5.refs_15_ = f32[48,128]{1,0:T(8,128)S(1)} collective-permute-done((f32[48,128]{1,0:T(8,128)S(1)}, f32[48,128]{1,0:T(8,128)S(1)}, u32[]{:S(2)}, u32[]{:S(2)}) %collective-permute-start.5) | collective-permute-done | bytes 24608 | tf_op jit(solution)/shard_map/ppermute | solution.py:593
  27.1 0.0 collective-permute-done.2.refs_12_
  27.1 0.0 collective-permute-done.3.refs_13_
  27.1 0.0 copy-done
  27.1 0.0 copy-done.1
  27.1 0.0 copy-done.2
  27.1 0.0 copy-done.3
  27.1 0.0 copy-done.4
  27.2 0.0 copy-done.5
  27.2 0.0 copy-done.6
  27.2 0.0 copy-done.7
  27.2 0.0 copy-done.8
  27.2 0.0 copy-done.9
  27.2 0.0 copy-done.10
  27.2 0.0 copy-done.11
  27.2 7.3 %shard_map.141 = (f32[3,7,16,256]{3,2,1,0:T(8,128)S(1)}, f32[3,7,8,128]{3,2,1,0:T(8,128)S(1)}, f32[2,3,2,16,128]{4,3,2,1,0:T(8,128)S(1)}, f32[2,3,8,128]{3,2,1,0...) custom-call(f32[3,8,16,256]{3,2,1,0:T(8,128)S(1)} %copy-done, f32[3,8,16,256]{3,2,1,0:T(8,128)S(1)} %copy-done.1, ...), custom_call_target="tpu_custom_call" | custom-call | tf_op jit(solution)/shard_map/pallas_call | solution.py:690
  34.6 23.5 %all_to_all.22 = f32[32,1,128]{2,1,0:T(1,128)S(1)} all-to-all(f32[32,1,128]{2,1,0:T(1,128)S(1)} %bitcast.15), channel_id=1, replica_groups={{0,4,8,12,16,20,24,28,32,36,40,44,48,52,56,60,64,68,72,76,80,84,88,92,9..., dimensions={0} | all-to-all | bytes 32768 | tf_op jit(solution)/shard_map/all_to_all | solution.py:698
  58.0 1.3 %shard_map.142 = f32[16,128]{1,0:T(8,128)S(1)} custom-call(f32[32,128]{1,0:T(8,128)S(1)} %bitcast.12), custom_call_target="tpu_custom_call" | custom-call | tf_op jit(solution)/shard_map/pallas_call | solution.py:699
  59.3 17.1 %all_to_all.23 = f32[16,1,128]{2,1,0:T(1,128)S(1)} all-to-all(f32[16,1,128]{2,1,0:T(1,128)S(1)} %bitcast.14), channel_id=1, replica_groups={{0,1,2,3,128,129,130,131,256,257,258,259,384,385,386,387},{4,5,6,7,132,..., dimensions={0} | all-to-all | bytes 16384 | tf_op jit(solution)/shard_map/all_to_all | solution.py:700
  76.4 1.0 %shard_map.143 = (f32[3,8,16,256]{3,2,1,0:T(8,128)}, f32[3,8,8,128]{3,2,1,0:T(8,128)}, f32[1]{0:T(128)}, f32[1]{0:T(128)}, s32[1]{0:T(128)}) custom-call(f32[16,128]{1,0:T(8,128)S(1)} %bitcast.13, f32[3,8,16,256]{3,2,1,0:T(8,128)S(1)} %copy-done, f32[3,8,16,256]{3,2,1,0:T(8,128)S(1)} %copy-done.1, f32[3,8,8,128]{3,2,1,0:T(8,128)S(1)} %copy-done.2, ...), custom_call_target="tpu_custom_call" | custom-call | tf_op jit(solution)/shard_map/pallas_call | solution.py:701
  (2 shorter events, 0.0 us)
Async XLA Ops:
  2.9 16.3 %collective-permute-start = (f32[40,128]{1,0:T(8,128)}, f32[40,128]{1,0:T(8,128)S(1)}, u32[]{:S(2)}, u32[]{:S(2)}) collective-permute-start(f32[40,128]{1,0:T(8,128)} %get-tuple-element.30), channel_id=1, source_target_pairs={{0,1},{1,0},{2,3},{3,2},{4,5},{5,4},{6,7},{7,6},{8,9},{9,8},{10,11... | collective-permute-start | bytes 61448 | tf_op jit(solution)/shard_map/ppermute | solution.py:593
  12.6 6.7 %collective-permute-start.1 = (f32[40,128]{1,0:T(8,128)}, f32[40,128]{1,0:T(8,128)S(1)}, u32[]{:S(2)}, u32[]{:S(2)}) collective-permute-start(f32[40,128]{1,0:T(8,128)} %get-tuple-element.31), channel_id=1, source_target_pairs={{1,2},{3,4},{5,6},{7,8},{9,10},{11,12},{13,14},{2,1},{4,3},{6,5},{... | collective-permute-start | bytes 61448 | tf_op jit(solution)/shard_map/ppermute | solution.py:593
  13.2 13.9 %collective-permute-start.2 = (f32[456,128]{1,0:T(8,128)}, f32[456,128]{1,0:T(8,128)}, u32[]{:S(2)}, u32[]{:S(2)}) collective-permute-start(f32[456,128]{1,0:T(8,128)} %get-tuple-element.32), channel_id=1, source_target_pairs={{0,16},{16,0},{32,48},{48,32},{64,80},{80,64},{96,112},{112,96},{1... | collective-permute-start | bytes 700424 | tf_op jit(solution)/shard_map/ppermute | solution.py:593
  16.1 11.0 %collective-permute-start.3 = (f32[456,128]{1,0:T(8,128)}, f32[456,128]{1,0:T(8,128)}, u32[]{:S(2)}, u32[]{:S(2)}) collective-permute-start(f32[456,128]{1,0:T(8,128)} %get-tuple-element.33), channel_id=1, source_target_pairs={{16,32},{48,64},{80,96},{112,128},{144,160},{176,192},{208,224},{2... | collective-permute-start | bytes 700424 | tf_op jit(solution)/shard_map/ppermute | solution.py:593
  19.2 7.9 %copy-start = (f32[3,8,16,256]{3,2,1,0:T(8,128)S(1)}, f32[3,8,16,256]{3,2,1,0:T(8,128)}, u32[]{:S(2)}) copy-start(f32[3,8,16,256]{3,2,1,0:T(8,128)} %fn.1) | copy-start | bytes 1179652
  19.2 7.9 %copy-start.1 = (f32[3,8,16,256]{3,2,1,0:T(8,128)S(1)}, f32[3,8,16,256]{3,2,1,0:T(8,128)}, u32[]{:S(2)}) copy-start(f32[3,8,16,256]{3,2,1,0:T(8,128)} %fb.1) | copy-start | bytes 1179652
  19.3 7.9 %copy-start.2 = (f32[3,8,8,128]{3,2,1,0:T(8,128)S(1)}, f32[3,8,8,128]{3,2,1,0:T(8,128)}, u32[]{:S(2)}) copy-start(f32[3,8,8,128]{3,2,1,0:T(8,128)} %cn.1) | copy-start | bytes 294916
  19.3 7.9 %copy-start.3 = (f32[3,8,8,128]{3,2,1,0:T(8,128)S(1)}, f32[3,8,8,128]{3,2,1,0:T(8,128)}, u32[]{:S(2)}) copy-start(f32[3,8,8,128]{3,2,1,0:T(8,128)} %cb.1) | copy-start | bytes 294916
  19.3 7.9 %copy-start.4 = (f32[8,16,256]{2,1,0:T(8,128)S(1)}, f32[8,16,256]{2,1,0:T(8,128)}, u32[]{:S(2)}) copy-start(f32[8,16,256]{2,1,0:T(8,128)} %refs_2_.3) | copy-start | bytes 393220
  19.3 7.9 %copy-start.5 = (f32[8,16,256]{2,1,0:T(8,128)S(1)}, f32[8,16,256]{2,1,0:T(8,128)}, u32[]{:S(2)}) copy-start(f32[8,16,256]{2,1,0:T(8,128)} %refs_3_.3) | copy-start | bytes 393220
  19.3 7.9 %copy-start.6 = (f32[8,16,256]{2,1,0:T(8,128)S(1)}, f32[8,16,256]{2,1,0:T(8,128)}, u32[]{:S(2)}) copy-start(f32[8,16,256]{2,1,0:T(8,128)} %refs_4_.3) | copy-start | bytes 393220
  19.3 7.9 %copy-start.7 = (bf16[384,512]{1,0:T(8,128)(2,1)S(1)}, bf16[384,512]{1,0:T(8,128)(2,1)}, u32[]{:S(2)}) copy-start(bf16[384,512]{1,0:T(8,128)(2,1)} %constant.12.clone.refs_16_) | copy-start | bytes 1179652
  19.3 7.9 %copy-start.8 = (f32[8,8,128]{2,1,0:T(8,128)S(1)}, f32[8,8,128]{2,1,0:T(8,128)}, u32[]{:S(2)}) copy-start(f32[8,8,128]{2,1,0:T(8,128)} %refs_7_.3) | copy-start | bytes 98308
  19.3 7.9 %copy-start.9 = (f32[8,8,128]{2,1,0:T(8,128)S(1)}, f32[8,8,128]{2,1,0:T(8,128)}, u32[]{:S(2)}) copy-start(f32[8,8,128]{2,1,0:T(8,128)} %refs_8_.3) | copy-start | bytes 98308
  19.4 7.9 %copy-start.10 = (f32[8,8,128]{2,1,0:T(8,128)S(1)}, f32[8,8,128]{2,1,0:T(8,128)}, u32[]{:S(2)}) copy-start(f32[8,8,128]{2,1,0:T(8,128)} %refs_9_.3) | copy-start | bytes 98308
  19.4 7.8 %copy-start.11 = (bf16[256,256]{1,0:T(8,128)(2,1)S(1)}, bf16[256,256]{1,0:T(8,128)(2,1)}, u32[]{:S(2)}) copy-start(bf16[256,256]{1,0:T(8,128)(2,1)} %constant.13.clone.refs_17_) | copy-start | bytes 393220
  19.4 5.7 %collective-permute-start.4 = (f32[48,128]{1,0:T(8,128)S(1)}, f32[48,128]{1,0:T(8,128)S(1)}, u32[]{:S(2)}, u32[]{:S(2)}) collective-permute-start(f32[48,128]{1,0:T(8,128)S(1)} %get-tuple-element.34), channel_id=1, source_target_pairs={{0,16},{16,0},{32,48},{48,32},{64,80},{80,64},{96,112},{112,96},{1... | collective-permute-start | bytes 73736 | tf_op jit(solution)/shard_map/ppermute | solution.py:593
  22.0 5.1 %collective-permute-start.5 = (f32[48,128]{1,0:T(8,128)S(1)}, f32[48,128]{1,0:T(8,128)S(1)}, u32[]{:S(2)}, u32[]{:S(2)}) collective-permute-start(f32[48,128]{1,0:T(8,128)S(1)} %get-tuple-element.35), channel_id=1, source_target_pairs={{16,32},{48,64},{80,96},{112,128},{144,160},{176,192},{208,224},{2... | collective-permute-start | bytes 73736 | tf_op jit(solution)/shard_map/ppermute | solution.py:593

commit v3 on v2

--- a/solution.py
+++ b/solution.py
@@ -100,9 +100,11 @@
 
 def pack(*refs):
     sources = dict(zip(NAMES, refs[:10]))
-    column_outs, row_outs = refs[10:12], refs[12:14]
-    named = dict(zip(NAMES, refs[14:24]))
-    sems = refs[24]
+    targets, packs = refs[10:14], refs[14:18]
+    column_outs, row_outs = packs[:2], packs[2:]
+    named = dict(zip(NAMES, refs[18:28]))
+    sems, out_sems = refs[28:30]
+    sends = [pltpu.make_async_copy(source, target, out_sems.at[i]) for i, (source, target) in enumerate(zip(packs, targets))]
     copies = []
     for i, (name, part) in enumerate(PACK_SOURCES):
         source, target = sources[name], named[name]
@@ -125,6 +127,8 @@
             high_sum = jnp.where(inside, turned(own_tile(named, key, 0), at, 1), high_sum)
         span = slice(base, base + rows)
         column_outs[0][span, :], column_outs[1][span, :] = pair("gy", low_sum, high_sum)
+    for send in sends[:2]:
+        send.start()
     row_outs[0][RIM_ROWS - 8 :, :] = jnp.zeros((8, LANES), jnp.float32)
     row_outs[1][RIM_ROWS - 8 :, :] = jnp.zeros((8, LANES), jnp.float32)
     for (name, index), low, _, _, _, row, own in ENTRIES:
@@ -136,6 +140,10 @@
             row_outs[0][span, :], row_outs[1][span, :] = pair(
                 "gx", ref[index + (slice(rows - low, rows), lanes)], ref[index + (slice(0, low), lanes)]
             )
+    for send in sends[2:]:
+        send.start()
+    for send in sends:
+        send.wait()
 
 
 def pack_corners(first, second, first_out, second_out):
@@ -262,12 +270,23 @@
     return jnp.max(total)
 
 
-def start_line(lines):
-    ends = [a + STEP_LOW * b for a, b in lines]
-    top = largest(ends)
-    slope = largest([jnp.where(e == top, b, FAR) for e, (_, b) in zip(ends, lines)])
-    begin = largest([jnp.where((e == top) & (b == slope), a, FAR) for e, (a, b) in zip(ends, lines)])
+def smallest(values):
+    total = values[0]
+    for value in values[1:]:
+        total = jnp.minimum(total, value)
+    return jnp.min(total)
+
+
+def pick(lines, marks, wanted):
+    begin = smallest([jnp.where(m == wanted, a, -FAR) for m, (a, _) in zip(marks, lines)])
+    slope = largest([jnp.where(m == wanted, b, FAR) for m, (_, b) in zip(marks, lines)])
     return begin, slope
+
+
+def top_line(lines, step):
+    values = [a + step * b for a, b in lines]
+    top = largest(values)
+    return pick(lines, values, top)
 
 
 def next_line(lines, begin, slope, limit):
@@ -275,21 +294,24 @@
     for a, b in lines:
         steeper = b - slope
         crossings.append(jnp.where(steeper > 0.0, (begin - a) / steeper, -FAR))
-    nearest = -largest([-s for s in crossings])
+    nearest = smallest(crossings)
     found = nearest <= limit
-    new_slope = largest([jnp.where(s == nearest, b, FAR) for s, (_, b) in zip(crossings, lines)])
-    new_begin = largest(
-        [jnp.where((s == nearest) & (b == new_slope), a, FAR) for s, (a, b) in zip(crossings, lines)]
-    )
+    new_begin, new_slope = pick(lines, crossings, nearest)
     return jnp.where(found, new_begin, begin), jnp.where(found, new_slope, slope), found
 
 
 def envelopes(first, last, peak):
     lane = iota((1, LANES), 1)
     bound = 0.3 / jnp.full((8, LANES), peak, jnp.float32)
-    limit = jnp.max(bound * bound) * 1.00001
-    first_begin, first_slope = start_line(first)
-    last_begin, last_slope = start_line(last)
+    bound = bound * bound * 1.00001
+    limit = jnp.max(bound)
+    first_begin, first_slope = top_line(first, STEP_LOW)
+    last_begin, last_slope = top_line(last, STEP_LOW)
+    first_top = largest([a + bound * b for a, b in first])
+    last_top = largest([a + bound * b for a, b in last])
+    single = (jnp.max(first_begin + bound * first_slope) >= first_top) & (
+        jnp.max(last_begin + bound * last_slope) >= last_top
+    )
     message = jnp.where(
         lane < 32,
         first_begin,
@@ -301,16 +323,17 @@
 
     def step(state):
         n, _, fa, fb, la, lb, message = state
+        fa, fb, found_first = next_line(first, fa, fb, limit)
+        la, lb, found_last = next_line(last, la, lb, limit)
         message = jnp.where(lane == n, fa, message)
         message = jnp.where(lane == n + 32, fb, message)
         message = jnp.where(lane == n + 64, la, message)
         message = jnp.where(lane == n + 96, lb, message)
-        fa, fb, found_first = next_line(first, fa, fb, limit)
-        la, lb, found_last = next_line(last, la, lb, limit)
         found = (found_first | found_last).astype(jnp.int32)
         return n + 1, found, fa, fb, la, lb, message
 
-    start = (jnp.int32(0), jnp.int32(1), first_begin, first_slope, last_begin, last_slope, message)
+    left = jnp.where(single, 0, 1).astype(jnp.int32)
+    start = (jnp.int32(1), left, first_begin, first_slope, last_begin, last_slope, message)
     _, left, _, _, _, _, message = lax.while_loop(more, step, start)
     return message, left.astype(jnp.float32)
 
@@ -339,12 +362,16 @@
 
 def main_kernel(*refs):
     named = dict(zip(NAMES, refs[:10]))
-    sides, rims, corners = refs[10:12], refs[12:14], refs[14:16]
+    sides, rim_sources, corners = refs[10:12], refs[12:14], refs[14:16]
     split_pick, weave_pick = refs[16:18]
     fine_rate, coarse_rate, plane_out, iterate_out, lines_out, message_out = refs[18:24]
     fine, fine_x, fine_y, rest, coarse, coarse_x, coarse_y, coarse_rest = refs[24:32]
     mixed, planes, parted, woven, ends = refs[32:37]
     packed = dict(zip("ABC", zip(refs[37:40], refs[40:43])))
+    rims, sems = refs[43:45], refs[45]
+    copies = [pltpu.make_async_copy(source, rims[i], sems.at[i]) for i, source in enumerate(rim_sources)]
+    for copy in copies:
+        copy.start()
 
     def received(axis, pieces, span):
         return pair(axis, pieces[1][span, :], pieces[0][span, :])
@@ -375,15 +402,11 @@
         target = home(key)
         rows = TILE_ROWS[tile][1]
         total = target.shape[1]
-        if low > 2:
-            for t in range(own):
+        for t in range(own):
+            if low > 2:
                 target[t, 0:rows, :] = jnp.zeros((rows, LANES), jnp.float32)
                 target[t, 2 * rows : total, :] = jnp.zeros((total - 2 * rows, LANES), jnp.float32)
-        for t in range(own):
             target[t, rows : 2 * rows, :] = own_tile(named, key, t)
-            below, beyond = received("gx", rims, slice(row + t * low, row + t * low + low))
-            target[t, rows - low : rows, :] = below
-            target[t, 2 * rows : 2 * rows + low, :] = beyond
         low_side, high_side = packed[tile][0][...], packed[tile][1][...]
         lane = iota(low_side.shape, 1)
         target[own, :, :] = jnp.where(
@@ -391,18 +414,24 @@
             turned(high_side, -at, 1),
             jnp.where(lane >= LANES - low, turned(low_side, -(at + low), 1), 0.0),
         )
+    for copy in copies:
+        copy.wait()
+    for key, low, high, tile, at, row, own in ENTRIES:
+        target = home(key)
+        rows = TILE_ROWS[tile][1]
+        for t in range(own):
+            below, beyond = received("gx", rims, slice(row + t * low, row + t * low + low))
+            target[t, rows - low : rows, :] = below
+            target[t, 2 * rows : 2 * rows + low, :] = beyond
     coarse[:, 8] = jnp.zeros(coarse.shape[:1] + coarse.shape[2:], jnp.float32)
 
-    def fine_slopes(k, carry):
+    for k in range(5):
         slopes(fine, fine_x, fine_y, k, 16, 16, 2, 1.0)
-        return carry
-
-    lax.fori_loop(0, 5, fine_slopes, 0)
     for k in (5, 6, 7):
         slopes(fine, fine_x, fine_y, k, 8, 32, 3, 1.0)
 
-    def fine_plane(k, carry):
-        above = jnp.where(k == 0, 1, k - 1)
+    def fine_plane(k):
+        above = 1 if k == 0 else k - 1
         own = [slice(t * LANES, (t + 1) * LANES) for t in range(2)]
         shear = [named["fs"][k, :, lanes] for lanes in own]
         lame = [named["fl"][k, :, lanes] for lanes in own]
@@ -410,9 +439,9 @@
         for c in range(3):
             for t in range(2):
                 fine_rate[c, k, :, own[t]] = accel[c][t] / named["fd"][k, :, own[t]]
-        return carry
-
-    lax.fori_loop(0, 6, fine_plane, 0)
+
+    for k in range(6):
+        fine_plane(k)
 
     window = slice(8, 40)
     shear = [rest[slot[("fs", (6,))], t, window, :] for t in range(3)]
@@ -457,15 +486,15 @@
     coarse_x[8] = jnp.zeros(coarse_x.shape[1:], jnp.float32)
     coarse_y[8] = jnp.zeros(coarse_y.shape[1:], jnp.float32)
 
-    def coarse_plane(k, carry):
+    def coarse_plane(k):
         shear = [named["cs"][k]]
         lame = [named["cl"][k]]
         accel = acceleration(coarse, coarse_x, coarse_y, mixed, (k - 1, k, k + 1), 8, 8, 1, 2.0, shear, lame)
         for c in range(3):
             coarse_rate[c, k - 1] = accel[c][0] / named["cd"][k]
-        return carry
-
-    lax.fori_loop(2, 8, coarse_plane, 0)
+
+    for k in range(2, 8):
+        coarse_plane(k)
     band = slice(4, 20)
 
     def coarse_pair(name, k):
@@ -594,12 +623,13 @@
 
 
 def gather_groups(columns, rows):
-    near, ring = {}, {}
+    ring, plane = {}, {}
     for i in range(columns):
         for j in range(rows):
-            near.setdefault((i // 8, j % 4), []).append(i * rows + j)
-            ring.setdefault((i % 8, j // 4), []).append(i * rows + j)
-    return list(near.values()), list(ring.values())
+            chip_y, core, z, x = i // 2 % 4, i % 2, (i // 8, j % 4), j // 4
+            ring.setdefault((x, chip_y), []).append(i * rows + j)
+            plane.setdefault((z, core), []).append(i * rows + j)
+    return list(ring.values()), list(plane.values())
 
 
 def split_matrix():
@@ -627,7 +657,7 @@
 
 
 def make_shards(columns, rows):
-    near, ring = gather_groups(columns, rows)
+    ring, plane_groups = gather_groups(columns, rows)
     axes = ("gx", "gy")
 
     def shards(*args):
@@ -651,7 +681,11 @@
             pack,
             [in_hbm] * 10,
             (f32(PACKED_ROWS, LANES),) * 2 + (f32(RIM_ROWS, LANES),) * 2,
-            [vm(*a.shape) for a in args] + [pltpu.SemaphoreType.DMA((len(PACK_SOURCES),))],
+            [vm(PACKED_ROWS, LANES)] * 2
+            + [vm(RIM_ROWS, LANES)] * 2
+            + [vm(*a.shape) for a in args]
+            + [pltpu.SemaphoreType.DMA((len(PACK_SOURCES),)), pltpu.SemaphoreType.DMA((4,))],
+            out_specs=[in_hbm] * 4,
             limit=63,
         )(*args)
         sides = exchange(first_side, second_side, "gy", rows)
@@ -663,14 +697,14 @@
             cost=pl.CostEstimate(flops=10**12, bytes_accessed=10**9, transcendentals=0),
         )(*sides)
         corners = exchange(first, second, "gx", columns)
-        near_size, ring_size = len(near[0]), len(ring[0])
+        ring_size, plane_size = len(ring[0]), len(plane_groups[0])
         outs = (
             f32(3, 7, 16, 256),
             f32(3, 7, 8, 128),
             f32(2, 3, 2, 16, 128),
             f32(2, 3, 8, 128),
             f32(4, 3, 8, 128),
-            f32(near_size, LANES),
+            f32(ring_size, LANES),
         )
         scratch = (
             vm(3, 8, 3, 48, LANES),
@@ -687,7 +721,9 @@
             vm(192, 256),
             vm(6, 3, 16, LANES),
         ) + (vm(48, LANES), vm(48, LANES), vm(24, LANES)) * 2
-        fine_rate, coarse_rate, plane, iterate, lines, message = call(main_kernel, [in_vmem] * 18, outs, scratch)(
+        scratch += (vm(RIM_ROWS, LANES), vm(RIM_ROWS, LANES), pltpu.SemaphoreType.DMA((2,)))
+        ins = [in_vmem] * 12 + [in_hbm] * 2 + [in_vmem] * 4
+        fine_rate, coarse_rate, plane, iterate, lines, message = call(main_kernel, ins, outs, scratch)(
             *args,
             *sides,
             *rims,
@@ -695,9 +731,9 @@
             jnp.asarray(split_matrix()),
             jnp.asarray(weave_matrix()),
         )
-        received = lax.all_to_all(message, axes, 0, 0, tiled=True, axis_index_groups=near)
-        message = call(merge_kernel, [in_vmem], f32(ring_size, LANES))(received)
         received = lax.all_to_all(message, axes, 0, 0, tiled=True, axis_index_groups=ring)
+        message = call(merge_kernel, [in_vmem], f32(plane_size, LANES))(received)
+        received = lax.all_to_all(message, axes, 0, 0, tiled=True, axis_index_groups=plane_groups)
         fine_next, coarse_next, ratio, square, flag = call(
             final_kernel,
             [in_vmem] * 9,

time: 78.3 us -> 75 us (0.958)
  Pallas kernels: 11.9 us -> 8.49 us
    all_to_all x1, blocking collectives: 17.1 us -> 29.2 us  [shards(): lax.all_to_all(message, axes, 0, 0, tiled=True, axis_index_groups=ring)]
    all_to_all x1, blocking collectives: 23.5 us -> 11.4 us  [shards(): lax.all_to_all(message, axes, 0, 0, tiled=True, axis_index_groups=plane_g...]
    pallas_call x2, Pallas kernels: 8.63 us -> 5.19 us  [the longest x1 4.71 us: shards(): call(main_kernel, ins, outs, scratch)]
where the time goes in v3:
time: 75 us; the launch traced here: 74.7 us
  blocking collectives  40.6 us (54%)
  starting transfers between devices  21.9 us (29%)
  Pallas kernels  8.49 us (11%)
  waiting for transfers between devices  2.04 us (3%)
  between operations  1.49 us (2%)
    all_to_all x1, blocking collectives, shards(): lax.all_to_all(message, axes, 0, 0, tiled=True, axis_index_groups=ring)  29.2 us
    ppermute x6, starting transfers between devices, exchange(): return (lax.ppermute(first, axis, near), lax.ppermute(second, axis, far))  21.9 us
    all_to_all x1, blocking collectives, shards(): lax.all_to_all(message, axes, 0, 0, tiled=True, axis_index_groups=plane_g...  11.4 us
    pallas_call x1, Pallas kernels, shards(): call(main_kernel, ins, outs, scratch)  4.71 us
    pallas_call x1, Pallas kernels, shards(): call(pack, [in_hbm] * 10, (f32(PACKED_ROWS, LANES),) * 2 + (f32(RIM_ROWS,...  2.31 us
    ppermute x6, waiting for transfers between devices, exchange(): return (lax.ppermute(first, axis, near), lax.ppermute(second, axis, far))  2.04 us
  transfers between devices with their start and end apart: 6, of which 1 were waited for; matrix products, arithmetic and copies ran while one was open for 0% of the time, Pallas kernels for 0%

profile of v3, /device:TPU:1, one launch (start us, length us, event | category | flops | bytes accessed | tf_op | source)
XLA Modules:
  0.0 74.7 jit_solution(6547043607686557769)
XLA Ops:
  0.6 2.3 %shard_map.139 = (f32[40,128]{1,0:T(8,128)}, f32[40,128]{1,0:T(8,128)}, f32[456,128]{1,0:T(8,128)}, f32[456,128]{1,0:T(8,128)}) custom-call(f32[3,8,16,256]{3,2,1,0:T(8,128)} %fn.1, f32[3,8,16,256]{3,2,1,0:T(8,128)} %fb.1, f32[8,16,256]{2,1,0:T(8,128)} %refs_2_.3, f32[8,16,256]{2,1,0:T(8,128)} %refs_3_.3, f32[8,16,256]{2,1,0:T(8,128)} %refs_4_.3, ...), custom_call_target="tpu_custom_call" | custom-call | tf_op jit(solution)/shard_map/pallas_call | solution.py:680
  2.9 9.6 %collective-permute-start = (f32[40,128]{1,0:T(8,128)}, f32[40,128]{1,0:T(8,128)S(1)}, u32[]{:S(2)}, u32[]{:S(2)}) collective-permute-start(f32[40,128]{1,0:T(8,128)} %get-tuple-element.30), channel_id=1, source_target_pairs={{0,1},{1,0},{2,3},{3,2},{4,5},{5,4},{6,7},{7,6},{8,9},{9,8},{10,11... | collective-permute-start | bytes 61448 | tf_op jit(solution)/shard_map/ppermute | solution.py:622
  12.6 0.7 collective-permute-start.1
  13.3 2.9 %collective-permute-start.2 = (f32[456,128]{1,0:T(8,128)}, f32[456,128]{1,0:T(8,128)}, u32[]{:S(2)}, u32[]{:S(2)}) collective-permute-start(f32[456,128]{1,0:T(8,128)} %get-tuple-element.32), channel_id=1, source_target_pairs={{0,16},{16,0},{32,48},{48,32},{64,80},{80,64},{96,112},{112,96},{1... | collective-permute-start | bytes 700424 | tf_op jit(solution)/shard_map/ppermute | solution.py:622
  16.1 3.1 %collective-permute-start.3 = (f32[456,128]{1,0:T(8,128)}, f32[456,128]{1,0:T(8,128)}, u32[]{:S(2)}, u32[]{:S(2)}) collective-permute-start(f32[456,128]{1,0:T(8,128)} %get-tuple-element.33), channel_id=1, source_target_pairs={{16,32},{48,64},{80,96},{112,128},{144,160},{176,192},{208,224},{2... | collective-permute-start | bytes 700424 | tf_op jit(solution)/shard_map/ppermute | solution.py:622
  19.3 0.0 collective-permute-done.first.refs_10_
  19.3 0.0 collective-permute-done.1.second.refs_11_
  19.3 0.0 copy-start
  19.3 0.0 copy-start.1
  19.3 0.0 copy-start.2
  19.3 0.0 copy-start.3
  19.3 0.0 copy-start.4
  19.3 0.0 copy-start.5
  19.3 0.0 copy-start.6
  19.4 0.0 copy-start.7
  19.4 0.0 copy-start.8
  19.4 0.0 copy-start.9
  19.4 0.0 copy-start.10
  19.4 0.0 copy-start.11
  19.5 2.5 %collective-permute-start.4 = (f32[48,128]{1,0:T(8,128)S(1)}, f32[48,128]{1,0:T(8,128)S(1)}, u32[]{:S(2)}, u32[]{:S(2)}) collective-permute-start(f32[48,128]{1,0:T(8,128)S(1)} %get-tuple-element.34), channel_id=1, source_target_pairs={{0,16},{16,0},{32,48},{48,32},{64,80},{80,64},{96,112},{112,96},{1... | collective-permute-start | bytes 73736 | tf_op jit(solution)/shard_map/ppermute | solution.py:622
  22.0 3.1 %collective-permute-start.5 = (f32[48,128]{1,0:T(8,128)S(1)}, f32[48,128]{1,0:T(8,128)S(1)}, u32[]{:S(2)}, u32[]{:S(2)}) collective-permute-start(f32[48,128]{1,0:T(8,128)S(1)} %get-tuple-element.35), channel_id=1, source_target_pairs={{16,32},{48,64},{80,96},{112,128},{144,160},{176,192},{208,224},{2... | collective-permute-start | bytes 73736 | tf_op jit(solution)/shard_map/ppermute | solution.py:622
  25.1 0.0 collective-permute-done.4.refs_14_
  25.1 2.0 %collective-permute-done.5.refs_15_ = f32[48,128]{1,0:T(8,128)S(1)} collective-permute-done((f32[48,128]{1,0:T(8,128)S(1)}, f32[48,128]{1,0:T(8,128)S(1)}, u32[]{:S(2)}, u32[]{:S(2)}) %collective-permute-start.5) | collective-permute-done | bytes 24608 | tf_op jit(solution)/shard_map/ppermute | solution.py:622
  27.1 0.0 collective-permute-done.2.refs_12_
  27.1 0.0 collective-permute-done.3.refs_13_
  27.2 0.0 copy-done
  27.2 0.0 copy-done.1
  27.2 0.0 copy-done.2
  27.2 0.0 copy-done.3
  27.2 0.0 copy-done.4
  27.2 0.0 copy-done.5
  27.2 0.0 copy-done.6
  27.2 0.0 copy-done.7
  27.2 0.0 copy-done.8
  27.2 0.0 copy-done.9
  27.2 0.0 copy-done.10
  27.3 0.0 copy-done.11
  27.3 4.7 %shard_map.141 = (f32[3,7,16,256]{3,2,1,0:T(8,128)S(1)}, f32[3,7,8,128]{3,2,1,0:T(8,128)S(1)}, f32[2,3,2,16,128]{4,3,2,1,0:T(8,128)S(1)}, f32[2,3,8,128]{3,2,1,0...) custom-call(f32[3,8,16,256]{3,2,1,0:T(8,128)S(1)} %copy-done, f32[3,8,16,256]{3,2,1,0:T(8,128)S(1)} %copy-done.1, ...), custom_call_target="tpu_custom_call" | custom-call | tf_op jit(solution)/shard_map/pallas_call | solution.py:726
  32.0 29.2 %all_to_all.22 = f32[32,1,128]{2,1,0:T(1,128)S(1)} all-to-all(f32[32,1,128]{2,1,0:T(1,128)S(1)} %bitcast.15), channel_id=1, replica_groups={{0,1,2,3,16,17,18,19,128,129,130,131,144,145,146,147,256,257,258,259,27..., dimensions={0} | all-to-all | bytes 32768 | tf_op jit(solution)/shard_map/all_to_all | solution.py:734
  61.2 0.5 shard_map.142
  61.7 11.4 %all_to_all.23 = f32[16,1,128]{2,1,0:T(1,128)S(1)} all-to-all(f32[16,1,128]{2,1,0:T(1,128)S(1)} %bitcast.14), channel_id=1, replica_groups={{0,4,8,12,32,36,40,44,64,68,72,76,96,100,104,108},{1,5,9,13,33,37,41,45..., dimensions={0} | all-to-all | bytes 16384 | tf_op jit(solution)/shard_map/all_to_all | solution.py:736
  73.1 1.0 %shard_map.143 = (f32[3,8,16,256]{3,2,1,0:T(8,128)}, f32[3,8,8,128]{3,2,1,0:T(8,128)}, f32[1]{0:T(128)}, f32[1]{0:T(128)}, s32[1]{0:T(128)}) custom-call(f32[16,128]{1,0:T(8,128)S(1)} %bitcast.13, f32[3,8,16,256]{3,2,1,0:T(8,128)S(1)} %copy-done, f32[3,8,16,256]{3,2,1,0:T(8,128)S(1)} %copy-done.1, f32[3,8,8,128]{3,2,1,0:T(8,128)S(1)} %copy-done.2, ...), custom_call_target="tpu_custom_call" | custom-call | tf_op jit(solution)/shard_map/pallas_call | solution.py:737
  (2 shorter events, 0.0 us)
Async XLA Ops:
  2.9 16.3 %collective-permute-start = (f32[40,128]{1,0:T(8,128)}, f32[40,128]{1,0:T(8,128)S(1)}, u32[]{:S(2)}, u32[]{:S(2)}) collective-permute-start(f32[40,128]{1,0:T(8,128)} %get-tuple-element.30), channel_id=1, source_target_pairs={{0,1},{1,0},{2,3},{3,2},{4,5},{5,4},{6,7},{7,6},{8,9},{9,8},{10,11... | collective-permute-start | bytes 61448 | tf_op jit(solution)/shard_map/ppermute | solution.py:622
  12.6 6.7 %collective-permute-start.1 = (f32[40,128]{1,0:T(8,128)}, f32[40,128]{1,0:T(8,128)S(1)}, u32[]{:S(2)}, u32[]{:S(2)}) collective-permute-start(f32[40,128]{1,0:T(8,128)} %get-tuple-element.31), channel_id=1, source_target_pairs={{1,2},{3,4},{5,6},{7,8},{9,10},{11,12},{13,14},{2,1},{4,3},{6,5},{... | collective-permute-start | bytes 61448 | tf_op jit(solution)/shard_map/ppermute | solution.py:622
  13.3 13.9 %collective-permute-start.2 = (f32[456,128]{1,0:T(8,128)}, f32[456,128]{1,0:T(8,128)}, u32[]{:S(2)}, u32[]{:S(2)}) collective-permute-start(f32[456,128]{1,0:T(8,128)} %get-tuple-element.32), channel_id=1, source_target_pairs={{0,16},{16,0},{32,48},{48,32},{64,80},{80,64},{96,112},{112,96},{1... | collective-permute-start | bytes 700424 | tf_op jit(solution)/shard_map/ppermute | solution.py:622
  16.1 11.0 %collective-permute-start.3 = (f32[456,128]{1,0:T(8,128)}, f32[456,128]{1,0:T(8,128)}, u32[]{:S(2)}, u32[]{:S(2)}) collective-permute-start(f32[456,128]{1,0:T(8,128)} %get-tuple-element.33), channel_id=1, source_target_pairs={{16,32},{48,64},{80,96},{112,128},{144,160},{176,192},{208,224},{2... | collective-permute-start | bytes 700424 | tf_op jit(solution)/shard_map/ppermute | solution.py:622
  19.3 7.9 %copy-start = (f32[3,8,16,256]{3,2,1,0:T(8,128)S(1)}, f32[3,8,16,256]{3,2,1,0:T(8,128)}, u32[]{:S(2)}) copy-start(f32[3,8,16,256]{3,2,1,0:T(8,128)} %fn.1) | copy-start | bytes 1179652
  19.3 7.9 %copy-start.1 = (f32[3,8,16,256]{3,2,1,0:T(8,128)S(1)}, f32[3,8,16,256]{3,2,1,0:T(8,128)}, u32[]{:S(2)}) copy-start(f32[3,8,16,256]{3,2,1,0:T(8,128)} %fb.1) | copy-start | bytes 1179652
  19.3 7.9 %copy-start.2 = (f32[3,8,8,128]{3,2,1,0:T(8,128)S(1)}, f32[3,8,8,128]{3,2,1,0:T(8,128)}, u32[]{:S(2)}) copy-start(f32[3,8,8,128]{3,2,1,0:T(8,128)} %cn.1) | copy-start | bytes 294916
  19.3 7.9 %copy-start.3 = (f32[3,8,8,128]{3,2,1,0:T(8,128)S(1)}, f32[3,8,8,128]{3,2,1,0:T(8,128)}, u32[]{:S(2)}) copy-start(f32[3,8,8,128]{3,2,1,0:T(8,128)} %cb.1) | copy-start | bytes 294916
  19.3 7.9 %copy-start.4 = (f32[8,16,256]{2,1,0:T(8,128)S(1)}, f32[8,16,256]{2,1,0:T(8,128)}, u32[]{:S(2)}) copy-start(f32[8,16,256]{2,1,0:T(8,128)} %refs_2_.3) | copy-start | bytes 393220
  19.3 7.9 %copy-start.5 = (f32[8,16,256]{2,1,0:T(8,128)S(1)}, f32[8,16,256]{2,1,0:T(8,128)}, u32[]{:S(2)}) copy-start(f32[8,16,256]{2,1,0:T(8,128)} %refs_3_.3) | copy-start | bytes 393220
  19.3 7.9 %copy-start.6 = (f32[8,16,256]{2,1,0:T(8,128)S(1)}, f32[8,16,256]{2,1,0:T(8,128)}, u32[]{:S(2)}) copy-start(f32[8,16,256]{2,1,0:T(8,128)} %refs_4_.3) | copy-start | bytes 393220
  19.4 7.9 %copy-start.7 = (bf16[384,512]{1,0:T(8,128)(2,1)S(1)}, bf16[384,512]{1,0:T(8,128)(2,1)}, u32[]{:S(2)}) copy-start(bf16[384,512]{1,0:T(8,128)(2,1)} %constant.12.clone.refs_16_) | copy-start | bytes 1179652
  19.4 7.9 %copy-start.8 = (f32[8,8,128]{2,1,0:T(8,128)S(1)}, f32[8,8,128]{2,1,0:T(8,128)}, u32[]{:S(2)}) copy-start(f32[8,8,128]{2,1,0:T(8,128)} %refs_7_.3) | copy-start | bytes 98308
  19.4 7.9 %copy-start.9 = (f32[8,8,128]{2,1,0:T(8,128)S(1)}, f32[8,8,128]{2,1,0:T(8,128)}, u32[]{:S(2)}) copy-start(f32[8,8,128]{2,1,0:T(8,128)} %refs_8_.3) | copy-start | bytes 98308
  19.4 7.9 %copy-start.10 = (f32[8,8,128]{2,1,0:T(8,128)S(1)}, f32[8,8,128]{2,1,0:T(8,128)}, u32[]{:S(2)}) copy-start(f32[8,8,128]{2,1,0:T(8,128)} %refs_9_.3) | copy-start | bytes 98308
  19.4 7.8 %copy-start.11 = (bf16[256,256]{1,0:T(8,128)(2,1)S(1)}, bf16[256,256]{1,0:T(8,128)(2,1)}, u32[]{:S(2)}) copy-start(bf16[256,256]{1,0:T(8,128)(2,1)} %constant.13.clone.refs_17_) | copy-start | bytes 393220
  19.5 5.7 %collective-permute-start.4 = (f32[48,128]{1,0:T(8,128)S(1)}, f32[48,128]{1,0:T(8,128)S(1)}, u32[]{:S(2)}, u32[]{:S(2)}) collective-permute-start(f32[48,128]{1,0:T(8,128)S(1)} %get-tuple-element.34), channel_id=1, source_target_pairs={{0,16},{16,0},{32,48},{48,32},{64,80},{80,64},{96,112},{112,96},{1... | collective-permute-start | bytes 73736 | tf_op jit(solution)/shard_map/ppermute | solution.py:622
  22.0 5.1 %collective-permute-start.5 = (f32[48,128]{1,0:T(8,128)S(1)}, f32[48,128]{1,0:T(8,128)S(1)}, u32[]{:S(2)}, u32[]{:S(2)}) collective-permute-start(f32[48,128]{1,0:T(8,128)S(1)} %get-tuple-element.35), channel_id=1, source_target_pairs={{16,32},{48,64},{80,96},{112,128},{144,160},{176,192},{208,224},{2... | collective-permute-start | bytes 73736 | tf_op jit(solution)/shard_map/ppermute | solution.py:622

commit v4 on v3

--- a/solution.py
+++ b/solution.py
@@ -181,7 +181,7 @@
 
 
 def slopes(field, along_x, along_y, plane, start, rows, wanted, spacing):
-    count = field.shape[2]
+    count = field.count
     for t in range(count):
         down2, down1, up1, up2 = (field[0, plane, t, pl.ds(start + d, rows), :] for d in (-2, -1, 1, 2))
         along_x[plane, t, start : start + rows, :] = first_of(down2, down1, up1, up2, spacing)
@@ -193,7 +193,7 @@
 
 def acceleration(field, along_x, along_y, mixed, planes, start, rows, wanted, spacing, shear, lame):
     above, plane, under = planes
-    count = field.shape[2]
+    count = field.count
     half = 1.0 / (2.0 * spacing)
     square = 1.0 / (spacing * spacing)
     span = slice(start, start + rows)
@@ -360,21 +360,62 @@
     return first, last, largest(peak), largest(flag)
 
 
+class Tiles:
+    def __init__(self, own, rim):
+        self.own, self.rim = own, rim
+        self.count = own.shape[-3] + 1
+
+    def __getitem__(self, index):
+        *plane, tile, rows, lanes = index
+        if tile < self.count - 1:
+            return self.own[(*plane, tile, rows, lanes)]
+        return self.rim[(*plane, rows, lanes)]
+
+
+def home(key, fine, rest, coarse, coarse_rest):
+    if key in DEEP_REST:
+        return rest.at[DEEP_REST.index(key)]
+    if key in COARSE_REST:
+        return coarse_rest.at[COARSE_REST.index(key)]
+    return (fine if key[0] == "fn" else coarse).at[key[1]]
+
+
+def received(axis, pieces, span):
+    return pair(axis, pieces[1][span, :], pieces[0][span, :])
+
+
+def place_kernel(*refs):
+    named = dict(zip(NAMES, refs[:10]))
+    rims, targets = refs[10:12], refs[12:16]
+    for key, low, _, tile, _, row, own in ENTRIES:
+        target = home(key, *targets)
+        rows = TILE_ROWS[tile][1]
+        total = target.shape[1]
+        for t in range(own):
+            if low > 2:
+                target[t, 0:rows, :] = jnp.zeros((rows, LANES), jnp.float32)
+                target[t, 2 * rows : total, :] = jnp.zeros((total - 2 * rows, LANES), jnp.float32)
+            target[t, rows : 2 * rows, :] = own_tile(named, key, t)
+            below, beyond = received("gx", rims, slice(row + t * low, row + t * low + low))
+            target[t, rows - low : rows, :] = below
+            target[t, 2 * rows : 2 * rows + low, :] = beyond
+    coarse = targets[2]
+    coarse[:, 8] = jnp.zeros(coarse.shape[:1] + coarse.shape[2:], jnp.float32)
+
+
 def main_kernel(*refs):
-    named = dict(zip(NAMES, refs[:10]))
-    sides, rim_sources, corners = refs[10:12], refs[12:14], refs[14:16]
-    split_pick, weave_pick = refs[16:18]
-    fine_rate, coarse_rate, plane_out, iterate_out, lines_out, message_out = refs[18:24]
-    fine, fine_x, fine_y, rest, coarse, coarse_x, coarse_y, coarse_rest = refs[24:32]
-    mixed, planes, parted, woven, ends = refs[32:37]
-    packed = dict(zip("ABC", zip(refs[37:40], refs[40:43])))
-    rims, sems = refs[43:45], refs[45]
-    copies = [pltpu.make_async_copy(source, rims[i], sems.at[i]) for i, source in enumerate(rim_sources)]
-    for copy in copies:
-        copy.start()
-
-    def received(axis, pieces, span):
-        return pair(axis, pieces[1][span, :], pieces[0][span, :])
+    named = dict(zip(("fd", "fs", "fl", "cd", "cs", "cl"), refs[:6]))
+    sides, corners = refs[6:8], refs[8:10]
+    split_pick, weave_pick = refs[10:12]
+    owns = refs[12:16]
+    fine_rate, coarse_rate, plane_out, iterate_out, lines_out, message_out = refs[16:22]
+    rims = refs[22:26]
+    fine_x, fine_y, coarse_x, coarse_y = refs[26:30]
+    mixed, planes, parted, woven, ends = refs[30:35]
+    packed = dict(zip("ABC", zip(refs[35:38], refs[38:41])))
+    fine, rest, coarse, coarse_rest = (Tiles(own, rim) for own, rim in zip(owns, rims))
+    slot = {key: i for i, key in enumerate(DEEP_REST)}
+    coarse_slot = {key: i for i, key in enumerate(COARSE_REST)}
 
     for tile, (base, rows) in TILE_ROWS.items():
         rim = TILE_RIM[tile]
@@ -387,43 +428,15 @@
             low, high = received("gx", corners, slice(row, row + rim))
             target[rows - rim : rows, :] = low
             target[2 * rows : 2 * rows + rim, :] = high
-
-    slot = {key: i for i, key in enumerate(DEEP_REST)}
-    coarse_slot = {key: i for i, key in enumerate(COARSE_REST)}
-
-    def home(key):
-        if key in slot:
-            return rest.at[slot[key]]
-        if key in coarse_slot:
-            return coarse_rest.at[coarse_slot[key]]
-        return (fine if key[0] == "fn" else coarse).at[key[1]]
-
-    for key, low, high, tile, at, row, own in ENTRIES:
-        target = home(key)
-        rows = TILE_ROWS[tile][1]
-        total = target.shape[1]
-        for t in range(own):
-            if low > 2:
-                target[t, 0:rows, :] = jnp.zeros((rows, LANES), jnp.float32)
-                target[t, 2 * rows : total, :] = jnp.zeros((total - 2 * rows, LANES), jnp.float32)
-            target[t, rows : 2 * rows, :] = own_tile(named, key, t)
+    for key, low, high, tile, at, _, _ in ENTRIES:
         low_side, high_side = packed[tile][0][...], packed[tile][1][...]
         lane = iota(low_side.shape, 1)
-        target[own, :, :] = jnp.where(
+        home(key, *rims)[...] = jnp.where(
             lane < high,
             turned(high_side, -at, 1),
             jnp.where(lane >= LANES - low, turned(low_side, -(at + low), 1), 0.0),
         )
-    for copy in copies:
-        copy.wait()
-    for key, low, high, tile, at, row, own in ENTRIES:
-        target = home(key)
-        rows = TILE_ROWS[tile][1]
-        for t in range(own):
-            below, beyond = received("gx", rims, slice(row + t * low, row + t * low + low))
-            target[t, rows - low : rows, :] = below
-            target[t, 2 * rows : 2 * rows + low, :] = beyond
-    coarse[:, 8] = jnp.zeros(coarse.shape[:1] + coarse.shape[2:], jnp.float32)
+    rims[2][:, 8] = jnp.zeros(rims[2].shape[:1] + rims[2].shape[2:], jnp.float32)
 
     for k in range(5):
         slopes(fine, fine_x, fine_y, k, 16, 16, 2, 1.0)
@@ -665,7 +678,7 @@
         in_smem = pl.BlockSpec(memory_space=pltpu.SMEM)
         in_hbm = pl.BlockSpec(memory_space=pltpu.HBM)
 
-        def call(kernel, ins, outs, scratch=(), out_specs=None, cost=None, limit=48):
+        def call(kernel, ins, outs, scratch=(), out_specs=None, cost=None, limit=16):
             return pl.pallas_call(
                 kernel,
                 out_shape=outs,
@@ -698,6 +711,8 @@
         )(*sides)
         corners = exchange(first, second, "gx", columns)
         ring_size, plane_size = len(ring[0]), len(plane_groups[0])
+        own_shapes = ((3, 8, 2, 48, LANES), (8, 2, 48, LANES), (3, 9, 1, 24, LANES), (11, 1, 24, LANES))
+        owns = call(place_kernel, [in_vmem] * 12, tuple(f32(*shape) for shape in own_shapes))(*args, *rims)
         outs = (
             f32(3, 7, 16, 256),
             f32(3, 7, 8, 128),
@@ -706,30 +721,26 @@
             f32(4, 3, 8, 128),
             f32(ring_size, LANES),
         )
-        scratch = (
-            vm(3, 8, 3, 48, LANES),
+        scratch = [vm(*shape[:-3], *shape[-2:]) for shape in own_shapes] + [
             vm(8, 3, 48, LANES),
             vm(8, 3, 48, LANES),
-            vm(8, 3, 48, LANES),
-            vm(3, 9, 2, 24, LANES),
             vm(9, 2, 24, LANES),
             vm(9, 2, 24, LANES),
-            vm(11, 2, 24, LANES),
             vm(3, 48, LANES),
             vm(8, 3, 32, LANES),
             vm(256, 512),
             vm(192, 256),
             vm(6, 3, 16, LANES),
-        ) + (vm(48, LANES), vm(48, LANES), vm(24, LANES)) * 2
-        scratch += (vm(RIM_ROWS, LANES), vm(RIM_ROWS, LANES), pltpu.SemaphoreType.DMA((2,)))
-        ins = [in_vmem] * 12 + [in_hbm] * 2 + [in_vmem] * 4
-        fine_rate, coarse_rate, plane, iterate, lines, message = call(main_kernel, ins, outs, scratch)(
-            *args,
+        ]
+        scratch += [vm(48, LANES), vm(48, LANES), vm(24, LANES)] * 2
+        fine_rate, coarse_rate, plane, iterate, lines, message = call(main_kernel, [in_vmem] * 16, outs, scratch)(
+            *args[2:5],
+            *args[7:],
             *sides,
-            *rims,
             *corners,
             jnp.asarray(split_matrix()),
             jnp.asarray(weave_matrix()),
+            *owns,
         )
         received = lax.all_to_all(message, axes, 0, 0, tiled=True, axis_index_groups=ring)
         message = call(merge_kernel, [in_vmem], f32(plane_size, LANES))(received)

time: 75 us -> 73.9 us (0.985)
  waiting for transfers between devices: 2.04 us -> 0.69 us
    ppermute x6, waiting for transfers between devices: 2.04 us -> 0.69 us  [exchange(): return (lax.ppermute(first, axis, near), lax.ppermute(second, axis, far))]
    pallas_call x1 -> x2, Pallas kernels: 4.71 us -> 4.93 us  [the longest x1 3.71 us: shards(): call(main_kernel, [in_vmem] * 16, outs, scratch)]
  transfers between devices with their start and end apart: 6 -> 6, of which waited for: 1 -> 1; matrix products, arithmetic and copies ran while one was open for 0% -> 0% of each run, Pallas kernels for 0% -> 2%
where the time goes in v4:
time: 73.9 us; the launch traced here: 73.6 us
  blocking collectives  40.6 us (55%)
  starting transfers between devices  21.9 us (30%)
  Pallas kernels  8.72 us (12%)
  between operations  1.56 us (2%)
    all_to_all x1, blocking collectives, shards(): lax.all_to_all(message, axes, 0, 0, tiled=True, axis_index_groups=ring)  29.2 us
    ppermute x6, starting transfers between devices, exchange(): return (lax.ppermute(first, axis, near), lax.ppermute(second, axis, far))  21.9 us
    all_to_all x1, blocking collectives, shards(): lax.all_to_all(message, axes, 0, 0, tiled=True, axis_index_groups=plane_g...  11.4 us
    pallas_call x1, Pallas kernels, shards(): call(main_kernel, [in_vmem] * 16, outs, scratch)  3.71 us
    pallas_call x1, Pallas kernels, shards(): call(pack, [in_hbm] * 10, (f32(PACKED_ROWS, LANES),) * 2 + (f32(RIM_ROWS,...  2.31 us
  transfers between devices with their start and end apart: 6, of which 1 were waited for; matrix products, arithmetic and copies ran while one was open for 0% of the time, Pallas kernels for 2%

profile of v4, /device:TPU:1, one launch (start us, length us, event | category | flops | bytes accessed | tf_op | source)
XLA Modules:
  0.0 73.6 jit_solution(119267954513269447)
XLA Ops:
  0.6 2.3 %shard_map.139 = (f32[40,128]{1,0:T(8,128)}, f32[40,128]{1,0:T(8,128)}, f32[456,128]{1,0:T(8,128)}, f32[456,128]{1,0:T(8,128)}) custom-call(f32[3,8,16,256]{3,2,1,0:T(8,128)} %fn.1, f32[3,8,16,256]{3,2,1,0:T(8,128)} %fb.1, f32[8,16,256]{2,1,0:T(8,128)} %refs_0_.5, f32[8,16,256]{2,1,0:T(8,128)} %refs_1_.5, f32[8,16,256]{2,1,0:T(8,128)} %refs_2_.5, ...), custom_call_target="tpu_custom_call" | custom-call | tf_op jit(solution)/shard_map/pallas_call | solution.py:693
  3.0 9.6 %collective-permute-start = (f32[40,128]{1,0:T(8,128)}, f32[40,128]{1,0:T(8,128)S(1)}, u32[]{:S(2)}, u32[]{:S(2)}) collective-permute-start(f32[40,128]{1,0:T(8,128)} %get-tuple-element.34), channel_id=1, source_target_pairs={{0,1},{1,0},{2,3},{3,2},{4,5},{5,4},{6,7},{7,6},{8,9},{9,8},{10,11... | collective-permute-start | bytes 61448 | tf_op jit(solution)/shard_map/ppermute | solution.py:635
  12.6 0.7 collective-permute-start.1
  13.3 2.9 %collective-permute-start.4 = (f32[456,128]{1,0:T(8,128)}, f32[456,128]{1,0:T(8,128)}, u32[]{:S(2)}, u32[]{:S(2)}) collective-permute-start(f32[456,128]{1,0:T(8,128)} %get-tuple-element.38), channel_id=1, source_target_pairs={{0,16},{16,0},{32,48},{48,32},{64,80},{80,64},{96,112},{112,96},{1... | collective-permute-start | bytes 700424 | tf_op jit(solution)/shard_map/ppermute | solution.py:635
  16.1 3.1 %collective-permute-start.5 = (f32[456,128]{1,0:T(8,128)}, f32[456,128]{1,0:T(8,128)}, u32[]{:S(2)}, u32[]{:S(2)}) collective-permute-start(f32[456,128]{1,0:T(8,128)} %get-tuple-element.39), channel_id=1, source_target_pairs={{16,32},{48,64},{80,96},{112,128},{144,160},{176,192},{208,224},{2... | collective-permute-start | bytes 700424 | tf_op jit(solution)/shard_map/ppermute | solution.py:635
  19.3 0.0 collective-permute-done.first.refs_6_
  19.3 0.0 collective-permute-done.1.second.refs_7_
  19.3 0.0 copy-start
  19.3 0.0 copy-start.1
  19.3 0.0 copy-start.2
  19.3 0.0 copy-start.3
  19.3 0.0 copy-start.4
  19.3 0.0 copy-start.5
  19.4 0.0 copy-start.6
  19.4 0.0 copy-start.8
  19.4 0.0 copy-start.9
  19.4 0.0 copy-start.10
  19.4 0.0 copy-start.7
  19.4 0.0 copy-start.11
  19.5 2.5 %collective-permute-start.2 = (f32[48,128]{1,0:T(8,128)S(1)}, f32[48,128]{1,0:T(8,128)S(1)}, u32[]{:S(2)}, u32[]{:S(2)}) collective-permute-start(f32[48,128]{1,0:T(8,128)S(1)} %get-tuple-element.36), channel_id=1, source_target_pairs={{0,16},{16,0},{32,48},{48,32},{64,80},{80,64},{96,112},{112,96},{1... | collective-permute-start | bytes 73736 | tf_op jit(solution)/shard_map/ppermute | solution.py:635
  22.0 3.1 %collective-permute-start.3 = (f32[48,128]{1,0:T(8,128)S(1)}, f32[48,128]{1,0:T(8,128)S(1)}, u32[]{:S(2)}, u32[]{:S(2)}) collective-permute-start(f32[48,128]{1,0:T(8,128)S(1)} %get-tuple-element.37), channel_id=1, source_target_pairs={{16,32},{48,64},{80,96},{112,128},{144,160},{176,192},{208,224},{2... | collective-permute-start | bytes 73736 | tf_op jit(solution)/shard_map/ppermute | solution.py:635
  25.1 0.0 collective-permute-done.4.refs_10_
  25.1 0.0 collective-permute-done.5.refs_11_
  25.1 0.0 copy-done
  25.1 0.0 copy-done.1
  25.2 0.0 copy-done.2
  25.2 0.0 copy-done.3
  25.2 0.0 copy-done.4
  25.2 0.0 copy-done.5
  25.2 0.0 copy-done.6
  25.2 0.0 copy-done.8
  25.2 0.0 copy-done.9
  25.2 0.0 copy-done.10
  25.2 1.2 %shard_map.141 = (f32[3,8,2,48,128]{4,3,2,1,0:T(8,128)S(1)}, f32[8,2,48,128]{3,2,1,0:T(8,128)S(1)}, f32[3,9,1,24,128]{4,3,2,1,0:T(8,128)S(1)}, f32[11,1,24,128]{3,2,1,0:T(8,128)S(1)}) custom-call(f32[3,8,16,256]{3,2,1,0:T(8,128)S(1)} %copy-done, f32[3,8,16,256]{3,2,1,0:T(8,128)S(1)} %copy-done.1, f32[8,16,256]{2,1,0:T(8,128)S(1)} %copy-done.2, ...), custom_call_target="tpu_custom_call" | custom-call | tf_op jit(solution)/shard_map/pallas_call | solution.py:715
  26.5 0.0 collective-permute-done.2.refs_8_
  26.5 0.7 collective-permute-done.3.refs_9_
  27.2 0.0 copy-done.7
  27.2 0.0 copy-done.11
  27.2 3.7 %shard_map.142 = (f32[3,7,16,256]{3,2,1,0:T(8,128)S(1)}, f32[3,7,8,128]{3,2,1,0:T(8,128)S(1)}, f32[2,3,2,16,128]{4,3,2,1,0:T(8,128)S(1)}, f32[2,3,8,128]{3,2,1,0...) custom-call(f32[8,16,256]{2,1,0:T(8,128)S(1)} %copy-done.2, f32[8,16,256]{2,1,0:T(8,128)S(1)} %copy-done.3, ...), custom_call_target="tpu_custom_call" | custom-call | tf_op jit(solution)/shard_map/pallas_call | solution.py:736
  30.9 29.2 %all_to_all.22 = f32[32,1,128]{2,1,0:T(1,128)S(1)} all-to-all(f32[32,1,128]{2,1,0:T(1,128)S(1)} %bitcast.15), channel_id=1, replica_groups={{0,1,2,3,16,17,18,19,128,129,130,131,144,145,146,147,256,257,258,259,27..., dimensions={0} | all-to-all | bytes 32768 | tf_op jit(solution)/shard_map/all_to_all | solution.py:745
  60.1 0.5 shard_map.143
  60.6 11.4 %all_to_all.23 = f32[16,1,128]{2,1,0:T(1,128)S(1)} all-to-all(f32[16,1,128]{2,1,0:T(1,128)S(1)} %bitcast.14), channel_id=1, replica_groups={{0,4,8,12,32,36,40,44,64,68,72,76,96,100,104,108},{1,5,9,13,33,37,41,45..., dimensions={0} | all-to-all | bytes 16384 | tf_op jit(solution)/shard_map/all_to_all | solution.py:747
  71.9 1.0 %shard_map.144 = (f32[3,8,16,256]{3,2,1,0:T(8,128)}, f32[3,8,8,128]{3,2,1,0:T(8,128)}, f32[1]{0:T(128)}, f32[1]{0:T(128)}, s32[1]{0:T(128)}) custom-call(f32[16,128]{1,0:T(8,128)S(1)} %bitcast.13, f32[3,8,16,256]{3,2,1,0:T(8,128)S(1)} %copy-done, f32[3,8,16,256]{3,2,1,0:T(8,128)S(1)} %copy-done.1, f32[3,8,8,128]{3,2,1,0:T(8,128)S(1)} %copy-done.5, ...), custom_call_target="tpu_custom_call" | custom-call | tf_op jit(solution)/shard_map/pallas_call | solution.py:748
  (2 shorter events, 0.0 us)
Async XLA Ops:
  3.0 16.3 %collective-permute-start = (f32[40,128]{1,0:T(8,128)}, f32[40,128]{1,0:T(8,128)S(1)}, u32[]{:S(2)}, u32[]{:S(2)}) collective-permute-start(f32[40,128]{1,0:T(8,128)} %get-tuple-element.34), channel_id=1, source_target_pairs={{0,1},{1,0},{2,3},{3,2},{4,5},{5,4},{6,7},{7,6},{8,9},{9,8},{10,11... | collective-permute-start | bytes 61448 | tf_op jit(solution)/shard_map/ppermute | solution.py:635
  12.6 6.7 %collective-permute-start.1 = (f32[40,128]{1,0:T(8,128)}, f32[40,128]{1,0:T(8,128)S(1)}, u32[]{:S(2)}, u32[]{:S(2)}) collective-permute-start(f32[40,128]{1,0:T(8,128)} %get-tuple-element.35), channel_id=1, source_target_pairs={{1,2},{3,4},{5,6},{7,8},{9,10},{11,12},{13,14},{2,1},{4,3},{6,5},{... | collective-permute-start | bytes 61448 | tf_op jit(solution)/shard_map/ppermute | solution.py:635
  13.3 11.8 %collective-permute-start.4 = (f32[456,128]{1,0:T(8,128)}, f32[456,128]{1,0:T(8,128)}, u32[]{:S(2)}, u32[]{:S(2)}) collective-permute-start(f32[456,128]{1,0:T(8,128)} %get-tuple-element.38), channel_id=1, source_target_pairs={{0,16},{16,0},{32,48},{48,32},{64,80},{80,64},{96,112},{112,96},{1... | collective-permute-start | bytes 700424 | tf_op jit(solution)/shard_map/ppermute | solution.py:635
  16.1 9.0 %collective-permute-start.5 = (f32[456,128]{1,0:T(8,128)}, f32[456,128]{1,0:T(8,128)}, u32[]{:S(2)}, u32[]{:S(2)}) collective-permute-start(f32[456,128]{1,0:T(8,128)} %get-tuple-element.39), channel_id=1, source_target_pairs={{16,32},{48,64},{80,96},{112,128},{144,160},{176,192},{208,224},{2... | collective-permute-start | bytes 700424 | tf_op jit(solution)/shard_map/ppermute | solution.py:635
  19.3 5.9 %copy-start = (f32[3,8,16,256]{3,2,1,0:T(8,128)S(1)}, f32[3,8,16,256]{3,2,1,0:T(8,128)}, u32[]{:S(2)}) copy-start(f32[3,8,16,256]{3,2,1,0:T(8,128)} %fn.1) | copy-start | bytes 1179652
  19.3 5.9 %copy-start.1 = (f32[3,8,16,256]{3,2,1,0:T(8,128)S(1)}, f32[3,8,16,256]{3,2,1,0:T(8,128)}, u32[]{:S(2)}) copy-start(f32[3,8,16,256]{3,2,1,0:T(8,128)} %fb.1) | copy-start | bytes 1179652
  19.3 5.9 %copy-start.2 = (f32[8,16,256]{2,1,0:T(8,128)S(1)}, f32[8,16,256]{2,1,0:T(8,128)}, u32[]{:S(2)}) copy-start(f32[8,16,256]{2,1,0:T(8,128)} %refs_0_.5) | copy-start | bytes 393220
  19.3 5.9 %copy-start.3 = (f32[8,16,256]{2,1,0:T(8,128)S(1)}, f32[8,16,256]{2,1,0:T(8,128)}, u32[]{:S(2)}) copy-start(f32[8,16,256]{2,1,0:T(8,128)} %refs_1_.5) | copy-start | bytes 393220
  19.3 5.8 %copy-start.4 = (f32[8,16,256]{2,1,0:T(8,128)S(1)}, f32[8,16,256]{2,1,0:T(8,128)}, u32[]{:S(2)}) copy-start(f32[8,16,256]{2,1,0:T(8,128)} %refs_2_.5) | copy-start | bytes 393220
  19.3 5.8 %copy-start.5 = (f32[3,8,8,128]{3,2,1,0:T(8,128)S(1)}, f32[3,8,8,128]{3,2,1,0:T(8,128)}, u32[]{:S(2)}) copy-start(f32[3,8,8,128]{3,2,1,0:T(8,128)} %cn.1) | copy-start | bytes 294916
  19.4 5.8 %copy-start.6 = (f32[3,8,8,128]{3,2,1,0:T(8,128)S(1)}, f32[3,8,8,128]{3,2,1,0:T(8,128)}, u32[]{:S(2)}) copy-start(f32[3,8,8,128]{3,2,1,0:T(8,128)} %cb.1) | copy-start | bytes 294916
  19.4 5.8 %copy-start.8 = (f32[8,8,128]{2,1,0:T(8,128)S(1)}, f32[8,8,128]{2,1,0:T(8,128)}, u32[]{:S(2)}) copy-start(f32[8,8,128]{2,1,0:T(8,128)} %refs_3_.5) | copy-start | bytes 98308
  19.4 5.8 %copy-start.9 = (f32[8,8,128]{2,1,0:T(8,128)S(1)}, f32[8,8,128]{2,1,0:T(8,128)}, u32[]{:S(2)}) copy-start(f32[8,8,128]{2,1,0:T(8,128)} %refs_4_.5) | copy-start | bytes 98308
  19.4 5.8 %copy-start.10 = (f32[8,8,128]{2,1,0:T(8,128)S(1)}, f32[8,8,128]{2,1,0:T(8,128)}, u32[]{:S(2)}) copy-start(f32[8,8,128]{2,1,0:T(8,128)} %refs_5_.5) | copy-start | bytes 98308
  19.4 7.7 %copy-start.7 = (bf16[384,512]{1,0:T(8,128)(2,1)S(1)}, bf16[384,512]{1,0:T(8,128)(2,1)}, u32[]{:S(2)}) copy-start(bf16[384,512]{1,0:T(8,128)(2,1)} %constant.12.clone.refs_10_) | copy-start | bytes 1179652
  19.4 7.7 %copy-start.11 = (bf16[256,256]{1,0:T(8,128)(2,1)S(1)}, bf16[256,256]{1,0:T(8,128)(2,1)}, u32[]{:S(2)}) copy-start(bf16[256,256]{1,0:T(8,128)(2,1)} %constant.13.clone.refs_11_) | copy-start | bytes 393220
  19.5 7.0 %collective-permute-start.2 = (f32[48,128]{1,0:T(8,128)S(1)}, f32[48,128]{1,0:T(8,128)S(1)}, u32[]{:S(2)}, u32[]{:S(2)}) collective-permute-start(f32[48,128]{1,0:T(8,128)S(1)} %get-tuple-element.36), channel_id=1, source_target_pairs={{0,16},{16,0},{32,48},{48,32},{64,80},{80,64},{96,112},{112,96},{1... | collective-permute-start | bytes 73736 | tf_op jit(solution)/shard_map/ppermute | solution.py:635
  22.0 5.1 %collective-permute-start.3 = (f32[48,128]{1,0:T(8,128)S(1)}, f32[48,128]{1,0:T(8,128)S(1)}, u32[]{:S(2)}, u32[]{:S(2)}) collective-permute-start(f32[48,128]{1,0:T(8,128)S(1)} %get-tuple-element.37), channel_id=1, source_target_pairs={{16,32},{48,64},{80,96},{112,128},{144,160},{176,192},{208,224},{2... | collective-permute-start | bytes 73736 | tf_op jit(solution)/shard_map/ppermute | solution.py:635

commit v5 on v4

--- a/solution.py
+++ b/solution.py
@@ -24,28 +24,29 @@
 ]
 COARSE_THIN = [("cn", (c, k)) for c in range(3) for k in range(3, 8)]
 
-TILE_ROWS = {"A": (0, 16), "B": (16, 16), "C": (32, 8)}
-TILE_RIM = {"A": 9, "B": 7, "C": 5}
-PACKED_ROWS = 40
+TILE_ROWS = {"A": (0, 16), "B": (16, 16), "C": (16, 8), "D": (24, 8)}
+TILE_RIM = {"A": 9, "B": 7, "C": 5, "D": 5}
+PACKED_ROWS = 32
 
 
 def plan():
-    entries, lane, row = [], {"A": 0, "B": 0, "C": 0}, 0
+    entries, lane, row = [], {"A": 0, "B": 0, "C": 7 * len(DEEP_REST), "D": 7 * len(DEEP_REST)}, 0
     for tile, keys, low, high in (
         ("A", DEEP_NOW, 9, 8),
         ("A", THIN_NOW, 2, 2),
         ("B", DEEP_REST, 7, 6),
         ("C", COARSE_NOW, 5, 5),
-        ("C", COARSE_REST, 4, 4),
-        ("C", COARSE_THIN, 2, 2),
+        ("D", COARSE_REST, 4, 4),
+        ("C", COARSE_THIN[:13], 2, 2),
+        ("D", COARSE_THIN[13:], 2, 2),
     ):
         for key in keys:
-            own = 1 if tile == "C" else 2
+            own = 1 if tile in "CD" else 2
             entries.append((key, low, high, tile, lane[tile], row, own))
             lane[tile] += low
             row += own * low
     corners, corner_row = {}, 0
-    for tile in "ABC":
+    for tile in TILE_ROWS:
         for side in range(2):
             corners[tile, side] = corner_row
             corner_row += TILE_RIM[tile]
@@ -89,13 +90,13 @@
     return refs[name][index + (slice(None), slice(tile * LANES, (tile + 1) * LANES))]
 
 
-def is_even(axis):
-    return lax.axis_index(axis) % 2 == 0
-
-
-def pair(axis, low, high):
-    even = is_even(axis)
-    return jnp.where(even, low, high), jnp.where(even, high, low)
+FIRST_PAIRS = {"columns": ("gy", 1), "rows": ("gx", 1), "corners": ("gx", 1)}
+
+
+def pair(what, low, high):
+    axis, begin = FIRST_PAIRS[what]
+    upward = lax.axis_index(axis) % 2 == begin
+    return jnp.where(upward, low, high), jnp.where(upward, high, low)
 
 
 def pack(*refs):
@@ -126,7 +127,9 @@
             low_sum = jnp.where(inside, turned(own_tile(named, key, own - 1), at + low, 1), low_sum)
             high_sum = jnp.where(inside, turned(own_tile(named, key, 0), at, 1), high_sum)
         span = slice(base, base + rows)
-        column_outs[0][span, :], column_outs[1][span, :] = pair("gy", low_sum, high_sum)
+        sums = pair("columns", low_sum, high_sum)
+        for out, value in zip(column_outs, sums):
+            out[span, :] = out[span, :] + value if tile in "CD" else value
     for send in sends[:2]:
         send.start()
     row_outs[0][RIM_ROWS - 8 :, :] = jnp.zeros((8, LANES), jnp.float32)
@@ -138,7 +141,7 @@
             lanes = slice(tile * LANES, (tile + 1) * LANES)
             span = slice(row + tile * low, row + tile * low + low)
             row_outs[0][span, :], row_outs[1][span, :] = pair(
-                "gx", ref[index + (slice(rows - low, rows), lanes)], ref[index + (slice(0, low), lanes)]
+                "rows", ref[index + (slice(rows - low, rows), lanes)], ref[index + (slice(0, low), lanes)]
             )
     for send in sends[2:]:
         send.start()
@@ -152,11 +155,11 @@
     for tile, (base, rows) in TILE_ROWS.items():
         rim = TILE_RIM[tile]
         end, begin = slice(base + rows - rim, base + rows), slice(base, base + rim)
-        ends = pair("gy", second[end, :], first[end, :])
-        begins = pair("gy", second[begin, :], first[begin, :])
+        ends = pair("columns", second[end, :], first[end, :])
+        begins = pair("columns", second[begin, :], first[begin, :])
         for side in range(2):
             row = CORNERS[tile, side]
-            first_out[row : row + rim, :], second_out[row : row + rim, :] = pair("gx", ends[side], begins[side])
+            first_out[row : row + rim, :], second_out[row : row + rim, :] = pair("corners", ends[side], begins[side])
 
 
 def across(tiles, steps, wanted):
@@ -380,8 +383,8 @@
     return (fine if key[0] == "fn" else coarse).at[key[1]]
 
 
-def received(axis, pieces, span):
-    return pair(axis, pieces[1][span, :], pieces[0][span, :])
+def received(what, pieces, span):
+    return pair(what, pieces[1][span, :], pieces[0][span, :])
 
 
 def place_kernel(*refs):
@@ -396,7 +399,7 @@
                 target[t, 0:rows, :] = jnp.zeros((rows, LANES), jnp.float32)
                 target[t, 2 * rows : total, :] = jnp.zeros((total - 2 * rows, LANES), jnp.float32)
             target[t, rows : 2 * rows, :] = own_tile(named, key, t)
-            below, beyond = received("gx", rims, slice(row + t * low, row + t * low + low))
+            below, beyond = received("rows", rims, slice(row + t * low, row + t * low + low))
             target[t, rows - low : rows, :] = below
             target[t, 2 * rows : 2 * rows + low, :] = beyond
     coarse = targets[2]
@@ -412,20 +415,20 @@
     rims = refs[22:26]
     fine_x, fine_y, coarse_x, coarse_y = refs[26:30]
     mixed, planes, parted, woven, ends = refs[30:35]
-    packed = dict(zip("ABC", zip(refs[35:38], refs[38:41])))
+    packed = dict(zip(TILE_ROWS, zip(refs[35:39], refs[39:43])))
     fine, rest, coarse, coarse_rest = (Tiles(own, rim) for own, rim in zip(owns, rims))
     slot = {key: i for i, key in enumerate(DEEP_REST)}
     coarse_slot = {key: i for i, key in enumerate(COARSE_REST)}
 
     for tile, (base, rows) in TILE_ROWS.items():
         rim = TILE_RIM[tile]
-        own = received("gy", sides, slice(base, base + rows))
+        own = received("columns", sides, slice(base, base + rows))
         for side in range(2):
             target = packed[tile][side]
             target[...] = jnp.zeros(target.shape, jnp.float32)
             target[rows : 2 * rows, :] = own[side]
             row = CORNERS[tile, side]
-            low, high = received("gx", corners, slice(row, row + rim))
+            low, high = received("corners", corners, slice(row, row + rim))
             target[rows - rim : rows, :] = low
             target[2 * rows : 2 * rows + rim, :] = high
     for key, low, high, tile, at, _, _ in ENTRIES:
@@ -629,10 +632,14 @@
             fine_out[c, 7, :, t * LANES : (t + 1) * LANES] = plane[0, c, t] + square * plane[1, c, t]
 
 
-def exchange(first, second, axis, count):
-    near = [(i, i ^ 1) for i in range(count) if i ^ 1 < count]
-    far = [(i, i + 1) for i in range(1, count - 1, 2)] + [(i + 1, i) for i in range(1, count - 1, 2)]
-    return lax.ppermute(first, axis, near), lax.ppermute(second, axis, far)
+def exchange(first, second, what, count):
+    axis, begin = FIRST_PAIRS[what]
+
+    def swap(value, parity):
+        ups = [(i, i + 1) for i in range(parity, count - 1, 2)]
+        return lax.ppermute(value, axis, ups + [(j, i) for i, j in ups])
+
+    return swap(first, begin), swap(second, 1 - begin)
 
 
 def gather_groups(columns, rows):
@@ -701,15 +708,15 @@
             out_specs=[in_hbm] * 4,
             limit=63,
         )(*args)
-        sides = exchange(first_side, second_side, "gy", rows)
-        rims = exchange(first_rim, second_rim, "gx", columns)
+        sides = exchange(first_side, second_side, "columns", rows)
+        rims = exchange(first_rim, second_rim, "rows", columns)
         first, second = call(
             pack_corners,
             [in_vmem] * 2,
             (f32(CORNER_ROWS, LANES),) * 2,
             cost=pl.CostEstimate(flops=10**12, bytes_accessed=10**9, transcendentals=0),
         )(*sides)
-        corners = exchange(first, second, "gx", columns)
+        corners = exchange(first, second, "corners", columns)
         ring_size, plane_size = len(ring[0]), len(plane_groups[0])
         own_shapes = ((3, 8, 2, 48, LANES), (8, 2, 48, LANES), (3, 9, 1, 24, LANES), (11, 1, 24, LANES))
         owns = call(place_kernel, [in_vmem] * 12, tuple(f32(*shape) for shape in own_shapes))(*args, *rims)
@@ -732,7 +739,7 @@
             vm(192, 256),
             vm(6, 3, 16, LANES),
         ]
-        scratch += [vm(48, LANES), vm(48, LANES), vm(24, LANES)] * 2
+        scratch += [vm(48, LANES), vm(48, LANES), vm(24, LANES), vm(24, LANES)] * 2
         fine_rate, coarse_rate, plane, iterate, lines, message = call(main_kernel, [in_vmem] * 16, outs, scratch)(
             *args[2:5],
             *args[7:],

time: 73.9 us -> 71.1 us (0.962)
  blocking collectives: 40.6 us -> 30 us
  starting transfers between devices: 21.9 us -> 30.4 us
    all_to_all x1, blocking collectives: 29.2 us -> 17.6 us  [shards(): lax.all_to_all(message, axes, 0, 0, tiled=True, axis_index_groups=ring)]
    ppermute x6, starting transfers between devices: 21.9 us -> 30.4 us  [swap(): return lax.ppermute(value, axis, ups + [(j, i) for i, j in ups])]
    all_to_all x1, blocking collectives: 11.4 us -> 12.4 us  [shards(): lax.all_to_all(message, axes, 0, 0, tiled=True, axis_index_groups=plane_g...]
  transfers between devices with their start and end apart: 6 -> 6, of which waited for: 1 -> 0; matrix products, arithmetic and copies ran while one was open for 0% -> 0% of each run, Pallas kernels for 2% -> 2%
where the time goes in v5:
time: 71.1 us; the launch traced here: 70.7 us
  starting transfers between devices  30.4 us (43%)
  blocking collectives  30 us (42%)
  Pallas kernels  8.68 us (12%)
  between operations  1.58 us (2%)
    ppermute x6, starting transfers between devices, swap(): return lax.ppermute(value, axis, ups + [(j, i) for i, j in ups])  30.4 us
    all_to_all x1, blocking collectives, shards(): lax.all_to_all(message, axes, 0, 0, tiled=True, axis_index_groups=ring)  17.6 us
    all_to_all x1, blocking collectives, shards(): lax.all_to_all(message, axes, 0, 0, tiled=True, axis_index_groups=plane_g...  12.4 us
    pallas_call x1, Pallas kernels, shards(): call(main_kernel, [in_vmem] * 16, outs, scratch)  3.68 us
    pallas_call x1, Pallas kernels, shards(): call(pack, [in_hbm] * 10, (f32(PACKED_ROWS, LANES),) * 2 + (f32(RIM_ROWS,...  2.31 us
  transfers between devices with their start and end apart: 6, of which 0 were waited for; matrix products, arithmetic and copies ran while one was open for 0% of the time, Pallas kernels for 2%

profile of v5, /device:TPU:1, one launch (start us, length us, event | category | flops | bytes accessed | tf_op | source)
XLA Modules:
  0.0 70.7 jit_solution(14511153370272923800)
XLA Ops:
  0.6 2.3 %shard_map.139 = (f32[32,128]{1,0:T(8,128)}, f32[32,128]{1,0:T(8,128)}, f32[456,128]{1,0:T(8,128)}, f32[456,128]{1,0:T(8,128)}) custom-call(f32[3,8,16,256]{3,2,1,0:T(8,128)} %fn.1, f32[3,8,16,256]{3,2,1,0:T(8,128)} %fb.1, f32[8,16,256]{2,1,0:T(8,128)} %refs_0_.5, f32[8,16,256]{2,1,0:T(8,128)} %refs_1_.5, f32[8,16,256]{2,1,0:T(8,128)} %refs_2_.5, ...), custom_call_target="tpu_custom_call" | custom-call | tf_op jit(solution)/shard_map/pallas_call | solution.py:700
  3.0 0.7 collective-permute-start
  3.6 17.8 %collective-permute-start.1 = (f32[32,128]{1,0:T(8,128)}, f32[32,128]{1,0:T(8,128)S(1)}, u32[]{:S(2)}, u32[]{:S(2)}) collective-permute-start(f32[32,128]{1,0:T(8,128)} %get-tuple-element.35), channel_id=1, source_target_pairs={{0,1},{2,3},{4,5},{6,7},{8,9},{10,11},{12,13},{14,15},{1,0},{3,2},... | collective-permute-start | bytes 49160 | tf_op jit(solution)/shard_map/ppermute | solution.py:640
  21.4 4.3 %collective-permute-start.4 = (f32[456,128]{1,0:T(8,128)}, f32[456,128]{1,0:T(8,128)}, u32[]{:S(2)}, u32[]{:S(2)}) collective-permute-start(f32[456,128]{1,0:T(8,128)} %get-tuple-element.38), channel_id=1, source_target_pairs={{16,32},{48,64},{80,96},{112,128},{144,160},{176,192},{208,224},{2... | collective-permute-start | bytes 700424 | tf_op jit(solution)/shard_map/ppermute | solution.py:640
  25.8 1.9 %collective-permute-start.5 = (f32[456,128]{1,0:T(8,128)}, f32[456,128]{1,0:T(8,128)}, u32[]{:S(2)}, u32[]{:S(2)}) collective-permute-start(f32[456,128]{1,0:T(8,128)} %get-tuple-element.39), channel_id=1, source_target_pairs={{0,16},{32,48},{64,80},{96,112},{128,144},{160,176},{192,208},{224... | collective-permute-start | bytes 700424 | tf_op jit(solution)/shard_map/ppermute | solution.py:640
  27.7 0.0 collective-permute-done.first.refs_6_
  27.7 0.0 collective-permute-done.1.second.refs_7_
  27.7 0.0 copy-start
  27.7 0.0 copy-start.1
  27.7 0.0 copy-start.2
  27.8 0.0 copy-start.3
  27.8 0.0 copy-start.4
  27.8 0.0 copy-start.5
  27.8 0.0 copy-start.6
  27.8 0.0 copy-start.8
  27.8 0.0 copy-start.9
  27.8 0.0 copy-start.10
  27.9 0.0 copy-start.7
  27.9 0.0 copy-start.11
  27.9 3.7 %collective-permute-start.2 = (f32[56,128]{1,0:T(8,128)S(1)}, f32[56,128]{1,0:T(8,128)S(1)}, u32[]{:S(2)}, u32[]{:S(2)}) collective-permute-start(f32[56,128]{1,0:T(8,128)S(1)} %get-tuple-element.36), channel_id=1, source_target_pairs={{16,32},{48,64},{80,96},{112,128},{144,160},{176,192},{208,224},{2... | collective-permute-start | bytes 86024 | tf_op jit(solution)/shard_map/ppermute | solution.py:640
  31.6 1.9 %collective-permute-start.3 = (f32[56,128]{1,0:T(8,128)S(1)}, f32[56,128]{1,0:T(8,128)S(1)}, u32[]{:S(2)}, u32[]{:S(2)}) collective-permute-start(f32[56,128]{1,0:T(8,128)S(1)} %get-tuple-element.37), channel_id=1, source_target_pairs={{0,16},{32,48},{64,80},{96,112},{128,144},{160,176},{192,208},{224... | collective-permute-start | bytes 86024 | tf_op jit(solution)/shard_map/ppermute | solution.py:640
  33.6 0.0 collective-permute-done.4.refs_10_
  33.6 0.0 collective-permute-done.5.refs_11_
  33.6 0.0 copy-done
  33.6 0.0 copy-done.1
  33.6 0.0 copy-done.2
  33.6 0.0 copy-done.3
  33.6 0.0 copy-done.4
  33.6 0.0 copy-done.5
  33.6 0.0 copy-done.6
  33.6 0.0 copy-done.8
  33.7 0.0 copy-done.9
  33.7 0.0 copy-done.10
  33.7 1.2 %shard_map.141 = (f32[3,8,2,48,128]{4,3,2,1,0:T(8,128)S(1)}, f32[8,2,48,128]{3,2,1,0:T(8,128)S(1)}, f32[3,9,1,24,128]{4,3,2,1,0:T(8,128)S(1)}, f32[11,1,24,128]{3,2,1,0:T(8,128)S(1)}) custom-call(f32[3,8,16,256]{3,2,1,0:T(8,128)S(1)} %copy-done, f32[3,8,16,256]{3,2,1,0:T(8,128)S(1)} %copy-done.1, f32[8,16,256]{2,1,0:T(8,128)S(1)} %copy-done.2, ...), custom_call_target="tpu_custom_call" | custom-call | tf_op jit(solution)/shard_map/pallas_call | solution.py:722
  34.9 0.0 collective-permute-done.2.refs_8_
  34.9 0.0 collective-permute-done.3.refs_9_
  34.9 0.0 copy-done.7
  34.9 0.0 copy-done.11
  34.9 3.7 %shard_map.142 = (f32[3,7,16,256]{3,2,1,0:T(8,128)S(1)}, f32[3,7,8,128]{3,2,1,0:T(8,128)S(1)}, f32[2,3,2,16,128]{4,3,2,1,0:T(8,128)S(1)}, f32[2,3,8,128]{3,2,1,0...) custom-call(f32[8,16,256]{2,1,0:T(8,128)S(1)} %copy-done.2, f32[8,16,256]{2,1,0:T(8,128)S(1)} %copy-done.3, ...), custom_call_target="tpu_custom_call" | custom-call | tf_op jit(solution)/shard_map/pallas_call | solution.py:743
  38.6 17.6 %all_to_all.22 = f32[32,1,128]{2,1,0:T(1,128)S(1)} all-to-all(f32[32,1,128]{2,1,0:T(1,128)S(1)} %bitcast.15), channel_id=1, replica_groups={{0,1,2,3,16,17,18,19,128,129,130,131,144,145,146,147,256,257,258,259,27..., dimensions={0} | all-to-all | bytes 32768 | tf_op jit(solution)/shard_map/all_to_all | solution.py:752
  56.3 0.5 shard_map.143
  56.7 12.4 %all_to_all.23 = f32[16,1,128]{2,1,0:T(1,128)S(1)} all-to-all(f32[16,1,128]{2,1,0:T(1,128)S(1)} %bitcast.14), channel_id=1, replica_groups={{0,4,8,12,32,36,40,44,64,68,72,76,96,100,104,108},{1,5,9,13,33,37,41,45..., dimensions={0} | all-to-all | bytes 16384 | tf_op jit(solution)/shard_map/all_to_all | solution.py:754
  69.1 1.0 %shard_map.144 = (f32[3,8,16,256]{3,2,1,0:T(8,128)}, f32[3,8,8,128]{3,2,1,0:T(8,128)}, f32[1]{0:T(128)}, f32[1]{0:T(128)}, s32[1]{0:T(128)}) custom-call(f32[16,128]{1,0:T(8,128)S(1)} %bitcast.13, f32[3,8,16,256]{3,2,1,0:T(8,128)S(1)} %copy-done, f32[3,8,16,256]{3,2,1,0:T(8,128)S(1)} %copy-done.1, f32[3,8,8,128]{3,2,1,0:T(8,128)S(1)} %copy-done.5, ...), custom_call_target="tpu_custom_call" | custom-call | tf_op jit(solution)/shard_map/pallas_call | solution.py:755
  (2 shorter events, 0.0 us)
Async XLA Ops:
  3.0 24.7 %collective-permute-start = (f32[32,128]{1,0:T(8,128)}, f32[32,128]{1,0:T(8,128)S(1)}, u32[]{:S(2)}, u32[]{:S(2)}) collective-permute-start(f32[32,128]{1,0:T(8,128)} %get-tuple-element.34), channel_id=1, source_target_pairs={{1,2},{3,4},{5,6},{7,8},{9,10},{11,12},{13,14},{2,1},{4,3},{6,5},{... | collective-permute-start | bytes 49160 | tf_op jit(solution)/shard_map/ppermute | solution.py:640
  3.6 24.1 %collective-permute-start.1 = (f32[32,128]{1,0:T(8,128)}, f32[32,128]{1,0:T(8,128)S(1)}, u32[]{:S(2)}, u32[]{:S(2)}) collective-permute-start(f32[32,128]{1,0:T(8,128)} %get-tuple-element.35), channel_id=1, source_target_pairs={{0,1},{2,3},{4,5},{6,7},{8,9},{10,11},{12,13},{14,15},{1,0},{3,2},... | collective-permute-start | bytes 49160 | tf_op jit(solution)/shard_map/ppermute | solution.py:640
  21.4 12.1 %collective-permute-start.4 = (f32[456,128]{1,0:T(8,128)}, f32[456,128]{1,0:T(8,128)}, u32[]{:S(2)}, u32[]{:S(2)}) collective-permute-start(f32[456,128]{1,0:T(8,128)} %get-tuple-element.38), channel_id=1, source_target_pairs={{16,32},{48,64},{80,96},{112,128},{144,160},{176,192},{208,224},{2... | collective-permute-start | bytes 700424 | tf_op jit(solution)/shard_map/ppermute | solution.py:640
  25.8 7.8 %collective-permute-start.5 = (f32[456,128]{1,0:T(8,128)}, f32[456,128]{1,0:T(8,128)}, u32[]{:S(2)}, u32[]{:S(2)}) collective-permute-start(f32[456,128]{1,0:T(8,128)} %get-tuple-element.39), channel_id=1, source_target_pairs={{0,16},{32,48},{64,80},{96,112},{128,144},{160,176},{192,208},{224... | collective-permute-start | bytes 700424 | tf_op jit(solution)/shard_map/ppermute | solution.py:640
  27.7 5.9 %copy-start = (f32[3,8,16,256]{3,2,1,0:T(8,128)S(1)}, f32[3,8,16,256]{3,2,1,0:T(8,128)}, u32[]{:S(2)}) copy-start(f32[3,8,16,256]{3,2,1,0:T(8,128)} %fn.1) | copy-start | bytes 1179652
  27.7 5.9 %copy-start.1 = (f32[3,8,16,256]{3,2,1,0:T(8,128)S(1)}, f32[3,8,16,256]{3,2,1,0:T(8,128)}, u32[]{:S(2)}) copy-start(f32[3,8,16,256]{3,2,1,0:T(8,128)} %fb.1) | copy-start | bytes 1179652
  27.7 5.9 %copy-start.2 = (f32[8,16,256]{2,1,0:T(8,128)S(1)}, f32[8,16,256]{2,1,0:T(8,128)}, u32[]{:S(2)}) copy-start(f32[8,16,256]{2,1,0:T(8,128)} %refs_0_.5) | copy-start | bytes 393220
  27.8 5.9 %copy-start.3 = (f32[8,16,256]{2,1,0:T(8,128)S(1)}, f32[8,16,256]{2,1,0:T(8,128)}, u32[]{:S(2)}) copy-start(f32[8,16,256]{2,1,0:T(8,128)} %refs_1_.5) | copy-start | bytes 393220
  27.8 5.9 %copy-start.4 = (f32[8,16,256]{2,1,0:T(8,128)S(1)}, f32[8,16,256]{2,1,0:T(8,128)}, u32[]{:S(2)}) copy-start(f32[8,16,256]{2,1,0:T(8,128)} %refs_2_.5) | copy-start | bytes 393220
  27.8 5.8 %copy-start.5 = (f32[3,8,8,128]{3,2,1,0:T(8,128)S(1)}, f32[3,8,8,128]{3,2,1,0:T(8,128)}, u32[]{:S(2)}) copy-start(f32[3,8,8,128]{3,2,1,0:T(8,128)} %cn.1) | copy-start | bytes 294916
  27.8 5.8 %copy-start.6 = (f32[3,8,8,128]{3,2,1,0:T(8,128)S(1)}, f32[3,8,8,128]{3,2,1,0:T(8,128)}, u32[]{:S(2)}) copy-start(f32[3,8,8,128]{3,2,1,0:T(8,128)} %cb.1) | copy-start | bytes 294916
  27.8 5.8 %copy-start.8 = (f32[8,8,128]{2,1,0:T(8,128)S(1)}, f32[8,8,128]{2,1,0:T(8,128)}, u32[]{:S(2)}) copy-start(f32[8,8,128]{2,1,0:T(8,128)} %refs_3_.5) | copy-start | bytes 98308
  27.8 5.8 %copy-start.9 = (f32[8,8,128]{2,1,0:T(8,128)S(1)}, f32[8,8,128]{2,1,0:T(8,128)}, u32[]{:S(2)}) copy-start(f32[8,8,128]{2,1,0:T(8,128)} %refs_4_.5) | copy-start | bytes 98308
  27.8 5.8 %copy-start.10 = (f32[8,8,128]{2,1,0:T(8,128)S(1)}, f32[8,8,128]{2,1,0:T(8,128)}, u32[]{:S(2)}) copy-start(f32[8,8,128]{2,1,0:T(8,128)} %refs_5_.5) | copy-start | bytes 98308
  27.9 7.0 %copy-start.7 = (bf16[384,512]{1,0:T(8,128)(2,1)S(1)}, bf16[384,512]{1,0:T(8,128)(2,1)}, u32[]{:S(2)}) copy-start(bf16[384,512]{1,0:T(8,128)(2,1)} %constant.12.clone.refs_10_) | copy-start | bytes 1179652
  27.9 7.0 %copy-start.11 = (bf16[256,256]{1,0:T(8,128)(2,1)S(1)}, bf16[256,256]{1,0:T(8,128)(2,1)}, u32[]{:S(2)}) copy-start(bf16[256,256]{1,0:T(8,128)(2,1)} %constant.13.clone.refs_11_) | copy-start | bytes 393220
  27.9 7.0 %collective-permute-start.2 = (f32[56,128]{1,0:T(8,128)S(1)}, f32[56,128]{1,0:T(8,128)S(1)}, u32[]{:S(2)}, u32[]{:S(2)}) collective-permute-start(f32[56,128]{1,0:T(8,128)S(1)} %get-tuple-element.36), channel_id=1, source_target_pairs={{16,32},{48,64},{80,96},{112,128},{144,160},{176,192},{208,224},{2... | collective-permute-start | bytes 86024 | tf_op jit(solution)/shard_map/ppermute | solution.py:640
  31.6 3.3 %collective-permute-start.3 = (f32[56,128]{1,0:T(8,128)S(1)}, f32[56,128]{1,0:T(8,128)S(1)}, u32[]{:S(2)}, u32[]{:S(2)}) collective-permute-start(f32[56,128]{1,0:T(8,128)S(1)} %get-tuple-element.37), channel_id=1, source_target_pairs={{0,16},{32,48},{64,80},{96,112},{128,144},{160,176},{192,208},{224... | collective-permute-start | bytes 86024 | tf_op jit(solution)/shard_map/ppermute | solution.py:640

commit v6 on v5

--- a/solution.py
+++ b/solution.py
@@ -91,21 +91,24 @@
 
 
 FIRST_PAIRS = {"columns": ("gy", 1), "rows": ("gx", 1), "corners": ("gx", 1)}
+TURN = 16
+
+
+def begins(what, row):
+    begin = FIRST_PAIRS[what][1]
+    return jnp.where(row < TURN, begin, 1 - begin) if what == "columns" else begin
 
 
 def pair(what, low, high):
-    axis, begin = FIRST_PAIRS[what]
-    upward = lax.axis_index(axis) % 2 == begin
+    upward = lax.axis_index(FIRST_PAIRS[what][0]) % 2 == begins(what, lax.axis_index("gx"))
     return jnp.where(upward, low, high), jnp.where(upward, high, low)
 
 
 def pack(*refs):
     sources = dict(zip(NAMES, refs[:10]))
-    targets, packs = refs[10:14], refs[14:18]
-    column_outs, row_outs = packs[:2], packs[2:]
-    named = dict(zip(NAMES, refs[18:28]))
-    sems, out_sems = refs[28:30]
-    sends = [pltpu.make_async_copy(source, target, out_sems.at[i]) for i, (source, target) in enumerate(zip(packs, targets))]
+    column_outs, row_outs = refs[10:12], refs[12:14]
+    named = dict(zip(NAMES, refs[14:24]))
+    sems = refs[24]
     copies = []
     for i, (name, part) in enumerate(PACK_SOURCES):
         source, target = sources[name], named[name]
@@ -130,8 +133,6 @@
         sums = pair("columns", low_sum, high_sum)
         for out, value in zip(column_outs, sums):
             out[span, :] = out[span, :] + value if tile in "CD" else value
-    for send in sends[:2]:
-        send.start()
     row_outs[0][RIM_ROWS - 8 :, :] = jnp.zeros((8, LANES), jnp.float32)
     row_outs[1][RIM_ROWS - 8 :, :] = jnp.zeros((8, LANES), jnp.float32)
     for (name, index), low, _, _, _, row, own in ENTRIES:
@@ -143,10 +144,6 @@
             row_outs[0][span, :], row_outs[1][span, :] = pair(
                 "rows", ref[index + (slice(rows - low, rows), lanes)], ref[index + (slice(0, low), lanes)]
             )
-    for send in sends[2:]:
-        send.start()
-    for send in sends:
-        send.wait()
 
 
 def pack_corners(first, second, first_out, second_out):
@@ -632,12 +629,18 @@
             fine_out[c, 7, :, t * LANES : (t + 1) * LANES] = plane[0, c, t] + square * plane[1, c, t]
 
 
-def exchange(first, second, what, count):
+def exchange(first, second, what, columns, rows):
     axis, begin = FIRST_PAIRS[what]
 
     def swap(value, parity):
-        ups = [(i, i + 1) for i in range(parity, count - 1, 2)]
-        return lax.ppermute(value, axis, ups + [(j, i) for i, j in ups])
+        ups = []
+        for i in range(columns):
+            for j in range(rows):
+                turned_parity = 1 - parity if axis == "gy" and i >= TURN else parity
+                place, count, step = (j, rows, 1) if axis == "gy" else (i, columns, rows)
+                if place % 2 == turned_parity and place + 1 < count:
+                    ups.append((i * rows + j, i * rows + j + step))
+        return lax.ppermute(value, ("gx", "gy"), ups + [(j, i) for i, j in ups])
 
     return swap(first, begin), swap(second, 1 - begin)
 
@@ -700,26 +703,23 @@
         first_side, second_side, first_rim, second_rim = call(
             pack,
             [in_hbm] * 10,
-            (f32(PACKED_ROWS, LANES),) * 2 + (f32(RIM_ROWS, LANES),) * 2,
-            [vm(PACKED_ROWS, LANES)] * 2
-            + [vm(RIM_ROWS, LANES)] * 2
-            + [vm(*a.shape) for a in args]
-            + [pltpu.SemaphoreType.DMA((len(PACK_SOURCES),)), pltpu.SemaphoreType.DMA((4,))],
-            out_specs=[in_hbm] * 4,
-            limit=63,
-        )(*args)
-        sides = exchange(first_side, second_side, "columns", rows)
-        rims = exchange(first_rim, second_rim, "rows", columns)
+            (pltpu.VMEM((PACKED_ROWS, LANES), jnp.float32),) * 2 + (pltpu.VMEM((RIM_ROWS, LANES), jnp.float32),) * 2,
+            [vm(*a.shape) for a in args] + [pltpu.SemaphoreType.DMA((len(PACK_SOURCES),))],
+        )(*[pltpu.with_memory_space_constraint(a, pltpu.HBM) for a in args])
+        sides = exchange(first_side, second_side, "columns", columns, rows)
+        rims = exchange(first_rim, second_rim, "rows", columns, rows)
         first, second = call(
             pack_corners,
             [in_vmem] * 2,
             (f32(CORNER_ROWS, LANES),) * 2,
             cost=pl.CostEstimate(flops=10**12, bytes_accessed=10**9, transcendentals=0),
         )(*sides)
-        corners = exchange(first, second, "corners", columns)
+        corners = exchange(first, second, "corners", columns, rows)
         ring_size, plane_size = len(ring[0]), len(plane_groups[0])
         own_shapes = ((3, 8, 2, 48, LANES), (8, 2, 48, LANES), (3, 9, 1, 24, LANES), (11, 1, 24, LANES))
-        owns = call(place_kernel, [in_vmem] * 12, tuple(f32(*shape) for shape in own_shapes))(*args, *rims)
+        owns = call(place_kernel, [in_vmem] * 12, tuple(f32(*shape) for shape in own_shapes))(
+            *args, *[pltpu.with_memory_space_constraint(rim, pltpu.VMEM) for rim in rims]
+        )
         outs = (
             f32(3, 7, 16, 256),
             f32(3, 7, 8, 128),

time: 71.1 us -> 70.4 us (level)
    all_to_all x1, blocking collectives: 12.4 us -> 11 us  [shards(): lax.all_to_all(message, axes, 0, 0, tiled=True, axis_index_groups=plane_g...]
where the time goes in v6:
time: 70.4 us; the launch traced here: 70 us
  starting transfers between devices  30.4 us (43%)
  blocking collectives  29.4 us (42%)
  Pallas kernels  8.63 us (12%)
  between operations  1.58 us (2%)
    ppermute x6, starting transfers between devices, swap(): return lax.ppermute(value, ('gx', 'gy'), ups + [(j, i) for i, j in ups])  30.4 us
    all_to_all x1, blocking collectives, shards(): lax.all_to_all(message, axes, 0, 0, tiled=True, axis_index_groups=ring)  18.3 us
    all_to_all x1, blocking collectives, shards(): lax.all_to_all(message, axes, 0, 0, tiled=True, axis_index_groups=plane_g...  11 us
    pallas_call x1, Pallas kernels, shards(): call(main_kernel, [in_vmem] * 16, outs, scratch)  3.69 us
    pallas_call x1, Pallas kernels, shards(): call(pack, [in_hbm] * 10, (pltpu.VMEM((PACKED_ROWS, LANES), jnp.float32),...  2.24 us
  transfers between devices with their start and end apart: 6, of which 0 were waited for; matrix products, arithmetic and copies ran while one was open for 0% of the time, Pallas kernels for 2%

profile of v6, /device:TPU:1, one launch (start us, length us, event | category | flops | bytes accessed | tf_op | source)
XLA Modules:
  0.0 70.0 jit_solution(17943520760137283498)
XLA Ops:
  0.6 2.2 %shard_map.139 = (f32[32,128]{1,0:T(8,128)S(1)}, f32[32,128]{1,0:T(8,128)S(1)}, f32[456,128]{1,0:T(8,128)}, f32[456,128]{1,0:T(8,128)}) custom-call(f32[3,8,16,256]{3,2,1,0:T(8,128)} %fn.1, f32[3,8,16,256]{3,2,1,0:T(8,128)} %fb.1, f32[8,16,256]{2,1,0:T(8,128)} %refs_0_.5, f32[8,16,256]{2,1,0:T(8,128)} %refs_1_.5, f32[8,16,256]{2,1,0:T(8,128)} %refs_2_.5, ...), custom_call_target="tpu_custom_call" | custom-call | tf_op jit(solution)/shard_map/pallas_call | solution.py:703
  2.9 0.7 collective-permute-start
  3.6 17.8 %collective-permute-start.1 = (f32[32,128]{1,0:T(8,128)S(1)}, f32[32,128]{1,0:T(8,128)S(1)}, u32[]{:S(2)}, u32[]{:S(2)}) collective-permute-start(f32[32,128]{1,0:T(8,128)S(1)} %get-tuple-element.35), channel_id=1, source_target_pairs={{0,1},{2,3},{4,5},{6,7},{8,9},{10,11},{12,13},{14,15},{16,17},{18,... | collective-permute-start | bytes 49160 | tf_op jit(solution)/shard_map/ppermute | solution.py:643
  21.4 4.3 %collective-permute-start.4 = (f32[456,128]{1,0:T(8,128)}, f32[456,128]{1,0:T(8,128)}, u32[]{:S(2)}, u32[]{:S(2)}) collective-permute-start(f32[456,128]{1,0:T(8,128)} %get-tuple-element.38), channel_id=1, source_target_pairs={{16,32},{17,33},{18,34},{19,35},{20,36},{21,37},{22,38},{23,39},{2... | collective-permute-start | bytes 700424 | tf_op jit(solution)/shard_map/ppermute | solution.py:643
  25.7 1.9 %collective-permute-start.5 = (f32[456,128]{1,0:T(8,128)}, f32[456,128]{1,0:T(8,128)}, u32[]{:S(2)}, u32[]{:S(2)}) collective-permute-start(f32[456,128]{1,0:T(8,128)} %get-tuple-element.39), channel_id=1, source_target_pairs={{0,16},{1,17},{2,18},{3,19},{4,20},{5,21},{6,22},{7,23},{8,24},{9,... | collective-permute-start | bytes 700424 | tf_op jit(solution)/shard_map/ppermute | solution.py:643
  27.6 0.0 collective-permute-done.first.refs_6_
  27.6 0.0 collective-permute-done.1.second.refs_7_
  27.6 0.0 copy-start
  27.7 0.0 copy-start.1
  27.7 0.0 copy-start.2
  27.7 0.0 copy-start.3
  27.7 0.0 copy-start.4
  27.7 0.0 copy-start.5
  27.7 0.0 copy-start.6
  27.7 0.0 copy-start.8
  27.7 0.0 copy-start.9
  27.8 0.0 copy-start.10
  27.8 0.0 copy-start.7
  27.8 0.0 copy-start.11
  27.8 3.7 %collective-permute-start.2 = (f32[56,128]{1,0:T(8,128)S(1)}, f32[56,128]{1,0:T(8,128)S(1)}, u32[]{:S(2)}, u32[]{:S(2)}) collective-permute-start(f32[56,128]{1,0:T(8,128)S(1)} %get-tuple-element.36), channel_id=1, source_target_pairs={{16,32},{17,33},{18,34},{19,35},{20,36},{21,37},{22,38},{23,39},{2... | collective-permute-start | bytes 86024 | tf_op jit(solution)/shard_map/ppermute | solution.py:643
  31.6 1.9 %collective-permute-start.3 = (f32[56,128]{1,0:T(8,128)S(1)}, f32[56,128]{1,0:T(8,128)S(1)}, u32[]{:S(2)}, u32[]{:S(2)}) collective-permute-start(f32[56,128]{1,0:T(8,128)S(1)} %get-tuple-element.37), channel_id=1, source_target_pairs={{0,16},{1,17},{2,18},{3,19},{4,20},{5,21},{6,22},{7,23},{8,24},{9,... | collective-permute-start | bytes 86024 | tf_op jit(solution)/shard_map/ppermute | solution.py:643
  33.5 0.0 collective-permute-done.4.refs_10_
  33.5 0.0 collective-permute-done.5.refs_11_
  33.5 0.0 copy-done
  33.5 0.0 copy-done.1
  33.5 0.0 copy-done.2
  33.5 0.0 copy-done.3
  33.5 0.0 copy-done.4
  33.6 0.0 copy-done.5
  33.6 0.0 copy-done.6
  33.6 0.0 copy-done.8
  33.6 0.0 copy-done.9
  33.6 0.0 copy-done.10
  33.6 1.2 %shard_map.141 = (f32[3,8,2,48,128]{4,3,2,1,0:T(8,128)S(1)}, f32[8,2,48,128]{3,2,1,0:T(8,128)S(1)}, f32[3,9,1,24,128]{4,3,2,1,0:T(8,128)S(1)}, f32[11,1,24,128]{3,2,1,0:T(8,128)S(1)}) custom-call(f32[3,8,16,256]{3,2,1,0:T(8,128)S(1)} %copy-done, f32[3,8,16,256]{3,2,1,0:T(8,128)S(1)} %copy-done.1, f32[8,16,256]{2,1,0:T(8,128)S(1)} %copy-done.2, ...), custom_call_target="tpu_custom_call" | custom-call | tf_op jit(solution)/shard_map/pallas_call | solution.py:720
  34.8 0.0 collective-permute-done.2.refs_8_
  34.8 0.0 collective-permute-done.3.refs_9_
  34.8 0.0 copy-done.7
  34.9 0.0 copy-done.11
  34.9 3.7 %shard_map.142 = (f32[3,7,16,256]{3,2,1,0:T(8,128)S(1)}, f32[3,7,8,128]{3,2,1,0:T(8,128)S(1)}, f32[2,3,2,16,128]{4,3,2,1,0:T(8,128)S(1)}, f32[2,3,8,128]{3,2,1,0...) custom-call(f32[8,16,256]{2,1,0:T(8,128)S(1)} %copy-done.2, f32[8,16,256]{2,1,0:T(8,128)S(1)} %copy-done.3, ...), custom_call_target="tpu_custom_call" | custom-call | tf_op jit(solution)/shard_map/pallas_call | solution.py:743
  38.6 18.3 %all_to_all.22 = f32[32,1,128]{2,1,0:T(1,128)S(1)} all-to-all(f32[32,1,128]{2,1,0:T(1,128)S(1)} %bitcast.15), channel_id=1, replica_groups={{0,1,2,3,16,17,18,19,128,129,130,131,144,145,146,147,256,257,258,259,27..., dimensions={0} | all-to-all | bytes 32768 | tf_op jit(solution)/shard_map/all_to_all | solution.py:752
  56.9 0.5 shard_map.143
  57.4 11.0 %all_to_all.23 = f32[16,1,128]{2,1,0:T(1,128)S(1)} all-to-all(f32[16,1,128]{2,1,0:T(1,128)S(1)} %bitcast.14), channel_id=1, replica_groups={{0,4,8,12,32,36,40,44,64,68,72,76,96,100,104,108},{1,5,9,13,33,37,41,45..., dimensions={0} | all-to-all | bytes 16384 | tf_op jit(solution)/shard_map/all_to_all | solution.py:754
  68.4 1.0 %shard_map.144 = (f32[3,8,16,256]{3,2,1,0:T(8,128)}, f32[3,8,8,128]{3,2,1,0:T(8,128)}, f32[1]{0:T(128)}, f32[1]{0:T(128)}, s32[1]{0:T(128)}) custom-call(f32[16,128]{1,0:T(8,128)S(1)} %bitcast.13, f32[3,8,16,256]{3,2,1,0:T(8,128)S(1)} %copy-done, f32[3,8,16,256]{3,2,1,0:T(8,128)S(1)} %copy-done.1, f32[3,8,8,128]{3,2,1,0:T(8,128)S(1)} %copy-done.5, ...), custom_call_target="tpu_custom_call" | custom-call | tf_op jit(solution)/shard_map/pallas_call | solution.py:755
  (2 shorter events, 0.0 us)
Async XLA Ops:
  2.9 24.7 %collective-permute-start = (f32[32,128]{1,0:T(8,128)S(1)}, f32[32,128]{1,0:T(8,128)S(1)}, u32[]{:S(2)}, u32[]{:S(2)}) collective-permute-start(f32[32,128]{1,0:T(8,128)S(1)} %get-tuple-element.34), channel_id=1, source_target_pairs={{1,2},{3,4},{5,6},{7,8},{9,10},{11,12},{13,14},{17,18},{19,20},{21... | collective-permute-start | bytes 49160 | tf_op jit(solution)/shard_map/ppermute | solution.py:643
  3.6 24.1 %collective-permute-start.1 = (f32[32,128]{1,0:T(8,128)S(1)}, f32[32,128]{1,0:T(8,128)S(1)}, u32[]{:S(2)}, u32[]{:S(2)}) collective-permute-start(f32[32,128]{1,0:T(8,128)S(1)} %get-tuple-element.35), channel_id=1, source_target_pairs={{0,1},{2,3},{4,5},{6,7},{8,9},{10,11},{12,13},{14,15},{16,17},{18,... | collective-permute-start | bytes 49160 | tf_op jit(solution)/shard_map/ppermute | solution.py:643
  21.4 12.1 %collective-permute-start.4 = (f32[456,128]{1,0:T(8,128)}, f32[456,128]{1,0:T(8,128)}, u32[]{:S(2)}, u32[]{:S(2)}) collective-permute-start(f32[456,128]{1,0:T(8,128)} %get-tuple-element.38), channel_id=1, source_target_pairs={{16,32},{17,33},{18,34},{19,35},{20,36},{21,37},{22,38},{23,39},{2... | collective-permute-start | bytes 700424 | tf_op jit(solution)/shard_map/ppermute | solution.py:643
  25.7 7.8 %collective-permute-start.5 = (f32[456,128]{1,0:T(8,128)}, f32[456,128]{1,0:T(8,128)}, u32[]{:S(2)}, u32[]{:S(2)}) collective-permute-start(f32[456,128]{1,0:T(8,128)} %get-tuple-element.39), channel_id=1, source_target_pairs={{0,16},{1,17},{2,18},{3,19},{4,20},{5,21},{6,22},{7,23},{8,24},{9,... | collective-permute-start | bytes 700424 | tf_op jit(solution)/shard_map/ppermute | solution.py:643
  27.6 5.9 %copy-start = (f32[3,8,16,256]{3,2,1,0:T(8,128)S(1)}, f32[3,8,16,256]{3,2,1,0:T(8,128)}, u32[]{:S(2)}) copy-start(f32[3,8,16,256]{3,2,1,0:T(8,128)} %fn.1) | copy-start | bytes 1179652
  27.7 5.9 %copy-start.1 = (f32[3,8,16,256]{3,2,1,0:T(8,128)S(1)}, f32[3,8,16,256]{3,2,1,0:T(8,128)}, u32[]{:S(2)}) copy-start(f32[3,8,16,256]{3,2,1,0:T(8,128)} %fb.1) | copy-start | bytes 1179652
  27.7 5.9 %copy-start.2 = (f32[8,16,256]{2,1,0:T(8,128)S(1)}, f32[8,16,256]{2,1,0:T(8,128)}, u32[]{:S(2)}) copy-start(f32[8,16,256]{2,1,0:T(8,128)} %refs_0_.5) | copy-start | bytes 393220
  27.7 5.9 %copy-start.3 = (f32[8,16,256]{2,1,0:T(8,128)S(1)}, f32[8,16,256]{2,1,0:T(8,128)}, u32[]{:S(2)}) copy-start(f32[8,16,256]{2,1,0:T(8,128)} %refs_1_.5) | copy-start | bytes 393220
  27.7 5.9 %copy-start.4 = (f32[8,16,256]{2,1,0:T(8,128)S(1)}, f32[8,16,256]{2,1,0:T(8,128)}, u32[]{:S(2)}) copy-start(f32[8,16,256]{2,1,0:T(8,128)} %refs_2_.5) | copy-start | bytes 393220
  27.7 5.8 %copy-start.5 = (f32[3,8,8,128]{3,2,1,0:T(8,128)S(1)}, f32[3,8,8,128]{3,2,1,0:T(8,128)}, u32[]{:S(2)}) copy-start(f32[3,8,8,128]{3,2,1,0:T(8,128)} %cn.1) | copy-start | bytes 294916
  27.7 5.8 %copy-start.6 = (f32[3,8,8,128]{3,2,1,0:T(8,128)S(1)}, f32[3,8,8,128]{3,2,1,0:T(8,128)}, u32[]{:S(2)}) copy-start(f32[3,8,8,128]{3,2,1,0:T(8,128)} %cb.1) | copy-start | bytes 294916
  27.7 5.8 %copy-start.8 = (f32[8,8,128]{2,1,0:T(8,128)S(1)}, f32[8,8,128]{2,1,0:T(8,128)}, u32[]{:S(2)}) copy-start(f32[8,8,128]{2,1,0:T(8,128)} %refs_3_.5) | copy-start | bytes 98308
  27.7 5.8 %copy-start.9 = (f32[8,8,128]{2,1,0:T(8,128)S(1)}, f32[8,8,128]{2,1,0:T(8,128)}, u32[]{:S(2)}) copy-start(f32[8,8,128]{2,1,0:T(8,128)} %refs_4_.5) | copy-start | bytes 98308
  27.8 5.8 %copy-start.10 = (f32[8,8,128]{2,1,0:T(8,128)S(1)}, f32[8,8,128]{2,1,0:T(8,128)}, u32[]{:S(2)}) copy-start(f32[8,8,128]{2,1,0:T(8,128)} %refs_5_.5) | copy-start | bytes 98308
  27.8 7.0 %copy-start.7 = (bf16[384,512]{1,0:T(8,128)(2,1)S(1)}, bf16[384,512]{1,0:T(8,128)(2,1)}, u32[]{:S(2)}) copy-start(bf16[384,512]{1,0:T(8,128)(2,1)} %constant.12.clone.refs_10_) | copy-start | bytes 1179652
  27.8 7.0 %copy-start.11 = (bf16[256,256]{1,0:T(8,128)(2,1)S(1)}, bf16[256,256]{1,0:T(8,128)(2,1)}, u32[]{:S(2)}) copy-start(bf16[256,256]{1,0:T(8,128)(2,1)} %constant.13.clone.refs_11_) | copy-start | bytes 393220
  27.8 7.0 %collective-permute-start.2 = (f32[56,128]{1,0:T(8,128)S(1)}, f32[56,128]{1,0:T(8,128)S(1)}, u32[]{:S(2)}, u32[]{:S(2)}) collective-permute-start(f32[56,128]{1,0:T(8,128)S(1)} %get-tuple-element.36), channel_id=1, source_target_pairs={{16,32},{17,33},{18,34},{19,35},{20,36},{21,37},{22,38},{23,39},{2... | collective-permute-start | bytes 86024 | tf_op jit(solution)/shard_map/ppermute | solution.py:643
  31.6 3.3 %collective-permute-start.3 = (f32[56,128]{1,0:T(8,128)S(1)}, f32[56,128]{1,0:T(8,128)S(1)}, u32[]{:S(2)}, u32[]{:S(2)}) collective-permute-start(f32[56,128]{1,0:T(8,128)S(1)} %get-tuple-element.37), channel_id=1, source_target_pairs={{0,16},{1,17},{2,18},{3,19},{4,20},{5,21},{6,22},{7,23},{8,24},{9,... | collective-permute-start | bytes 86024 | tf_op jit(solution)/shard_map/ppermute | solution.py:643

commit v7 on v6

--- a/solution.py
+++ b/solution.py
@@ -688,7 +688,7 @@
         in_smem = pl.BlockSpec(memory_space=pltpu.SMEM)
         in_hbm = pl.BlockSpec(memory_space=pltpu.HBM)
 
-        def call(kernel, ins, outs, scratch=(), out_specs=None, cost=None, limit=16):
+        def call(kernel, ins, outs, scratch=(), out_specs=None, cost=None, limit=8):
             return pl.pallas_call(
                 kernel,
                 out_shape=outs,

time: 70.4 us -> 70.4 us (level)
  no operation moved by 1% of the time
where the time goes in v7:
time: 70.4 us; the launch traced here: 70 us
  starting transfers between devices  30.4 us (43%)
  blocking collectives  29.4 us (42%)
  Pallas kernels  8.63 us (12%)
  between operations  1.58 us (2%)
    ppermute x6, starting transfers between devices, swap(): return lax.ppermute(value, ('gx', 'gy'), ups + [(j, i) for i, j in ups])  30.4 us
    all_to_all x1, blocking collectives, shards(): lax.all_to_all(message, axes, 0, 0, tiled=True, axis_index_groups=ring)  18.3 us
    all_to_all x1, blocking collectives, shards(): lax.all_to_all(message, axes, 0, 0, tiled=True, axis_index_groups=plane_g...  11 us
    pallas_call x1, Pallas kernels, shards(): call(main_kernel, [in_vmem] * 16, outs, scratch)  3.69 us
    pallas_call x1, Pallas kernels, shards(): call(pack, [in_hbm] * 10, (pltpu.VMEM((PACKED_ROWS, LANES), jnp.float32),...  2.24 us
  transfers between devices with their start and end apart: 6, of which 0 were waited for; matrix products, arithmetic and copies ran while one was open for 0% of the time, Pallas kernels for 2%

profile of v7, /device:TPU:1, one launch (start us, length us, event | category | flops | bytes accessed | tf_op | source)
XLA Modules:
  0.0 70.0 jit_solution(13049222686413828382)
XLA Ops:
  0.6 2.2 %shard_map.139 = (f32[32,128]{1,0:T(8,128)S(1)}, f32[32,128]{1,0:T(8,128)S(1)}, f32[456,128]{1,0:T(8,128)}, f32[456,128]{1,0:T(8,128)}) custom-call(f32[3,8,16,256]{3,2,1,0:T(8,128)} %fn.1, f32[3,8,16,256]{3,2,1,0:T(8,128)} %fb.1, f32[8,16,256]{2,1,0:T(8,128)} %refs_0_.5, f32[8,16,256]{2,1,0:T(8,128)} %refs_1_.5, f32[8,16,256]{2,1,0:T(8,128)} %refs_2_.5, ...), custom_call_target="tpu_custom_call" | custom-call | tf_op jit(solution)/shard_map/pallas_call | solution.py:703
  2.9 0.7 collective-permute-start
  3.6 17.8 %collective-permute-start.1 = (f32[32,128]{1,0:T(8,128)S(1)}, f32[32,128]{1,0:T(8,128)S(1)}, u32[]{:S(2)}, u32[]{:S(2)}) collective-permute-start(f32[32,128]{1,0:T(8,128)S(1)} %get-tuple-element.35), channel_id=1, source_target_pairs={{0,1},{2,3},{4,5},{6,7},{8,9},{10,11},{12,13},{14,15},{16,17},{18,... | collective-permute-start | bytes 49160 | tf_op jit(solution)/shard_map/ppermute | solution.py:643
  21.4 4.3 %collective-permute-start.4 = (f32[456,128]{1,0:T(8,128)}, f32[456,128]{1,0:T(8,128)}, u32[]{:S(2)}, u32[]{:S(2)}) collective-permute-start(f32[456,128]{1,0:T(8,128)} %get-tuple-element.38), channel_id=1, source_target_pairs={{16,32},{17,33},{18,34},{19,35},{20,36},{21,37},{22,38},{23,39},{2... | collective-permute-start | bytes 700424 | tf_op jit(solution)/shard_map/ppermute | solution.py:643
  25.7 1.9 %collective-permute-start.5 = (f32[456,128]{1,0:T(8,128)}, f32[456,128]{1,0:T(8,128)}, u32[]{:S(2)}, u32[]{:S(2)}) collective-permute-start(f32[456,128]{1,0:T(8,128)} %get-tuple-element.39), channel_id=1, source_target_pairs={{0,16},{1,17},{2,18},{3,19},{4,20},{5,21},{6,22},{7,23},{8,24},{9,... | collective-permute-start | bytes 700424 | tf_op jit(solution)/shard_map/ppermute | solution.py:643
  27.6 0.0 collective-permute-done.first.refs_6_
  27.6 0.0 collective-permute-done.1.second.refs_7_
  27.6 0.0 copy-start
  27.7 0.0 copy-start.1
  27.7 0.0 copy-start.2
  27.7 0.0 copy-start.3
  27.7 0.0 copy-start.4
  27.7 0.0 copy-start.5
  27.7 0.0 copy-start.6
  27.7 0.0 copy-start.8
  27.7 0.0 copy-start.9
  27.8 0.0 copy-start.10
  27.8 0.0 copy-start.7
  27.8 0.0 copy-start.11
  27.8 3.7 %collective-permute-start.2 = (f32[56,128]{1,0:T(8,128)S(1)}, f32[56,128]{1,0:T(8,128)S(1)}, u32[]{:S(2)}, u32[]{:S(2)}) collective-permute-start(f32[56,128]{1,0:T(8,128)S(1)} %get-tuple-element.36), channel_id=1, source_target_pairs={{16,32},{17,33},{18,34},{19,35},{20,36},{21,37},{22,38},{23,39},{2... | collective-permute-start | bytes 86024 | tf_op jit(solution)/shard_map/ppermute | solution.py:643
  31.6 1.9 %collective-permute-start.3 = (f32[56,128]{1,0:T(8,128)S(1)}, f32[56,128]{1,0:T(8,128)S(1)}, u32[]{:S(2)}, u32[]{:S(2)}) collective-permute-start(f32[56,128]{1,0:T(8,128)S(1)} %get-tuple-element.37), channel_id=1, source_target_pairs={{0,16},{1,17},{2,18},{3,19},{4,20},{5,21},{6,22},{7,23},{8,24},{9,... | collective-permute-start | bytes 86024 | tf_op jit(solution)/shard_map/ppermute | solution.py:643
  33.5 0.0 collective-permute-done.4.refs_10_
  33.5 0.0 collective-permute-done.5.refs_11_
  33.5 0.0 copy-done
  33.5 0.0 copy-done.1
  33.5 0.0 copy-done.2
  33.5 0.0 copy-done.3
  33.5 0.0 copy-done.4
  33.6 0.0 copy-done.5
  33.6 0.0 copy-done.6
  33.6 0.0 copy-done.8
  33.6 0.0 copy-done.9
  33.6 0.0 copy-done.10
  33.6 1.2 %shard_map.141 = (f32[3,8,2,48,128]{4,3,2,1,0:T(8,128)S(1)}, f32[8,2,48,128]{3,2,1,0:T(8,128)S(1)}, f32[3,9,1,24,128]{4,3,2,1,0:T(8,128)S(1)}, f32[11,1,24,128]{3,2,1,0:T(8,128)S(1)}) custom-call(f32[3,8,16,256]{3,2,1,0:T(8,128)S(1)} %copy-done, f32[3,8,16,256]{3,2,1,0:T(8,128)S(1)} %copy-done.1, f32[8,16,256]{2,1,0:T(8,128)S(1)} %copy-done.2, ...), custom_call_target="tpu_custom_call" | custom-call | tf_op jit(solution)/shard_map/pallas_call | solution.py:720
  34.8 0.0 collective-permute-done.2.refs_8_
  34.8 0.0 collective-permute-done.3.refs_9_
  34.8 0.0 copy-done.7
  34.9 0.0 copy-done.11
  34.9 3.7 %shard_map.142 = (f32[3,7,16,256]{3,2,1,0:T(8,128)S(1)}, f32[3,7,8,128]{3,2,1,0:T(8,128)S(1)}, f32[2,3,2,16,128]{4,3,2,1,0:T(8,128)S(1)}, f32[2,3,8,128]{3,2,1,0...) custom-call(f32[8,16,256]{2,1,0:T(8,128)S(1)} %copy-done.2, f32[8,16,256]{2,1,0:T(8,128)S(1)} %copy-done.3, ...), custom_call_target="tpu_custom_call" | custom-call | tf_op jit(solution)/shard_map/pallas_call | solution.py:743
  38.6 18.3 %all_to_all.22 = f32[32,1,128]{2,1,0:T(1,128)S(1)} all-to-all(f32[32,1,128]{2,1,0:T(1,128)S(1)} %bitcast.15), channel_id=1, replica_groups={{0,1,2,3,16,17,18,19,128,129,130,131,144,145,146,147,256,257,258,259,27..., dimensions={0} | all-to-all | bytes 32768 | tf_op jit(solution)/shard_map/all_to_all | solution.py:752
  56.9 0.5 shard_map.143
  57.4 11.0 %all_to_all.23 = f32[16,1,128]{2,1,0:T(1,128)S(1)} all-to-all(f32[16,1,128]{2,1,0:T(1,128)S(1)} %bitcast.14), channel_id=1, replica_groups={{0,4,8,12,32,36,40,44,64,68,72,76,96,100,104,108},{1,5,9,13,33,37,41,45..., dimensions={0} | all-to-all | bytes 16384 | tf_op jit(solution)/shard_map/all_to_all | solution.py:754
  68.4 1.0 %shard_map.144 = (f32[3,8,16,256]{3,2,1,0:T(8,128)}, f32[3,8,8,128]{3,2,1,0:T(8,128)}, f32[1]{0:T(128)}, f32[1]{0:T(128)}, s32[1]{0:T(128)}) custom-call(f32[16,128]{1,0:T(8,128)S(1)} %bitcast.13, f32[3,8,16,256]{3,2,1,0:T(8,128)S(1)} %copy-done, f32[3,8,16,256]{3,2,1,0:T(8,128)S(1)} %copy-done.1, f32[3,8,8,128]{3,2,1,0:T(8,128)S(1)} %copy-done.5, ...), custom_call_target="tpu_custom_call" | custom-call | tf_op jit(solution)/shard_map/pallas_call | solution.py:755
  (2 shorter events, 0.0 us)
Async XLA Ops:
  2.9 24.7 %collective-permute-start = (f32[32,128]{1,0:T(8,128)S(1)}, f32[32,128]{1,0:T(8,128)S(1)}, u32[]{:S(2)}, u32[]{:S(2)}) collective-permute-start(f32[32,128]{1,0:T(8,128)S(1)} %get-tuple-element.34), channel_id=1, source_target_pairs={{1,2},{3,4},{5,6},{7,8},{9,10},{11,12},{13,14},{17,18},{19,20},{21... | collective-permute-start | bytes 49160 | tf_op jit(solution)/shard_map/ppermute | solution.py:643
  3.6 24.1 %collective-permute-start.1 = (f32[32,128]{1,0:T(8,128)S(1)}, f32[32,128]{1,0:T(8,128)S(1)}, u32[]{:S(2)}, u32[]{:S(2)}) collective-permute-start(f32[32,128]{1,0:T(8,128)S(1)} %get-tuple-element.35), channel_id=1, source_target_pairs={{0,1},{2,3},{4,5},{6,7},{8,9},{10,11},{12,13},{14,15},{16,17},{18,... | collective-permute-start | bytes 49160 | tf_op jit(solution)/shard_map/ppermute | solution.py:643
  21.4 12.1 %collective-permute-start.4 = (f32[456,128]{1,0:T(8,128)}, f32[456,128]{1,0:T(8,128)}, u32[]{:S(2)}, u32[]{:S(2)}) collective-permute-start(f32[456,128]{1,0:T(8,128)} %get-tuple-element.38), channel_id=1, source_target_pairs={{16,32},{17,33},{18,34},{19,35},{20,36},{21,37},{22,38},{23,39},{2... | collective-permute-start | bytes 700424 | tf_op jit(solution)/shard_map/ppermute | solution.py:643
  25.7 7.8 %collective-permute-start.5 = (f32[456,128]{1,0:T(8,128)}, f32[456,128]{1,0:T(8,128)}, u32[]{:S(2)}, u32[]{:S(2)}) collective-permute-start(f32[456,128]{1,0:T(8,128)} %get-tuple-element.39), channel_id=1, source_target_pairs={{0,16},{1,17},{2,18},{3,19},{4,20},{5,21},{6,22},{7,23},{8,24},{9,... | collective-permute-start | bytes 700424 | tf_op jit(solution)/shard_map/ppermute | solution.py:643
  27.6 5.9 %copy-start = (f32[3,8,16,256]{3,2,1,0:T(8,128)S(1)}, f32[3,8,16,256]{3,2,1,0:T(8,128)}, u32[]{:S(2)}) copy-start(f32[3,8,16,256]{3,2,1,0:T(8,128)} %fn.1) | copy-start | bytes 1179652
  27.7 5.9 %copy-start.1 = (f32[3,8,16,256]{3,2,1,0:T(8,128)S(1)}, f32[3,8,16,256]{3,2,1,0:T(8,128)}, u32[]{:S(2)}) copy-start(f32[3,8,16,256]{3,2,1,0:T(8,128)} %fb.1) | copy-start | bytes 1179652
  27.7 5.9 %copy-start.2 = (f32[8,16,256]{2,1,0:T(8,128)S(1)}, f32[8,16,256]{2,1,0:T(8,128)}, u32[]{:S(2)}) copy-start(f32[8,16,256]{2,1,0:T(8,128)} %refs_0_.5) | copy-start | bytes 393220
  27.7 5.9 %copy-start.3 = (f32[8,16,256]{2,1,0:T(8,128)S(1)}, f32[8,16,256]{2,1,0:T(8,128)}, u32[]{:S(2)}) copy-start(f32[8,16,256]{2,1,0:T(8,128)} %refs_1_.5) | copy-start | bytes 393220
  27.7 5.9 %copy-start.4 = (f32[8,16,256]{2,1,0:T(8,128)S(1)}, f32[8,16,256]{2,1,0:T(8,128)}, u32[]{:S(2)}) copy-start(f32[8,16,256]{2,1,0:T(8,128)} %refs_2_.5) | copy-start | bytes 393220
  27.7 5.8 %copy-start.5 = (f32[3,8,8,128]{3,2,1,0:T(8,128)S(1)}, f32[3,8,8,128]{3,2,1,0:T(8,128)}, u32[]{:S(2)}) copy-start(f32[3,8,8,128]{3,2,1,0:T(8,128)} %cn.1) | copy-start | bytes 294916
  27.7 5.8 %copy-start.6 = (f32[3,8,8,128]{3,2,1,0:T(8,128)S(1)}, f32[3,8,8,128]{3,2,1,0:T(8,128)}, u32[]{:S(2)}) copy-start(f32[3,8,8,128]{3,2,1,0:T(8,128)} %cb.1) | copy-start | bytes 294916
  27.7 5.8 %copy-start.8 = (f32[8,8,128]{2,1,0:T(8,128)S(1)}, f32[8,8,128]{2,1,0:T(8,128)}, u32[]{:S(2)}) copy-start(f32[8,8,128]{2,1,0:T(8,128)} %refs_3_.5) | copy-start | bytes 98308
  27.7 5.8 %copy-start.9 = (f32[8,8,128]{2,1,0:T(8,128)S(1)}, f32[8,8,128]{2,1,0:T(8,128)}, u32[]{:S(2)}) copy-start(f32[8,8,128]{2,1,0:T(8,128)} %refs_4_.5) | copy-start | bytes 98308
  27.8 5.8 %copy-start.10 = (f32[8,8,128]{2,1,0:T(8,128)S(1)}, f32[8,8,128]{2,1,0:T(8,128)}, u32[]{:S(2)}) copy-start(f32[8,8,128]{2,1,0:T(8,128)} %refs_5_.5) | copy-start | bytes 98308
  27.8 7.0 %copy-start.7 = (bf16[384,512]{1,0:T(8,128)(2,1)S(1)}, bf16[384,512]{1,0:T(8,128)(2,1)}, u32[]{:S(2)}) copy-start(bf16[384,512]{1,0:T(8,128)(2,1)} %constant.12.clone.refs_10_) | copy-start | bytes 1179652
  27.8 7.0 %copy-start.11 = (bf16[256,256]{1,0:T(8,128)(2,1)S(1)}, bf16[256,256]{1,0:T(8,128)(2,1)}, u32[]{:S(2)}) copy-start(bf16[256,256]{1,0:T(8,128)(2,1)} %constant.13.clone.refs_11_) | copy-start | bytes 393220
  27.8 7.0 %collective-permute-start.2 = (f32[56,128]{1,0:T(8,128)S(1)}, f32[56,128]{1,0:T(8,128)S(1)}, u32[]{:S(2)}, u32[]{:S(2)}) collective-permute-start(f32[56,128]{1,0:T(8,128)S(1)} %get-tuple-element.36), channel_id=1, source_target_pairs={{16,32},{17,33},{18,34},{19,35},{20,36},{21,37},{22,38},{23,39},{2... | collective-permute-start | bytes 86024 | tf_op jit(solution)/shard_map/ppermute | solution.py:643
  31.6 3.3 %collective-permute-start.3 = (f32[56,128]{1,0:T(8,128)S(1)}, f32[56,128]{1,0:T(8,128)S(1)}, u32[]{:S(2)}, u32[]{:S(2)}) collective-permute-start(f32[56,128]{1,0:T(8,128)S(1)} %get-tuple-element.37), channel_id=1, source_target_pairs={{0,16},{1,17},{2,18},{3,19},{4,20},{5,21},{6,22},{7,23},{8,24},{9,... | collective-permute-start | bytes 86024 | tf_op jit(solution)/shard_map/ppermute | solution.py:643
